TPU v7x, 32 devices: a whole 2x2x4 slice. The times are simulated.
32 devices in a mesh: section: 4 (over y, core), seq: 8 (over z, x).
Axes of the slice: x: 2, y: 2, z: 4, core: 2. Of those that a mesh axis runs over, the one named last changes fastest.
Arguments:
- queries: bfloat16 [4, 1024, 2560], P('section', 'seq'), may hold values from -6 to 6
- cache_keys: bfloat16 [1024, 512], P('seq', 'section'), may hold values from -6 to 6
- cache_values: bfloat16 [1024, 512], P('seq', 'section'), may hold values from -6 to 6
- saved_out: bfloat16 [4, 1024, 2560], P('section', 'seq'), may hold values from -1.5 to 1.5
- out_grads: bfloat16 [4, 1024, 2560], P('section', 'seq'), may hold values from -6 to 6
- log_sums: bfloat16 [4, 1024, 20], P('section', 'seq')
Outputs:
- query_grads: bfloat16 [4, 1024, 2560], P('section', 'seq')
- key_grads: bfloat16 [1024, 512], P('seq', 'section')
- value_grads: bfloat16 [1024, 512], P('seq', 'section')
All inputs are finite; a program needn't handle non-finite values.
Results may differ from a plain program's by a relative error of at most 0.0064.
Values may be sent and summed in bfloat16 or wider, within the bound.
No kernel may reach another device: no remote copies, remote signals or barrier semaphores. Data moves between devices by JAX's collectives and lax.ppermute only.
A program may use at most 64 MiB of HBM per device.

v0:
```python
import math

import jax
import jax.numpy as jnp
from jax import lax
from jax.sharding import PartitionSpec as P

ROW_DIMS = (((1,), (1,)), ((), ()))
COL_DIMS = (((0,), (0,)), ((), ()))


def tile_terms(
    query_vecs,
    grad_vecs,
    total_vecs,
    row_dots,
    positions,
    key_tile,
    value_tile,
    key_start,
    inv_root,
):
    scores = (
        lax.dot_general(query_vecs, key_tile, ROW_DIMS, preferred_element_type=jnp.float32)
        * inv_root
    )
    key_pos = key_start + lax.broadcasted_iota(jnp.int32, (1, key_tile.shape[0]), 1)
    allowed = key_pos <= positions[:, None]
    weights = jnp.where(allowed, jnp.exp(scores - total_vecs[:, None]), 0.0)
    weights_low = weights.astype(jnp.bfloat16)
    weight_grads = lax.dot_general(
        grad_vecs, value_tile, ROW_DIMS, preferred_element_type=jnp.float32
    )
    score_grads = (weights * (weight_grads - row_dots[:, None]) * inv_root).astype(jnp.bfloat16)
    query_part = jnp.dot(score_grads, key_tile, preferred_element_type=jnp.float32)
    key_part = lax.dot_general(
        score_grads, query_vecs, COL_DIMS, preferred_element_type=jnp.float32
    )
    value_part = lax.dot_general(
        weights_low, grad_vecs, COL_DIMS, preferred_element_type=jnp.float32
    )
    return (query_part, key_part, value_part)


def add_rows(buffer, part, key_start):
    current = lax.dynamic_slice_in_dim(buffer, key_start, part.shape[0], 0)
    return lax.dynamic_update_slice_in_dim(buffer, current + part, key_start, 0)


def prepare(arrays, first_pos, head_dim):
    query_rows, grad_rows, saved_rows, total_rows = arrays
    row_count = query_rows.shape[0]
    query_vecs = query_rows.reshape(-1, head_dim)
    grad_vecs = grad_rows.reshape(-1, head_dim)
    products = grad_rows.astype(jnp.float32) * saved_rows.astype(jnp.float32)
    row_dots = jnp.sum(products.reshape(-1, head_dim), axis=1)
    total_vecs = total_rows.reshape(-1).astype(jnp.float32)
    per_row = query_vecs.shape[0] // row_count
    positions = first_pos + lax.broadcasted_iota(jnp.int32, (query_vecs.shape[0],), 0) // per_row
    last_pos = first_pos + row_count - 1
    return (query_vecs, grad_vecs, total_vecs, row_dots, positions, last_pos)


def apply_tiles(prepared, totals, key_tile, value_tile, key_start, inv_root):
    query_accs, key_sum, value_sum = totals
    group_data = prepared[0]

    def compute(state):
        query_acc, key_buffer, value_buffer = state
        query_part, key_part, value_part = tile_terms(
            group_data[0],
            group_data[1],
            group_data[2],
            group_data[3],
            group_data[4],
            key_tile,
            value_tile,
            key_start,
            inv_root,
        )
        return (
            query_acc + query_part,
            add_rows(key_buffer, key_part, key_start),
            add_rows(value_buffer, value_part, key_start),
        )

    def unchanged(state):
        return state

    query_acc, key_sum, value_sum = lax.cond(
        key_start <= group_data[5], compute, unchanged, (query_accs[0], key_sum, value_sum)
    )
    updated = [query_acc]
    return (tuple(updated), key_sum, value_sum)


def local(queries, cache_keys, cache_values, saved_out, out_grads, log_sums):
    group_count = lax.axis_size("section")
    seq_count = lax.axis_size("seq")
    seq_index = lax.axis_index("seq")
    row_count = queries.shape[1]
    head_dim = cache_keys.shape[1]
    group_width = queries.shape[2] // group_count
    heads_each = log_sums.shape[2] // group_count
    token_count = row_count * seq_count
    tile_rows = min(512, token_count)
    inv_root = 1.0 / math.sqrt(head_dim)
    regrouped = (
        lax.all_to_all(
            queries.reshape(row_count, group_count, group_width),
            "section",
            split_axis=1,
            concat_axis=1,
            tiled=True,
        ),
        lax.all_to_all(
            out_grads.reshape(row_count, group_count, group_width),
            "section",
            split_axis=1,
            concat_axis=1,
            tiled=True,
        ),
        lax.all_to_all(
            saved_out.reshape(row_count, group_count, group_width),
            "section",
            split_axis=1,
            concat_axis=1,
            tiled=True,
        ),
        lax.all_to_all(
            log_sums.reshape(row_count, group_count, heads_each),
            "section",
            split_axis=1,
            concat_axis=1,
            tiled=True,
        ),
    )
    layer_count = regrouped[0].shape[1]
    prepared = [prepare(regrouped, seq_index * row_count, head_dim)]
    query_accs = tuple(
        (jnp.zeros((group_data[0].shape[0], head_dim), jnp.float32) for group_data in prepared)
    )
    empty_sum = jnp.zeros((token_count, head_dim), jnp.float32)
    initial = (query_accs, empty_sum, empty_sum)
    key_all, value_all = (
        lax.all_gather(cache_keys, "seq", axis=0, tiled=True),
        lax.all_gather(cache_values, "seq", axis=0, tiled=True),
    )
    last_pos = prepared[0][5]
    tile_total = last_pos // tile_rows + 1

    def sweep(tile_index, state):
        key_start = tile_index * tile_rows
        key_tile = lax.dynamic_slice_in_dim(key_all, key_start, tile_rows, 0)
        value_tile = lax.dynamic_slice_in_dim(value_all, key_start, tile_rows, 0)
        return apply_tiles(prepared, state, key_tile, value_tile, key_start, inv_root)

    totals = lax.fori_loop(0, tile_total, sweep, initial)
    query_accs, key_sum, value_sum = totals
    key_part, value_part = (
        lax.psum_scatter(key_sum, "seq", scatter_dimension=0, tiled=True),
        lax.psum_scatter(value_sum, "seq", scatter_dimension=0, tiled=True),
    )
    key_grads = key_part.astype(jnp.bfloat16)
    value_grads = value_part.astype(jnp.bfloat16)
    finished = [
        query_acc.reshape(-1, layer_count, group_width).astype(jnp.bfloat16)
        for query_acc in query_accs
    ]
    query_rows = finished[0]
    home_rows = lax.all_to_all(query_rows, "section", split_axis=1, concat_axis=1, tiled=True)
    query_grads = home_rows.reshape(1, row_count, group_count * group_width)
    return (query_grads, key_grads, value_grads)


def solution(mesh):
    placed = (
        P("section", "seq", None),
        P("seq", "section"),
        P("seq", "section"),
        P("section", "seq", None),
        P("section", "seq", None),
        P("section", "seq", None),
    )
    return jax.shard_map(
        local,
        mesh=mesh,
        in_specs=placed,
        out_specs=(P("section", "seq", None), P("seq", "section"), P("seq", "section")),
        check_vma=False,
    )
```

profile of v0, /device:TPU:0, one launch (start us, length us, event | category | flops | bytes accessed | tf_op | source)
XLA Modules:
  0.0 269.7 jit_solution(15459894053254621763)
XLA Ops:
  7.2 1.4 reshape.45
  8.5 4.2 %all-to-all-start.1 = ((bf16[128,4,5]{0,2,1:T(8,128)(2,1)}), bf16[128,4,5]{0,2,1:T(8,128)(2,1)S(1)}, u32[]{:S(2)}, u32[]{:S(2)}) async-start(bf16[128,4,5]{0,2,1:T(8,128)(2,1)} %reshape.45), calls=%async_computation.1 | async-start | bytes 16384 | tf_op jit(solution)/shard_map/all_to_all | solution.py:130
  12.8 1.4 copy.11
  14.2 1.1 copy.12
  15.3 1.3 all-to-all-done.1
  16.6 3.5 %all-to-all-start = ((bf16[128,4,640]{2,0,1:T(8,128)(2,1)}), bf16[128,4,640]{2,0,1:T(8,128)(2,1)S(1)}, u32[]{:S(2)}, u32[]{:S(2)}) async-start(bf16[128,4,640]{2,0,1:T(8,128)(2,1)} %copy.12), calls=%async_computation | async-start | bytes 1310720 | tf_op jit(solution)/shard_map/all_to_all | solution.py:109
  20.1 0.3 copy.15
  20.4 1.1 copy.16
  21.5 8.8 %all-to-all-done = bf16[128,4,640]{2,0,1:T(8,128)(2,1)S(1)} async-done(((bf16[128,4,640]{2,0,1:T(8,128)(2,1)}), bf16[128,4,640]{2,0,1:T(8,128)(2,1)S(1)}, u32[]{:S(2)}, u32[]{:S(2)}) %all-to-all-start) | async-done | bytes 655392 | tf_op jit(solution)/shard_map/all_to_all | solution.py:109
  30.3 3.5 %all-to-all-start.2 = ((bf16[128,4,640]{2,0,1:T(8,128)(2,1)}), bf16[128,4,640]{2,0,1:T(8,128)(2,1)S(1)}, u32[]{:S(2)}, u32[]{:S(2)}) async-start(bf16[128,4,640]{2,0,1:T(8,128)(2,1)} %copy.16), calls=%async_computation.2 | async-start | bytes 1310720 | tf_op jit(solution)/shard_map/all_to_all | solution.py:116
  33.8 0.3 copy.18
  34.1 1.1 copy.19
  35.2 8.8 %all-to-all-done.2 = bf16[128,4,640]{2,0,1:T(8,128)(2,1)S(1)} async-done(((bf16[128,4,640]{2,0,1:T(8,128)(2,1)}), bf16[128,4,640]{2,0,1:T(8,128)(2,1)S(1)}, u32[]{:S(2)}, u32[]{:S(2)}) %all-to-all-start.2) | async-done | bytes 655392 | tf_op jit(solution)/shard_map/all_to_all | solution.py:116
  44.0 3.5 %all-to-all-start.3 = ((bf16[128,4,640]{2,0,1:T(8,128)(2,1)}), bf16[128,4,640]{2,0,1:T(8,128)(2,1)S(1)}, u32[]{:S(2)}, u32[]{:S(2)}) async-start(bf16[128,4,640]{2,0,1:T(8,128)(2,1)} %copy.19), calls=%async_computation.3 | async-start | bytes 1310720 | tf_op jit(solution)/shard_map/all_to_all | solution.py:123
  47.6 31.7 %all_gather.6 = bf16[1024,128]{1,0:T(8,128)(2,1)S(1)} all-gather(bf16[128,128]{1,0:T(8,128)(2,1)S(1)} %copy-done.6), channel_id=1, replica_groups=mesh['section'=4,'seq'=8] {'seq'}, dimensions={0}, use_global_device_ids=true | all-gather | bytes 294912 | tf_op jit(solution)/shard_map/all_gather | solution.py:146
  79.2 32.9 %all_gather.7 = bf16[1024,128]{1,0:T(8,128)(2,1)} all-gather(bf16[128,128]{1,0:T(8,128)(2,1)S(1)} %copy-done.7), channel_id=1, replica_groups=mesh['section'=4,'seq'=8] {'seq'}, dimensions={0}, use_global_device_ids=true | all-gather | bytes 294912 | tf_op jit(solution)/shard_map/all_gather | solution.py:147
  112.1 0.2 copy.14
  112.3 0.3 reshape.51
  112.6 0.5 copy.13
  113.1 0.2 reshape.44
  113.3 1.3 copy.17
  114.7 1.6 reshape.47
  116.3 0.1 convert_multiply_fusion
  116.4 0.8 copy.20
  117.3 1.6 reshape.49
  118.9 1.7 reduce_sum.9
  120.6 0.8 broadcast_in_dim.17
  121.5 0.1 broadcast_in_dim.16
  121.6 5.5 %while.15 = (s32[]{:T(128)}, f32[2560,128]{1,0:T(8,128)S(1)}, f32[1024,128]{1,0:T(8,128)}, f32[1024,128]{1,0:T(8,128)S(1)}, s32[]{:T(128)}, /*index=5*/s32[]{:T(...) while((s32[]{:T(128)}, f32[2560,128]{1,0:T(8,128)S(1)}, ...), condition=%wide.region_4.5_spmd.clone, body=%wide.region_1.4_spmd.clone.sunk | while | flops 1690000384 | bytes 35654152 | solution.py:158
  121.6 5.5 %conditional.3 = ((f32[2560,128]{1,0:T(8,128)S(1)}, f32[1024,128]{1,0:T(8,128)}, f32[1024,128]{1,0:T(8,128)S(1)})) conditional(s32[]{:T(128)} %convert_element_type.61, (f32[2560,128]{1,0:T(8,128)S(1)}, f32[1024,128]{1,0:T(8,128)}, f32[1024,128]{1,0:T(8,128)S(1)}) %tuple.51, (s32[]{:T(128)}, s32[]{:T(128)}, bf16[1024,128]{1,0:T(8,128)(2,1)S(1)}, ...), branch_computations={%region_2.2_spmd, %region_3.3_spmd.clone} | conditional | flops 1689997824 | bytes 35623096 | solution.py:90
  121.7 0.2 fusion.16
  121.8 1.3 bitcast_select_fusion
  123.2 0.9 fusion.9
  124.1 0.9 fusion.3
  125.0 0.2 copy-done.1
  125.1 0.9 fusion.12
  126.0 1.1 convolution_add_fusion
  127.1 0.8 copy-done
  128.0 0.7 reduce-scatter.3.cloned.1.call-update
  128.8 0.3 convert_element_type.44
  129.1 0.1 copy.21
  129.1 13.1 %all_to_all.25 = bf16[128,4,640]{2,0,1:T(8,128)(2,1)S(1)} all-to-all(bf16[128,4,640]{2,0,1:T(8,128)(2,1)S(1)} %copy.21), channel_id=1, replica_groups=mesh['section'=4,'seq'=8] {'section'}, dimensions={1} | all-to-all | bytes 1310720 | tf_op jit(solution)/shard_map/all_to_all | solution.py:171
  142.2 0.3 copy.22
  142.6 1.1 copy.23
  143.6 53.1 %reduce-scatter.5.cloned.1.call-done = f32[128,128]{1,0:T(8,128)} async-done(((f32[1024,128]{1,0:T(8,128)}), f32[128,128]{1,0:T(8,128)}) %reduce-scatter.5.cloned.1.call-update) | async-done | bytes 65552 | tf_op jit(solution)/shard_map/reduce_scatter | solution.py:162
  196.7 1.5 convert_element_type.46
  198.2 63.2 %reduce-scatter.3.cloned.1.call-done = f32[128,128]{1,0:T(8,128)} async-done(((f32[1024,128]{1,0:T(8,128)}), f32[128,128]{1,0:T(8,128)}) %reduce-scatter.3.cloned.1.call-update) | async-done | bytes 65552 | tf_op jit(solution)/shard_map/reduce_scatter | solution.py:161
  261.4 1.5 convert_element_type.45
  (24 shorter events, 0.3 us)
Async XLA Ops:
  7.2 12.9 %copy-start.4 = (bf16[1,128,2560]{2,1,0:T(8,128)(2,1)S(1)}, bf16[1,128,2560]{2,1,0:T(8,128)(2,1)}, u32[]{:S(2)}) copy-start(bf16[1,128,2560]{2,1,0:T(8,128)(2,1)} %param.14) | copy-start | bytes 1966084
  8.5 8.1 %all-to-all-start.1 = ((bf16[128,4,5]{0,2,1:T(8,128)(2,1)}), bf16[128,4,5]{0,2,1:T(8,128)(2,1)S(1)}, u32[]{:S(2)}, u32[]{:S(2)}) async-start(bf16[128,4,5]{0,2,1:T(8,128)(2,1)} %reshape.45), calls=%async_computation.1 | async-start | bytes 16384 | tf_op jit(solution)/shard_map/all_to_all | solution.py:130
  15.3 18.5 %copy-start.5 = (bf16[1,128,2560]{2,1,0:T(8,128)(2,1)S(1)}, bf16[1,128,2560]{2,1,0:T(8,128)(2,1)}, u32[]{:S(2)}) copy-start(bf16[1,128,2560]{2,1,0:T(8,128)(2,1)} %param.13) | copy-start | bytes 1966084
  16.6 13.7 %all-to-all-start = ((bf16[128,4,640]{2,0,1:T(8,128)(2,1)}), bf16[128,4,640]{2,0,1:T(8,128)(2,1)S(1)}, u32[]{:S(2)}, u32[]{:S(2)}) async-start(bf16[128,4,640]{2,0,1:T(8,128)(2,1)} %copy.12), calls=%async_computation | async-start | bytes 1310720 | tf_op jit(solution)/shard_map/all_to_all | solution.py:109
  21.5 26.0 %copy-start.6 = (bf16[128,128]{1,0:T(8,128)(2,1)S(1)}, bf16[128,128]{1,0:T(8,128)(2,1)}, u32[]{:S(2)}) copy-start(bf16[128,128]{1,0:T(8,128)(2,1)} %param.11) | copy-start | bytes 98308
  21.5 57.7 %copy-start.7 = (bf16[128,128]{1,0:T(8,128)(2,1)S(1)}, bf16[128,128]{1,0:T(8,128)(2,1)}, u32[]{:S(2)}) copy-start(bf16[128,128]{1,0:T(8,128)(2,1)} %param.12) | copy-start | bytes 98308
  30.3 13.7 %all-to-all-start.2 = ((bf16[128,4,640]{2,0,1:T(8,128)(2,1)}), bf16[128,4,640]{2,0,1:T(8,128)(2,1)S(1)}, u32[]{:S(2)}, u32[]{:S(2)}) async-start(bf16[128,4,640]{2,0,1:T(8,128)(2,1)} %copy.16), calls=%async_computation.2 | async-start | bytes 1310720 | tf_op jit(solution)/shard_map/all_to_all | solution.py:116
  44.0 72.3 %all-to-all-start.3 = ((bf16[128,4,640]{2,0,1:T(8,128)(2,1)}), bf16[128,4,640]{2,0,1:T(8,128)(2,1)S(1)}, u32[]{:S(2)}, u32[]{:S(2)}) async-start(bf16[128,4,640]{2,0,1:T(8,128)(2,1)} %copy.19), calls=%async_computation.3 | async-start | bytes 1310720 | tf_op jit(solution)/shard_map/all_to_all | solution.py:123
  47.5 149.2 %reduce-scatter.5.cloned.1.call-start = ((), (), s32[]{:S(2)}) async-start(), calls=%async_computation.8 | async-start | bytes 589824 | tf_op jit(solution)/shard_map/reduce_scatter | solution.py:162
  123.1 1.0 copy-start.3
  124.1 1.0 copy-start.1
  126.0 1.1 copy-start.2
  127.1 0.8 copy-start
  127.9 133.5 %reduce-scatter.3.cloned.1.call-start = ((), (), s32[]{:S(2)}) async-start(), calls=%async_computation.7 | async-start | bytes 589824 | tf_op jit(solution)/shard_map/reduce_scatter | solution.py:161
Sparse Core Ops, SparseCore 0:
  128.1 68.6 reduce-scatter.4
  200.4 60.9 reduce-scatter.2
where the time goes:
time: 270 us
  waiting for transfers between devices  136 us (50%)
  blocking collectives  77.6 us (29%)
  local copies, waits for them, and re-layouts  17.1 us (6%)
  starting transfers between devices  14.8 us (5%)
  between operations  14.3 us (5%)
  other arithmetic  5 us (2%)
  matrix products  4.98 us (2%)
    reduce_scatter x1, waiting for transfers between devices, local(): lax.psum_scatter(key_sum, 'seq', scatter_dimension=0, tiled=True)  63.2 us
    reduce_scatter x1, waiting for transfers between devices, local(): lax.psum_scatter(value_sum, 'seq', scatter_dimension=0, tiled=True)  53.1 us
    all_gather x1, blocking collectives, local(): lax.all_gather(cache_values, 'seq', axis=0, tiled=True)  32.9 us
    all_gather x1, blocking collectives, local(): lax.all_gather(cache_keys, 'seq', axis=0, tiled=True)  31.7 us
    all_to_all x1, blocking collectives, local(): lax.all_to_all(query_rows, 'section', split_axis=1, concat_axis=1, tiled=...  13.1 us
    all_to_all x1, waiting for transfers between devices, local(): lax.all_to_all(out_grads.reshape(row_count, group_count, group_width), 's...  8.78 us
    all_to_all x1, waiting for transfers between devices, local(): lax.all_to_all(queries.reshape(row_count, group_count, group_width), 'sec...  8.76 us
  transfers between devices with their start and end apart: 6, of which 5 were waited for; matrix products, arithmetic and copies ran while one was open for 5% of the time, Pallas kernels for 0%

commit v1 on v0

v1 whole, which is shorter than its diff:
```python
import functools
import math

import jax
import jax.numpy as jnp
from jax import lax
from jax.experimental import pallas as pl
from jax.experimental.pallas import tpu as pltpu
from jax.sharding import PartitionSpec as P

NT_DIMS = (((1,), (1,)), ((), ()))
EXTRA = 4
VMEM_LIMIT = 32 * 1024 * 1024
SMEM = pl.BlockSpec(memory_space=pltpu.SMEM)
VMEM = pl.BlockSpec(memory_space=pltpu.VMEM)


def up16(rows):
    return -(-rows // 16) * 16


def pack_kernel(heads, head, places, queries, grads, saved, totals, *messages):
    rows = queries.shape[0]
    width = heads * head
    all_heads = queries.shape[1] // head
    lanes = lax.broadcasted_iota(jnp.int32, (rows, 128), 1)
    dots = jnp.zeros((rows, 128), jnp.float32)
    for h in range(all_heads):
        cols = slice(h * head, (h + 1) * head)
        product = grads[:, cols].astype(jnp.float32) * saved[:, cols].astype(jnp.float32)
        dots = jnp.where(lanes == h, jnp.sum(product, axis=1, keepdims=True), dots)
    dots_rows = jnp.transpose(dots)
    high = dots_rows.astype(jnp.bfloat16).astype(jnp.float32)
    rest = dots_rows - high
    middle = rest.astype(jnp.bfloat16).astype(jnp.float32)
    low = rest - middle
    padded = jnp.concatenate(
        [totals[...].astype(jnp.float32), jnp.zeros((rows, 128 - all_heads), jnp.float32)], axis=1
    )
    totals_rows = jnp.transpose(padded)
    parts = (totals_rows, high, middle, low)
    groups = all_heads // heads
    for k, message in enumerate(messages):
        place = places[k]
        start = pl.multiple_of(place * width, 128)
        for h in range(heads):
            at = pl.multiple_of(start + h * head, 128)
            message[h * rows : (h + 1) * rows, :] = queries[:, pl.ds(at, head)]
            message[(heads + h) * rows : (heads + h + 1) * rows, :] = grads[:, pl.ds(at, head)]
        blocks = []
        for part in parts:
            chosen = part[0:heads, :]
            for group in range(1, groups):
                chosen = jnp.where(
                    place == group, part[group * heads : (group + 1) * heads, :], chosen
                )
            blocks.append(chosen)
        extra = jnp.concatenate(blocks, axis=0)
        lines = message.shape[0] - 2 * heads * rows
        extra = jnp.concatenate(
            [extra, jnp.zeros((lines - extra.shape[0], 128), jnp.float32)], axis=0
        )
        message[2 * heads * rows :, :] = extra.astype(jnp.bfloat16)


def attend_kernel(layers, heads, head, outer, inv_root, info, *refs):
    messages = refs[:layers]
    own_blocks = refs[layers : layers + outer]
    other_blocks = refs[layers + outer]
    refs = refs[layers + outer + 1 :]
    query_outs = refs[:layers]
    mine, theirs = refs[layers : layers + 2]
    keys, values, query_all, grad_all, query_acc, sums = refs[layers + 2 :]
    rows = own_blocks[0].shape[0]
    pair = 2 * rows
    z, x = info[0], info[1]
    per_layer = heads * rows
    for k in range(outer):
        at = pl.multiple_of((z ^ k) * pair, pair)
        keys[pl.ds(at + x * rows, rows), :] = own_blocks[k][:, :head]
        values[pl.ds(at + x * rows, rows), :] = own_blocks[k][:, head:]
        keys[pl.ds(at + (1 - x) * rows, rows), :] = other_blocks[k, :, :head]
        values[pl.ds(at + (1 - x) * rows, rows), :] = other_blocks[k, :, head:]
    for layer in range(layers):
        there = slice(layer * per_layer, (layer + 1) * per_layer)
        query_all[there, :] = messages[layer][:per_layer, :]
        grad_all[there, :] = messages[layer][per_layer : 2 * per_layer, :]
    query_acc[...] = jnp.zeros_like(query_acc)
    chunks = [
        [(c // heads, c % heads) for c in range(i, min(i + 2, layers * heads))]
        for i in range(0, layers * heads, 2)
    ]

    def line(layer, h, part):
        at = 2 * per_layer + part * heads + h
        return messages[layer][at : at + 1, :].astype(jnp.float32)

    def sweep(j, masked):
        at = pl.multiple_of(j * pair, pair)
        key_tile = keys[pl.ds(at, pair), :]
        value_tile = values[pl.ds(at, pair), :]
        key_turned = jnp.transpose(key_tile)
        key_sum = jnp.zeros((pair, head), jnp.float32)
        value_sum = jnp.zeros((pair, head), jnp.float32)
        for chunk in chunks:
            first = (chunk[0][0] * heads + chunk[0][1]) * rows
            wide = len(chunk) * rows
            query = query_all[first : first + wide, :]
            grad = grad_all[first : first + wide, :]
            total = jnp.concatenate([line(a, b, 0) for a, b in chunk], axis=1)
            dot = jnp.concatenate(
                [line(a, b, 1) + (line(a, b, 2) + line(a, b, 3)) for a, b in chunk], axis=1
            )
            scores = lax.dot_general(key_tile, query, NT_DIMS, preferred_element_type=jnp.float32)
            weights = jnp.exp(scores * inv_root - total)
            if masked:
                key_pos = lax.broadcasted_iota(jnp.int32, (pair, wide), 0)
                query_pos = lax.broadcasted_iota(jnp.int32, (pair, wide), 1) % rows + x * rows
                weights = jnp.where(key_pos <= query_pos, weights, 0.0)
            weight_grads = lax.dot_general(
                value_tile, grad, NT_DIMS, preferred_element_type=jnp.float32
            )
            score_grads = (weights * (weight_grads - dot) * inv_root).astype(jnp.bfloat16)
            value_sum += jnp.dot(
                weights.astype(jnp.bfloat16), grad, preferred_element_type=jnp.float32
            )
            key_sum += jnp.dot(score_grads, query, preferred_element_type=jnp.float32)
            query_acc[:, first : first + wide] += jnp.dot(
                key_turned, score_grads, preferred_element_type=jnp.float32
            )
        sums[:, :head] = key_sum
        sums[:, head:] = value_sum
        place = j ^ z
        mine[place] = sums[pl.ds(pl.multiple_of(x * rows, rows), rows), :].astype(jnp.bfloat16)
        theirs[place] = sums[pl.ds(pl.multiple_of((1 - x) * rows, rows), rows), :].astype(
            jnp.bfloat16
        )

    def blank(j, carry):
        mine[j ^ z] = jnp.zeros(mine.shape[1:], jnp.bfloat16)
        theirs[j ^ z] = jnp.zeros(theirs.shape[1:], jnp.bfloat16)
        return carry

    def full(j, carry):
        sweep(j, False)
        return carry

    lax.fori_loop(0, z, full, 0)
    sweep(z, True)
    lax.fori_loop(z + 1, outer, blank, 0)
    for layer in range(layers):
        for h in range(heads):
            at = (layer * heads + h) * rows
            query_outs[layer][h * rows : (h + 1) * rows, :] = jnp.transpose(
                query_acc[:, at : at + rows]
            ).astype(jnp.bfloat16)


def add_kernel(mine, theirs, *outs):
    for k, out in enumerate(outs):
        out[...] = (mine[k].astype(jnp.float32) + theirs[k].astype(jnp.float32)).astype(
            jnp.bfloat16
        )


def place_kernel(heads, head, places, *refs):
    messages, out = refs[:-1], refs[-1]
    rows = out.shape[0]
    for k, message in enumerate(messages):
        start = pl.multiple_of(places[k] * heads * head, 128)
        for h in range(heads):
            at = pl.multiple_of(start + h * head, 128)
            out[:, pl.ds(at, head)] = message[h * rows : (h + 1) * rows, :]


def total_kernel(*refs):
    blocks, key_out, value_out = refs[:-2], refs[-2], refs[-1]
    total = blocks[0][...].astype(jnp.float32)
    for block in blocks[1:]:
        total = total + block[...].astype(jnp.float32)
    head = key_out.shape[1]
    key_out[...] = total[:, :head].astype(jnp.bfloat16)
    value_out[...] = total[:, head:].astype(jnp.bfloat16)


def call(kernel, outs, in_specs, scratch=()):
    return pl.pallas_call(
        kernel,
        out_shape=[jax.ShapeDtypeStruct(shape, jnp.bfloat16) for shape in outs],
        in_specs=in_specs,
        out_specs=[VMEM] * len(outs),
        scratch_shapes=list(scratch),
        compiler_params=pltpu.CompilerParams(vmem_limit_bytes=VMEM_LIMIT),
    )


def swap(array, axis, bits):
    size = lax.axis_size(axis)
    return lax.ppermute(array, axis, [(i, i ^ bits) for i in range(size)])


def local(queries, cache_keys, cache_values, saved_out, out_grads, log_sums):
    sections = lax.axis_size("section")
    seq = lax.axis_size("seq")
    outer = seq // 2
    section_at = lax.axis_index("section").astype(jnp.int32)
    seq_at = lax.axis_index("seq").astype(jnp.int32)
    rows, head = cache_keys.shape
    heads = log_sums.shape[2] // sections
    inv_root = 1.0 / math.sqrt(head)
    places = section_at ^ jnp.arange(sections, dtype=jnp.int32)
    info = jnp.stack([seq_at // 2, seq_at % 2])

    own = jnp.concatenate([cache_keys, cache_values], axis=1)
    own_blocks = [own] + [swap(own, "seq", 2 * k) for k in range(1, outer)]
    other_blocks = swap(jnp.stack(own_blocks), "seq", 1)

    lines = 2 * heads * rows + up16(EXTRA * heads)
    sent = call(
        functools.partial(pack_kernel, heads, head),
        [(lines, 128)] * sections,
        [SMEM] + [VMEM] * 4,
    )(places, queries[0], out_grads[0], saved_out[0], log_sums[0])
    messages = [sent[0]] + [swap(sent[k], "section", k) for k in range(1, sections)]

    results = call(
        functools.partial(attend_kernel, sections, heads, head, outer, inv_root),
        [(heads * rows, head)] * sections + [(outer, rows, 2 * head)] * 2,
        [SMEM] + [VMEM] * (sections + outer + 1),
        [
            pltpu.VMEM((seq * rows, head), jnp.bfloat16),
            pltpu.VMEM((seq * rows, head), jnp.bfloat16),
            pltpu.VMEM((sections * heads * rows, head), jnp.bfloat16),
            pltpu.VMEM((sections * heads * rows, head), jnp.bfloat16),
            pltpu.VMEM((head, sections * heads * rows), jnp.float32),
            pltpu.VMEM((2 * rows, 2 * head), jnp.float32),
        ],
    )(info, *messages, *own_blocks, other_blocks)
    mine, theirs = results[sections:]

    arrived = swap(theirs, "seq", 1)
    summed = call(add_kernel, [(rows, 2 * head)] * outer, [VMEM] * 2)(mine, arrived)
    blocks = [summed[0]] + [swap(summed[k], "seq", 2 * k) for k in range(1, outer)]
    key_grads, value_grads = call(total_kernel, [(rows, head)] * 2, [VMEM] * outer)(*blocks)

    back = [results[0]] + [swap(results[k], "section", k) for k in range(1, sections)]
    (query_grads,) = call(
        functools.partial(place_kernel, heads, head),
        [queries.shape[1:]],
        [SMEM] + [VMEM] * sections,
    )(places, *back)
    return (query_grads[None], key_grads, value_grads)


def solution(mesh):
    placed = (
        P("section", "seq", None),
        P("seq", "section"),
        P("seq", "section"),
        P("section", "seq", None),
        P("section", "seq", None),
        P("section", "seq", None),
    )
    return jax.shard_map(
        local,
        mesh=mesh,
        in_specs=placed,
        out_specs=(P("section", "seq", None), P("seq", "section"), P("seq", "section")),
        check_vma=False,
    )
```

time: 270 us -> 60 us (0.22)
  waiting for transfers between devices: 136 us -> 22.9 us
  blocking collectives: 77.6 us -> 0 us
  between operations: 14.3 us -> 0.72 us
  local copies, waits for them, and re-layouts: 17.1 us -> 4.18 us
  starting transfers between devices: 14.8 us -> 24.8 us
  Pallas kernels: 0 us -> 6.99 us
  matrix products: 4.98 us -> 0 us
  other arithmetic: 5 us -> 0.11 us
    reduce_scatter x2 -> x0, waiting for transfers between devices: 116 us -> none  [the longest x1 63.2 us: local(): lax.psum_scatter(key_sum, 'seq', scatter_dimension=0, tiled=True)]
    all_gather x2 -> x0, blocking collectives: 64.5 us -> none  [the longest x1 32.9 us: local(): lax.all_gather(cache_values, 'seq', axis=0, tiled=True)]
    ppermute x0 -> x14, starting transfers between devices: none -> 24.8 us  [swap(): return lax.ppermute(array, axis, [(i, i ^ bits) for i in range(size)])]
    ppermute x0 -> x14, waiting for transfers between devices: none -> 22.9 us  [swap(): return lax.ppermute(array, axis, [(i, i ^ bits) for i in range(size)])]
    all_to_all x4 -> x0, waiting for transfers between devices: 18.9 us -> none  [the longest x1 8.78 us: local(): lax.all_to_all(out_grads.reshape(row_count, group_count, group_width), 's...]
    all_to_all x4 -> x0, starting transfers between devices: 14.7 us -> none  [the longest x1 4.24 us: local(): lax.all_to_all(log_sums.reshape(row_count, group_count, heads_each), 'sec...]
    all_to_all x1 -> x0, blocking collectives: 13.1 us -> none  [local(): lax.all_to_all(query_rows, 'section', split_axis=1, concat_axis=1, tiled=...]
    reshape x7 -> x0, local copies, waits for them, and re-layouts: 8.07 us -> none  [the longest x1 1.6 us: prepare(): row_dots = jnp.sum(products.reshape(-1, head_dim), axis=1)]
  transfers between devices with their start and end apart: 6 -> 14, of which waited for: 5 -> 6; matrix products, arithmetic and copies ran while one was open for 5% -> 0% of each run, Pallas kernels for 0% -> 5%
where the time goes in v1:
time: 60 us; the launch traced here: 59.7 us
  starting transfers between devices  24.8 us (41%)
  waiting for transfers between devices  22.9 us (38%)
  Pallas kernels  6.99 us (12%)
  local copies, waits for them, and re-layouts  4.18 us (7%)
  between operations  0.72 us (1%)
    ppermute x14, starting transfers between devices, swap(): return lax.ppermute(array, axis, [(i, i ^ bits) for i in range(size)])  24.8 us
    ppermute x14, waiting for transfers between devices, swap(): return lax.ppermute(array, axis, [(i, i ^ bits) for i in range(size)])  22.9 us
    unnamed x12, local copies, waits for them, and re-layouts  4.17 us
    pallas_call x1, Pallas kernels, local(): call(functools.partial(attend_kernel, sections, heads, head, outer, inv_r...  3.6 us
    pallas_call x1, Pallas kernels, local(): call(functools.partial(place_kernel, heads, head), [queries.shape[1:]], [...  1.5 us
  transfers between devices with their start and end apart: 14, of which 6 were waited for; matrix products, arithmetic and copies ran while one was open for 0% of the time, Pallas kernels for 5%

profile of v1, /device:TPU:0, one launch (start us, length us, event | category | flops | bytes accessed | tf_op | source)
XLA Modules:
  0.0 59.7 jit_solution(5362797338708303467)
XLA Ops:
  0.6 0.0 copy-start.3
  0.6 0.8 %constant_dynamic-update-slice_fusion.1 = bf16[128,256]{1,0:T(8,128)(2,1)S(1)} fusion(bf16[128,128]{1,0:T(8,128)(2,1)} %param.7), kind=kLoop, calls=%fused_computation.2 | loop fusion | bytes 65536
  1.4 0.0 copy-done.3
  1.4 0.0 copy-start.4
  1.4 5.1 %collective-permute-start.5 = (bf16[128,256]{1,0:T(8,128)(2,1)S(1)}, bf16[128,256]{1,0:T(8,128)(2,1)S(1)}, u32[]{:S(2)}, u32[]{:S(2)}) collective-permute-start(bf16[128,256]{1,0:T(8,128)(2,1)S(1)} %constant_dynamic-update-slice_fusion.refs_4_), channel_id=1, source_target_pairs={{0,6},{1,7},{2,4},{3,5},{4,2},{5,3},{6,0},{7,1},{8,14},{9,15},{10,... | collective-permute-start | bytes 196616 | tf_op jit(solution)/shard_map/ppermute | solution.py:199
  6.6 0.0 collective-permute-start.4
  6.6 0.6 %collective-permute-start.3 = (bf16[128,256]{1,0:T(8,128)(2,1)S(1)}, bf16[128,256]{1,0:T(8,128)(2,1)S(1)}, u32[]{:S(2)}, u32[]{:S(2)}) collective-permute-start(bf16[128,256]{1,0:T(8,128)(2,1)S(1)} %constant_dynamic-update-slice_fusion.refs_4_), channel_id=1, source_target_pairs={{0,2},{1,3},{2,0},{3,1},{4,6},{5,7},{6,4},{7,5},{8,10},{9,11},{10,... | collective-permute-start | bytes 196616 | tf_op jit(solution)/shard_map/ppermute | solution.py:199
  7.2 0.0 copy-done.4
  7.2 0.1 copy.9
  7.3 0.0 copy-start
  7.4 1.1 %copy-done = bf16[1,128,2560]{2,1,0:T(8,128)(2,1)S(1)} copy-done((bf16[1,128,2560]{2,1,0:T(8,128)(2,1)S(1)}, bf16[1,128,2560]{2,1,0:T(8,128)(2,1)}, u32[]{:S(2)}) %copy-start) | copy-done | bytes 655384
  8.4 0.0 copy-start.1
  8.4 1.1 %copy-done.1 = bf16[1,128,2560]{2,1,0:T(8,128)(2,1)S(1)} copy-done((bf16[1,128,2560]{2,1,0:T(8,128)(2,1)S(1)}, bf16[1,128,2560]{2,1,0:T(8,128)(2,1)}, u32[]{:S(2)}) %copy-start.1) | copy-done | bytes 655384
  9.5 0.0 copy-start.2
  9.5 1.1 %copy-done.2 = bf16[1,128,2560]{2,1,0:T(8,128)(2,1)S(1)} copy-done((bf16[1,128,2560]{2,1,0:T(8,128)(2,1)S(1)}, bf16[1,128,2560]{2,1,0:T(8,128)(2,1)}, u32[]{:S(2)}) %copy-start.2) | copy-done | bytes 655384
  10.6 1.2 %shard_map.85 = (bf16[1312,128]{1,0:T(8,128)(2,1)S(1)}, bf16[1312,128]{1,0:T(8,128)(2,1)S(1)}, bf16[1312,128]{1,0:T(8,128)(2,1)S(1)}, bf16[1312,128]{1,0:T(8,128)(2,1)S(1)}) custom-call(s32[4]{0:T(128)S(1)} %iota_xor_fusion.places, bf16[128,2560]{1,0:T(8,128)(2,1)S(1)} %bitcast.11, bf16[128,2560]{1,0:T(8,128)(2,1)S(1)} %bitcast.12, ...), custom_call_target="tpu_custom_call" | custom-call | tf_op jit(solution)/shard_map/pallas_call | solution.py:219
  11.8 0.1 collective-permute-start
  11.9 1.7 %collective-permute-start.1 = (bf16[1312,128]{1,0:T(8,128)(2,1)S(1)}, bf16[1312,128]{1,0:T(8,128)(2,1)S(1)}, u32[]{:S(2)}, u32[]{:S(2)}) collective-permute-start(bf16[1312,128]{1,0:T(8,128)(2,1)S(1)} %get-tuple-element.21), channel_id=1, source_target_pairs={{0,16},{8,24},{16,0},{24,8},{1,17},{9,25},{17,1},{25,9},{2,18},{10... | collective-permute-start | bytes 1007624 | tf_op jit(solution)/shard_map/ppermute | solution.py:199
  13.6 0.0 collective-permute-done.5.refs_7_
  13.6 0.1 collective-permute-start.2
  13.7 0.0 collective-permute-done.4.refs_6_
  13.7 0.0 collective-permute-done.3.refs_5_
  13.8 1.7 %collective-permute-start.6 = (bf16[4,128,256]{2,1,0:T(8,128)(2,1)S(1)}, bf16[4,128,256]{2,1,0:T(8,128)(2,1)S(1)}, u32[]{:S(2)}, u32[]{:S(2)}) collective-permute-start(bf16[4,128,256]{2,1,0:T(8,128)(2,1)S(1)} %pad_maximum_fusion), channel_id=1, source_target_pairs={{0,1},{1,0},{2,3},{3,2},{4,5},{5,4},{6,7},{7,6},{8,9},{9,8},{10,11... | collective-permute-start | bytes 786440 | tf_op jit(solution)/shard_map/ppermute | solution.py:199
  15.5 0.1 pad_add_fusion.info
  15.6 6.8 %collective-permute-done.6.refs_8_ = bf16[4,128,256]{2,1,0:T(8,128)(2,1)S(1)} collective-permute-done((bf16[4,128,256]{2,1,0:T(8,128)(2,1)S(1)}, bf16[4,128,256]{2,1,0:T(8,128)(2,1)S(1)}, u32[]{:S(2)}, u32[]{:S(2)}) %collective-permute-start.6) | collective-permute-done | bytes 262176 | tf_op jit(solution)/shard_map/ppermute | solution.py:199
  22.4 0.0 collective-permute-done.refs_1_
  22.4 0.2 collective-permute-done.1.refs_2_
  22.6 6.3 %collective-permute-done.2.refs_3_ = bf16[1312,128]{1,0:T(8,128)(2,1)S(1)} collective-permute-done((bf16[1312,128]{1,0:T(8,128)(2,1)S(1)}, bf16[1312,128]{1,0:T(8,128)(2,1)S(1)}, u32[]{:S(2)}, u32[]{:S(2)}) %collective-permute-start.2) | collective-permute-done | bytes 335904 | tf_op jit(solution)/shard_map/ppermute | solution.py:199
  28.9 3.6 %shard_map.86 = (bf16[640,128]{1,0:T(8,128)(2,1)S(1)}, bf16[640,128]{1,0:T(8,128)(2,1)S(1)}, bf16[640,128]{1,0:T(8,128)(2,1)S(1)}, bf16[640,128]{1,0:T(8,128)(2,...) custom-call(s32[2]{0:T(128)S(1)} %pad_add_fusion.info, ...), custom_call_target="tpu_custom_call" | custom-call | tf_op jit(solution)/shard_map/pallas_call | solution.py:226
  32.5 1.7 %collective-permute-start.10 = (bf16[4,128,256]{2,1,0:T(8,128)(2,1)S(1)}, bf16[4,128,256]{2,1,0:T(8,128)(2,1)S(1)}, u32[]{:S(2)}, u32[]{:S(2)}) collective-permute-start(bf16[4,128,256]{2,1,0:T(8,128)(2,1)S(1)} %get-tuple-element.28), channel_id=1, source_target_pairs={{0,1},{1,0},{2,3},{3,2},{4,5},{5,4},{6,7},{7,6},{8,9},{9,8},{10,11... | collective-permute-start | bytes 786440 | tf_op jit(solution)/shard_map/ppermute | solution.py:199
  34.2 0.0 collective-permute-start.7
  34.2 1.5 %collective-permute-start.8 = (bf16[640,128]{1,0:T(8,128)(2,1)S(1)}, bf16[640,128]{1,0:T(8,128)(2,1)S(1)}, u32[]{:S(2)}, u32[]{:S(2)}) collective-permute-start(bf16[640,128]{1,0:T(8,128)(2,1)S(1)} %get-tuple-element.25), channel_id=1, source_target_pairs={{0,16},{8,24},{16,0},{24,8},{1,17},{9,25},{17,1},{25,9},{2,18},{10... | collective-permute-start | bytes 491528 | tf_op jit(solution)/shard_map/ppermute | solution.py:199
  35.7 0.3 collective-permute-start.9
  36.1 5.0 %collective-permute-done.10.theirs = bf16[4,128,256]{2,1,0:T(8,128)(2,1)S(1)} collective-permute-done((bf16[4,128,256]{2,1,0:T(8,128)(2,1)S(1)}, bf16[4,128,256]{2,1,0:T(8,128)(2,1)S(1)}, u32[]{:S(2)}, u32[]{:S(2)}) %collective-permute-start.10) | collective-permute-done | bytes 262176 | tf_op jit(solution)/shard_map/ppermute | solution.py:199
  41.1 0.1 shard_map.88
  41.1 3.9 %collective-permute-start.11 = (bf16[128,256]{1,0:T(8,128)(2,1)S(1)}, bf16[128,256]{1,0:T(8,128)(2,1)S(1)}, u32[]{:S(2)}, u32[]{:S(2)}) collective-permute-start(bf16[128,256]{1,0:T(8,128)(2,1)S(1)} %get-tuple-element.30), channel_id=1, source_target_pairs={{0,2},{1,3},{2,0},{3,1},{4,6},{5,7},{6,4},{7,5},{8,10},{9,11},{10,... | collective-permute-start | bytes 196616 | tf_op jit(solution)/shard_map/ppermute | solution.py:199
  45.1 7.9 %collective-permute-start.12 = (bf16[128,256]{1,0:T(8,128)(2,1)S(1)}, bf16[128,256]{1,0:T(8,128)(2,1)S(1)}, u32[]{:S(2)}, u32[]{:S(2)}) collective-permute-start(bf16[128,256]{1,0:T(8,128)(2,1)S(1)} %get-tuple-element.31), channel_id=1, source_target_pairs={{0,4},{1,5},{2,6},{3,7},{4,0},{5,1},{6,2},{7,3},{8,12},{9,13},{10,... | collective-permute-start | bytes 196616 | tf_op jit(solution)/shard_map/ppermute | solution.py:199
  53.0 0.0 collective-permute-done.7.refs_1_
  53.0 0.0 collective-permute-start.13
  53.0 0.0 collective-permute-done.8.refs_2_
  53.0 0.0 collective-permute-done.9.refs_3_
  53.0 1.5 %shard_map.87 = bf16[128,2560]{1,0:T(8,128)(2,1)} custom-call(s32[4]{0:T(128)S(1)} %iota_xor_fusion.places, bf16[640,128]{1,0:T(8,128)(2,1)S(1)} %get-tuple-element.23.refs_0_, bf16[640,128]{1,0:T(8,128)(2,1)S(1)} %collective-permute-done.7.refs_1_, bf16[640,128]{1,0:T(8,128)(2,1)S(1)} %collective-permute-done.8.refs_2_, ...), custom_call_target="tpu_custom_call" | custom-call | tf_op jit(solution)/shard_map/pallas_call | solution.py:247
  54.5 0.0 collective-permute-done.11.refs_1_
  54.5 2.7 %collective-permute-done.12.refs_2_ = bf16[128,256]{1,0:T(8,128)(2,1)S(1)} collective-permute-done((bf16[128,256]{1,0:T(8,128)(2,1)S(1)}, bf16[128,256]{1,0:T(8,128)(2,1)S(1)}, u32[]{:S(2)}, u32[]{:S(2)}) %collective-permute-start.12) | collective-permute-done | bytes 65568 | tf_op jit(solution)/shard_map/ppermute | solution.py:199
  57.2 1.8 %collective-permute-done.13.refs_3_ = bf16[128,256]{1,0:T(8,128)(2,1)S(1)} collective-permute-done((bf16[128,256]{1,0:T(8,128)(2,1)S(1)}, bf16[128,256]{1,0:T(8,128)(2,1)S(1)}, u32[]{:S(2)}, u32[]{:S(2)}) %collective-permute-start.13) | collective-permute-done | bytes 65568 | tf_op jit(solution)/shard_map/ppermute | solution.py:199
  59.0 0.7 %shard_map.89 = (bf16[128,128]{1,0:T(8,128)(2,1)}, bf16[128,128]{1,0:T(8,128)(2,1)}) custom-call(bf16[128,256]{1,0:T(8,128)(2,1)S(1)} %get-tuple-element.29.refs_0_, bf16[128,256]{1,0:T(8,128)(2,1)S(1)} %collective-permute-done.11.refs_1_, bf16[128,256]{1,0:T(8,128)(2,1)S(1)} %collective-permute-done.12.refs_2_, ...), custom_call_target="tpu_custom_call" | custom-call | tf_op jit(solution)/shard_map/pallas_call | solution.py:244
  (3 shorter events, 0.1 us)
Async XLA Ops:
  0.6 0.8 %copy-start.3 = (bf16[128,128]{1,0:T(8,128)(2,1)S(1)}, bf16[128,128]{1,0:T(8,128)(2,1)}, u32[]{:S(2)}) copy-start(bf16[128,128]{1,0:T(8,128)(2,1)} %param.8) | copy-start | bytes 98308
  1.4 5.8 %copy-start.4 = (bf16[1,128,20]{1,2,0:T(8,128)(2,1)S(1)}, bf16[1,128,20]{1,2,0:T(8,128)(2,1)}, u32[]{:S(2)}) copy-start(bf16[1,128,20]{1,2,0:T(8,128)(2,1)} %param.11) | copy-start | bytes 15364
  1.4 12.2 %collective-permute-start.5 = (bf16[128,256]{1,0:T(8,128)(2,1)S(1)}, bf16[128,256]{1,0:T(8,128)(2,1)S(1)}, u32[]{:S(2)}, u32[]{:S(2)}) collective-permute-start(bf16[128,256]{1,0:T(8,128)(2,1)S(1)} %constant_dynamic-update-slice_fusion.refs_4_), channel_id=1, source_target_pairs={{0,6},{1,7},{2,4},{3,5},{4,2},{5,3},{6,0},{7,1},{8,14},{9,15},{10,... | collective-permute-start | bytes 196616 | tf_op jit(solution)/shard_map/ppermute | solution.py:199
  6.6 7.2 %collective-permute-start.4 = (bf16[128,256]{1,0:T(8,128)(2,1)S(1)}, bf16[128,256]{1,0:T(8,128)(2,1)S(1)}, u32[]{:S(2)}, u32[]{:S(2)}) collective-permute-start(bf16[128,256]{1,0:T(8,128)(2,1)S(1)} %constant_dynamic-update-slice_fusion.refs_4_), channel_id=1, source_target_pairs={{0,4},{1,5},{2,6},{3,7},{4,0},{5,1},{6,2},{7,3},{8,12},{9,13},{10,... | collective-permute-start | bytes 196616 | tf_op jit(solution)/shard_map/ppermute | solution.py:199
  6.6 7.2 %collective-permute-start.3 = (bf16[128,256]{1,0:T(8,128)(2,1)S(1)}, bf16[128,256]{1,0:T(8,128)(2,1)S(1)}, u32[]{:S(2)}, u32[]{:S(2)}) collective-permute-start(bf16[128,256]{1,0:T(8,128)(2,1)S(1)} %constant_dynamic-update-slice_fusion.refs_4_), channel_id=1, source_target_pairs={{0,2},{1,3},{2,0},{3,1},{4,6},{5,7},{6,4},{7,5},{8,10},{9,11},{10,... | collective-permute-start | bytes 196616 | tf_op jit(solution)/shard_map/ppermute | solution.py:199
  7.3 1.1 %copy-start = (bf16[1,128,2560]{2,1,0:T(8,128)(2,1)S(1)}, bf16[1,128,2560]{2,1,0:T(8,128)(2,1)}, u32[]{:S(2)}) copy-start(bf16[1,128,2560]{2,1,0:T(8,128)(2,1)} %param.6) | copy-start | bytes 1966084
  8.4 1.1 %copy-start.1 = (bf16[1,128,2560]{2,1,0:T(8,128)(2,1)S(1)}, bf16[1,128,2560]{2,1,0:T(8,128)(2,1)}, u32[]{:S(2)}) copy-start(bf16[1,128,2560]{2,1,0:T(8,128)(2,1)} %param.10) | copy-start | bytes 1966084
  9.5 1.1 %copy-start.2 = (bf16[1,128,2560]{2,1,0:T(8,128)(2,1)S(1)}, bf16[1,128,2560]{2,1,0:T(8,128)(2,1)}, u32[]{:S(2)}) copy-start(bf16[1,128,2560]{2,1,0:T(8,128)(2,1)} %param.9) | copy-start | bytes 1966084
  11.8 10.6 %collective-permute-start = (bf16[1312,128]{1,0:T(8,128)(2,1)S(1)}, bf16[1312,128]{1,0:T(8,128)(2,1)S(1)}, u32[]{:S(2)}, u32[]{:S(2)}) collective-permute-start(bf16[1312,128]{1,0:T(8,128)(2,1)S(1)} %get-tuple-element.20), channel_id=1, source_target_pairs={{0,8},{8,0},{16,24},{24,16},{1,9},{9,1},{17,25},{25,17},{2,10},{10... | collective-permute-start | bytes 1007624 | tf_op jit(solution)/shard_map/ppermute | solution.py:199
  11.9 10.8 %collective-permute-start.1 = (bf16[1312,128]{1,0:T(8,128)(2,1)S(1)}, bf16[1312,128]{1,0:T(8,128)(2,1)S(1)}, u32[]{:S(2)}, u32[]{:S(2)}) collective-permute-start(bf16[1312,128]{1,0:T(8,128)(2,1)S(1)} %get-tuple-element.21), channel_id=1, source_target_pairs={{0,16},{8,24},{16,0},{24,8},{1,17},{9,25},{17,1},{25,9},{2,18},{10... | collective-permute-start | bytes 1007624 | tf_op jit(solution)/shard_map/ppermute | solution.py:199
  13.6 15.3 %collective-permute-start.2 = (bf16[1312,128]{1,0:T(8,128)(2,1)S(1)}, bf16[1312,128]{1,0:T(8,128)(2,1)S(1)}, u32[]{:S(2)}, u32[]{:S(2)}) collective-permute-start(bf16[1312,128]{1,0:T(8,128)(2,1)S(1)} %get-tuple-element.22), channel_id=1, source_target_pairs={{0,24},{8,16},{16,8},{24,0},{1,25},{9,17},{17,9},{25,1},{2,26},{10... | collective-permute-start | bytes 1007624 | tf_op jit(solution)/shard_map/ppermute | solution.py:199
  13.8 8.6 %collective-permute-start.6 = (bf16[4,128,256]{2,1,0:T(8,128)(2,1)S(1)}, bf16[4,128,256]{2,1,0:T(8,128)(2,1)S(1)}, u32[]{:S(2)}, u32[]{:S(2)}) collective-permute-start(bf16[4,128,256]{2,1,0:T(8,128)(2,1)S(1)} %pad_maximum_fusion), channel_id=1, source_target_pairs={{0,1},{1,0},{2,3},{3,2},{4,5},{5,4},{6,7},{7,6},{8,9},{9,8},{10,11... | collective-permute-start | bytes 786440 | tf_op jit(solution)/shard_map/ppermute | solution.py:199
  32.5 8.6 %collective-permute-start.10 = (bf16[4,128,256]{2,1,0:T(8,128)(2,1)S(1)}, bf16[4,128,256]{2,1,0:T(8,128)(2,1)S(1)}, u32[]{:S(2)}, u32[]{:S(2)}) collective-permute-start(bf16[4,128,256]{2,1,0:T(8,128)(2,1)S(1)} %get-tuple-element.28), channel_id=1, source_target_pairs={{0,1},{1,0},{2,3},{3,2},{4,5},{5,4},{6,7},{7,6},{8,9},{9,8},{10,11... | collective-permute-start | bytes 786440 | tf_op jit(solution)/shard_map/ppermute | solution.py:199
  34.2 18.8 %collective-permute-start.7 = (bf16[640,128]{1,0:T(8,128)(2,1)S(1)}, bf16[640,128]{1,0:T(8,128)(2,1)S(1)}, u32[]{:S(2)}, u32[]{:S(2)}) collective-permute-start(bf16[640,128]{1,0:T(8,128)(2,1)S(1)} %get-tuple-element.24), channel_id=1, source_target_pairs={{0,8},{8,0},{16,24},{24,16},{1,9},{9,1},{17,25},{25,17},{2,10},{10... | collective-permute-start | bytes 491528 | tf_op jit(solution)/shard_map/ppermute | solution.py:199
  34.2 18.8 %collective-permute-start.8 = (bf16[640,128]{1,0:T(8,128)(2,1)S(1)}, bf16[640,128]{1,0:T(8,128)(2,1)S(1)}, u32[]{:S(2)}, u32[]{:S(2)}) collective-permute-start(bf16[640,128]{1,0:T(8,128)(2,1)S(1)} %get-tuple-element.25), channel_id=1, source_target_pairs={{0,16},{8,24},{16,0},{24,8},{1,17},{9,25},{17,1},{25,9},{2,18},{10... | collective-permute-start | bytes 491528 | tf_op jit(solution)/shard_map/ppermute | solution.py:199
  35.7 17.2 %collective-permute-start.9 = (bf16[640,128]{1,0:T(8,128)(2,1)S(1)}, bf16[640,128]{1,0:T(8,128)(2,1)S(1)}, u32[]{:S(2)}, u32[]{:S(2)}) collective-permute-start(bf16[640,128]{1,0:T(8,128)(2,1)S(1)} %get-tuple-element.26), channel_id=1, source_target_pairs={{0,24},{8,16},{16,8},{24,0},{1,25},{9,17},{17,9},{25,1},{2,26},{10... | collective-permute-start | bytes 491528 | tf_op jit(solution)/shard_map/ppermute | solution.py:199
  41.1 13.4 %collective-permute-start.11 = (bf16[128,256]{1,0:T(8,128)(2,1)S(1)}, bf16[128,256]{1,0:T(8,128)(2,1)S(1)}, u32[]{:S(2)}, u32[]{:S(2)}) collective-permute-start(bf16[128,256]{1,0:T(8,128)(2,1)S(1)} %get-tuple-element.30), channel_id=1, source_target_pairs={{0,2},{1,3},{2,0},{3,1},{4,6},{5,7},{6,4},{7,5},{8,10},{9,11},{10,... | collective-permute-start | bytes 196616 | tf_op jit(solution)/shard_map/ppermute | solution.py:199
  45.1 12.1 %collective-permute-start.12 = (bf16[128,256]{1,0:T(8,128)(2,1)S(1)}, bf16[128,256]{1,0:T(8,128)(2,1)S(1)}, u32[]{:S(2)}, u32[]{:S(2)}) collective-permute-start(bf16[128,256]{1,0:T(8,128)(2,1)S(1)} %get-tuple-element.31), channel_id=1, source_target_pairs={{0,4},{1,5},{2,6},{3,7},{4,0},{5,1},{6,2},{7,3},{8,12},{9,13},{10,... | collective-permute-start | bytes 196616 | tf_op jit(solution)/shard_map/ppermute | solution.py:199
  53.0 6.1 %collective-permute-start.13 = (bf16[128,256]{1,0:T(8,128)(2,1)S(1)}, bf16[128,256]{1,0:T(8,128)(2,1)S(1)}, u32[]{:S(2)}, u32[]{:S(2)}) collective-permute-start(bf16[128,256]{1,0:T(8,128)(2,1)S(1)} %get-tuple-element.32), channel_id=1, source_target_pairs={{0,6},{1,7},{2,4},{3,5},{4,2},{5,3},{6,0},{7,1},{8,14},{9,15},{10,... | collective-permute-start | bytes 196616 | tf_op jit(solution)/shard_map/ppermute | solution.py:199

commit v2 on v1

v2 whole, which is shorter than its diff:
```python
import functools
import math

import jax
import jax.numpy as jnp
from jax import lax
from jax.experimental import pallas as pl
from jax.experimental.pallas import tpu as pltpu
from jax.sharding import PartitionSpec as P

NT_DIMS = (((1,), (1,)), ((), ()))
UNROLLED = 4
EXTRA = 4
VMEM_LIMIT = 32 * 1024 * 1024
PACK_LIMIT = 62 * 1024 * 1024
LOG2E = math.log2(math.e)
SMEM = pl.BlockSpec(memory_space=pltpu.SMEM)
VMEM = pl.BlockSpec(memory_space=pltpu.VMEM)
HBM = pl.BlockSpec(memory_space=pltpu.HBM)


def up16(rows):
    return -(-rows // 16) * 16


def pack_kernel(heads, head, place_ref, queries, grads, saved, cache_keys, cache_values, totals, *refs):
    *messages, block, query_here, grad_here, saved_here, sems = refs
    rows = queries.shape[0]
    width = heads * head
    groups = queries.shape[1] // width
    pairs = [(grads, grad_here), (saved, saved_here), (queries, query_here)]
    pairs += [
        (cache_keys, block.at[:, pl.ds(0, head)]),
        (cache_values, block.at[:, pl.ds(head, head)]),
    ]
    loads = [
        pltpu.make_async_copy(source, target, sems.at[i]) for i, (source, target) in enumerate(pairs)
    ]
    for load in loads:
        load.start()
    loads[0].wait()
    loads[1].wait()
    lanes = lax.broadcasted_iota(jnp.int32, (rows, 128), 1)
    dots = jnp.zeros((rows, 128), jnp.float32)
    for h in range(groups * heads):
        cols = slice(h * head, (h + 1) * head)
        product = grad_here[:, cols].astype(jnp.float32) * saved_here[:, cols].astype(jnp.float32)
        dots = jnp.where(lanes == h, jnp.sum(product, axis=1, keepdims=True), dots)
    dots = jnp.transpose(dots)
    high = dots.astype(jnp.bfloat16).astype(jnp.float32)
    rest = dots - high
    middle = rest.astype(jnp.bfloat16).astype(jnp.float32)
    low = rest - middle
    parts = (totals[...].astype(jnp.float32), high, middle, low)
    for load in loads[2:]:
        load.wait()
    for k, message in enumerate(messages):
        place = place_ref[0] ^ k
        start = pl.multiple_of(place * width, 128)
        for h in range(heads):
            at = pl.multiple_of(start + h * head, 128)
            message[h * rows : (h + 1) * rows, :] = query_here[:, pl.ds(at, head)]
            message[(heads + h) * rows : (heads + h + 1) * rows, :] = grad_here[:, pl.ds(at, head)]
        lines = message.shape[0] - 2 * heads * rows
        extra = []
        for part in parts:
            chosen = part[0:heads, :]
            for group in range(1, groups):
                chosen = jnp.where(
                    place == group, part[group * heads : (group + 1) * heads, :], chosen
                )
            extra.append(chosen)
        extra.append(jnp.zeros((lines - EXTRA * heads, 128), jnp.float32))
        message[2 * heads * rows :, :] = jnp.concatenate(extra, axis=0).astype(jnp.bfloat16)


def attend_kernel(layers, heads, head, outer, first, last, inv_root, info, *refs):
    messages = refs[:layers]
    own_blocks = refs[layers : layers + outer]
    other_blocks = refs[layers + outer]
    refs = refs[layers + outer + 1 :]
    if not first:
        earlier, refs = refs[0], refs[1:]
    query_outs, refs = refs[:layers], refs[layers:]
    if last:
        mine, theirs = refs[:2]
        refs = refs[2:]
    else:
        partial, refs = refs[0], refs[1:]
    keys, values, query_turned, grad_turned, totals, dots, weights_all, score_all, query_acc = refs
    rows = own_blocks[0].shape[0]
    pair = 2 * rows
    z, x = info[0], info[1]
    per_layer = heads * rows
    every = layers * per_layer
    for k in range(outer):

        @pl.when(k <= z)
        def _():
            at = pl.multiple_of((z - k) * pair, pair)
            keys[pl.ds(at + x * rows, rows), :] = own_blocks[k][:, :head]
            values[pl.ds(at + x * rows, rows), :] = own_blocks[k][:, head:]
            keys[pl.ds(at + (1 - x) * rows, rows), :] = other_blocks[k, :, :head]
            values[pl.ds(at + (1 - x) * rows, rows), :] = other_blocks[k, :, head:]

    for layer in range(layers):
        there = slice(layer * per_layer, (layer + 1) * per_layer)
        query_turned[:, there] = jnp.transpose(messages[layer][:per_layer, :])
        grad_turned[:, there] = jnp.transpose(messages[layer][per_layer : 2 * per_layer, :])
        extra = messages[layer][2 * per_layer :, :].astype(jnp.float32)
        high, middle, low = (extra[i * heads : (i + 1) * heads] for i in (1, 2, 3))
        spare = jnp.zeros((128 - 2 * heads, 128), jnp.float32)
        columns = jnp.transpose(
            jnp.concatenate([extra[:heads] * LOG2E, high + (middle + low), spare], axis=0)
        )
        for h in range(heads):
            at = layer * per_layer + h * rows
            totals[at : at + rows, :] = jnp.broadcast_to(columns[:, h : h + 1], (rows, 128))
            dots[at : at + rows, :] = jnp.broadcast_to(
                columns[:, heads + h : heads + h + 1], (rows, 128)
            )
    chunks = [
        (layer, h, min(2, heads - h)) for layer in range(layers) for h in range(0, heads, 2)
    ]

    def tiles(at, spot, masked):
        key_tile = keys[pl.ds(at, pair), :]
        value_tile = values[pl.ds(at, pair), :]
        for layer, h, count in chunks:
            tall = count * rows
            top = layer * per_layer + h * rows
            here = slice(top, top + tall)
            query = messages[layer][h * rows : h * rows + tall, :]
            grad = messages[layer][per_layer + h * rows : per_layer + h * rows + tall, :]
            total = jnp.concatenate([totals[here, :]] * (pair // 128), axis=1)
            dot = jnp.concatenate([dots[here, :]] * (pair // 128), axis=1)
            scores = lax.dot_general(query, key_tile, NT_DIMS, preferred_element_type=jnp.float32)
            weights = jnp.exp2(scores * (inv_root * LOG2E) - total)
            if masked:
                key_pos = lax.broadcasted_iota(jnp.int32, (1, pair), 1)
                query_pos = lax.broadcasted_iota(jnp.int32, (tall, 1), 0) % rows + x * rows
                weights = jnp.where(key_pos <= query_pos, weights, 0.0)
            weight_grads = lax.dot_general(
                grad, value_tile, NT_DIMS, preferred_element_type=jnp.float32
            )
            score_grads = weights * (weight_grads - dot) * inv_root
            weights_all[here, spot : spot + pair] = weights.astype(jnp.bfloat16)
            score_all[here, spot : spot + pair] = score_grads.astype(jnp.bfloat16)

    def leave(j, key_sum, value_sum):
        if not first:
            key_sum += earlier[j, :, :pair]
            value_sum += earlier[j, :, pair:]
        if not last:
            partial[j, :, :pair] = key_sum
            partial[j, :, pair:] = value_sum
            return
        both = (jnp.transpose(key_sum), jnp.transpose(value_sum))
        for half, out in ((0, mine), (1, theirs)):
            for part, total in enumerate(both):
                chosen = jnp.where(x == half, total[:rows], total[rows:]).astype(jnp.bfloat16)
                out[z - j, :, part * head : (part + 1) * head] = chosen

    def sweep(j, masked):
        at = pl.multiple_of(j * pair, pair)
        tiles(at, 0, masked)
        here = slice(0, pair)
        query_acc[...] += jnp.dot(
            score_all[:, here], keys[pl.ds(at, pair), :], preferred_element_type=jnp.float32
        )
        leave(
            j,
            jnp.dot(query_turned[...], score_all[:, here], preferred_element_type=jnp.float32),
            jnp.dot(grad_turned[...], weights_all[:, here], preferred_element_type=jnp.float32),
        )

    def full(j, carry):
        sweep(j, False)
        return carry

    def stepwise():
        query_acc[...] = jnp.zeros_like(query_acc)
        lax.fori_loop(0, z, full, 0)
        sweep(z, True)
        for layer in range(layers):
            query_outs[layer][...] = query_acc[
                layer * per_layer : (layer + 1) * per_layer, :
            ].astype(jnp.bfloat16)

    def whole():
        for j in range(outer):
            tiles(j * pair, j * pair, j == outer - 1)
        key_sum = jnp.dot(query_turned[...], score_all[...], preferred_element_type=jnp.float32)
        value_sum = jnp.dot(grad_turned[...], weights_all[...], preferred_element_type=jnp.float32)
        for j in range(outer):
            here = slice(j * pair, (j + 1) * pair)
            leave(j, key_sum[:, here], value_sum[:, here])
        for layer in range(layers):
            there = slice(layer * per_layer, (layer + 1) * per_layer)
            query_outs[layer][...] = jnp.dot(
                score_all[there, :], keys[...], preferred_element_type=jnp.float32
            ).astype(jnp.bfloat16)

    if outer <= UNROLLED:
        pl.when(z == outer - 1)(whole)
        pl.when(z < outer - 1)(stepwise)
    else:
        stepwise()
    if last:

        def blank(k, carry):
            mine[k] = jnp.zeros(mine.shape[1:], jnp.bfloat16)
            theirs[k] = jnp.zeros(theirs.shape[1:], jnp.bfloat16)
            return carry

        lax.fori_loop(z + 1, outer, blank, 0)


def add_kernel(mine, theirs, *outs):
    for k, out in enumerate(outs):
        out[...] = (mine[k].astype(jnp.float32) + theirs[k].astype(jnp.float32)).astype(
            jnp.bfloat16
        )


def place_kernel(heads, head, place_ref, *refs):
    messages, out = refs[:-1], refs[-1]
    rows = out.shape[0]
    for k, message in enumerate(messages):
        start = pl.multiple_of((place_ref[0] ^ k) * heads * head, 128)
        for h in range(heads):
            at = pl.multiple_of(start + h * head, 128)
            out[:, pl.ds(at, head)] = message[h * rows : (h + 1) * rows, :]


def total_kernel(*refs):
    blocks, key_out, value_out = refs[:-2], refs[-2], refs[-1]
    total = blocks[0][...].astype(jnp.float32)
    for block in blocks[1:]:
        total = total + block[...].astype(jnp.float32)
    head = key_out.shape[1]
    key_out[...] = total[:, :head].astype(jnp.bfloat16)
    value_out[...] = total[:, head:].astype(jnp.bfloat16)


def call(kernel, outs, in_specs, scratch=(), kinds=None, limit=VMEM_LIMIT):
    kinds = kinds or [jnp.bfloat16] * len(outs)
    return pl.pallas_call(
        kernel,
        out_shape=[jax.ShapeDtypeStruct(shape, kind) for shape, kind in zip(outs, kinds)],
        in_specs=in_specs,
        out_specs=[VMEM] * len(outs),
        scratch_shapes=list(scratch),
        compiler_params=pltpu.CompilerParams(vmem_limit_bytes=limit),
    )


def swap(array, axis, bits):
    size = lax.axis_size(axis)
    return lax.ppermute(array, axis, [(i, i ^ bits) for i in range(size)])


def move(array, step):
    size = lax.axis_size("seq")
    return lax.ppermute(
        array, "seq", [(i, i + step) for i in range(size) if 0 <= i + step < size]
    )


def local(queries, cache_keys, cache_values, saved_out, out_grads, log_sums):
    sections = lax.axis_size("section")
    seq = lax.axis_size("seq")
    outer = seq // 2
    section_at = lax.axis_index("section").astype(jnp.int32).reshape(1)
    seq_at = lax.axis_index("seq").astype(jnp.int32)
    rows, head = cache_keys.shape
    heads = log_sums.shape[2] // sections
    inv_root = 1.0 / math.sqrt(head)
    info = jnp.stack([seq_at // 2, seq_at % 2])
    lines = 2 * heads * rows + up16(EXTRA * heads)

    *sent, own = call(
        functools.partial(pack_kernel, heads, head),
        [(lines, 128)] * sections + [(rows, 2 * head)],
        [SMEM] + [HBM] * 5 + [VMEM],
        [pltpu.VMEM(queries.shape[1:], jnp.bfloat16)] * 3 + [pltpu.SemaphoreType.DMA((5,))],
        limit=PACK_LIMIT,
    )(
        section_at,
        queries[0],
        out_grads[0],
        saved_out[0],
        cache_keys,
        cache_values,
        jnp.transpose(log_sums[0]),
    )
    messages = [sent[0]] + [swap(sent[k], "section", k) for k in range(1, sections)]
    own_blocks = [own] + [move(own, 2 * k) for k in range(1, outer)]
    other_blocks = swap(jnp.stack(own_blocks), "seq", 1)

    def attend(which, first, last, earlier=()):
        count = len(which)
        outs = [(heads * rows, head)] * count
        kinds = [jnp.bfloat16] * count
        if last:
            outs, kinds = outs + [(outer, rows, 2 * head)] * 2, kinds + [jnp.bfloat16] * 2
        else:
            outs, kinds = outs + [(outer, head, 4 * rows)], kinds + [jnp.float32]
        every = count * heads * rows
        across = 2 * rows * (outer if outer <= UNROLLED else 1)
        return call(
            functools.partial(attend_kernel, count, heads, head, outer, first, last, inv_root),
            outs,
            [SMEM] + [VMEM] * (count + outer + 1 + len(earlier)),
            [pltpu.VMEM((seq * rows, head), jnp.bfloat16)] * 2
            + [pltpu.VMEM((head, every), jnp.bfloat16)] * 2
            + [pltpu.VMEM((every, 128), jnp.float32)] * 2
            + [pltpu.VMEM((every, across), jnp.bfloat16)] * 2
            + [pltpu.VMEM((every, head), jnp.float32)],
            kinds,
        )(info, *[messages[k] for k in which], *own_blocks, other_blocks, *earlier)

    late = sections - 1
    early = tuple(k for k in range(sections) if k != late)
    *grads, partial = attend(early, True, False)
    back = dict(zip(early, grads))
    back[late], mine, theirs = attend((late,), False, True, (partial,))

    arrived = swap(theirs, "seq", 1)
    summed = call(add_kernel, [(rows, 2 * head)] * outer, [VMEM] * 2)(mine, arrived)
    blocks = [summed[0]] + [move(summed[k], -2 * k) for k in range(1, outer)]
    key_grads, value_grads = call(total_kernel, [(rows, head)] * 2, [VMEM] * outer)(*blocks)

    back = [back[0]] + [swap(back[k], "section", k) for k in range(1, sections)]
    (query_grads,) = call(
        functools.partial(place_kernel, heads, head),
        [queries.shape[1:]],
        [SMEM] + [VMEM] * sections,
    )(section_at, *back)
    return (query_grads[None], key_grads, value_grads)


def solution(mesh):
    placed = (
        P("section", "seq", None),
        P("seq", "section"),
        P("seq", "section"),
        P("section", "seq", None),
        P("section", "seq", None),
        P("section", "seq", None),
    )
    return jax.shard_map(
        local,
        mesh=mesh,
        in_specs=placed,
        out_specs=(P("section", "seq", None), P("seq", "section"), P("seq", "section")),
        check_vma=False,
    )
```

time: 60 us -> 55.9 us (0.932)
  local copies, waits for them, and re-layouts: 4.18 us -> 0.01 us
  Pallas kernels: 6.99 us -> 10.3 us
  starting transfers between devices: 24.8 us -> 21.6 us
  waiting for transfers between devices: 22.9 us -> 21.8 us
  other arithmetic: 0.11 us -> 1.02 us
    ppermute x14 -> x8, starting transfers between devices: 24.8 us -> 6.91 us  [swap(): return lax.ppermute(array, axis, [(i, i ^ bits) for i in range(size)])]
    ppermute x0 -> x6, starting transfers between devices: none -> 14.7 us  [move(): lax.ppermute(array, 'seq', [(i, i + step) for i in range(size) if 0 <= i...]
    ppermute x14 -> x8, waiting for transfers between devices: 22.9 us -> 14.7 us  [swap(): return lax.ppermute(array, axis, [(i, i ^ bits) for i in range(size)])]
    ppermute x0 -> x6, waiting for transfers between devices: none -> 7.11 us  [move(): lax.ppermute(array, 'seq', [(i, i + step) for i in range(size) if 0 <= i...]
    unnamed x12 -> x4, local copies, waits for them, and re-layouts: 4.17 us -> 0.01 us
    pallas_call x1, Pallas kernels: 1.17 us -> 3.82 us  [local(): call(functools.partial(pack_kernel, heads, head), [(lines, 128)] * sectio...]
    pallas_call x1 -> x2, Pallas kernels: 3.6 us -> 4.78 us  [attend(): call(functools.partial(attend_kernel, count, heads, head, outer, first, l...]
    another operation x1, other arithmetic: 0.04 us -> 0.95 us  [local(): other_blocks = swap(jnp.stack(own_blocks), 'seq', 1)]
  transfers between devices with their start and end apart: 14 -> 14, of which waited for: 6 -> 7; matrix products, arithmetic and copies ran while one was open for 0% -> 2% of each run, Pallas kernels for 5% -> 7%
where the time goes in v2:
time: 55.9 us; the launch traced here: 55.6 us
  waiting for transfers between devices  21.8 us (39%)
  starting transfers between devices  21.6 us (39%)
  Pallas kernels  10.3 us (18%)
  other arithmetic  1.02 us (2%)
  between operations  0.78 us (1%)
    ppermute x6, starting transfers between devices, move(): lax.ppermute(array, 'seq', [(i, i + step) for i in range(size) if 0 <= i...  14.7 us
    ppermute x8, waiting for transfers between devices, swap(): return lax.ppermute(array, axis, [(i, i ^ bits) for i in range(size)])  14.7 us
    ppermute x6, waiting for transfers between devices, move(): lax.ppermute(array, 'seq', [(i, i + step) for i in range(size) if 0 <= i...  7.11 us
    ppermute x8, starting transfers between devices, swap(): return lax.ppermute(array, axis, [(i, i ^ bits) for i in range(size)])  6.91 us
    pallas_call x2, Pallas kernels, attend(): call(functools.partial(attend_kernel, count, heads, head, outer, first, l...  4.78 us
    pallas_call x1, Pallas kernels, local(): call(functools.partial(pack_kernel, heads, head), [(lines, 128)] * sectio...  3.82 us
  transfers between devices with their start and end apart: 14, of which 7 were waited for; matrix products, arithmetic and copies ran while one was open for 2% of the time, Pallas kernels for 7%

profile of v2, /device:TPU:0, one launch (start us, length us, event | category | flops | bytes accessed | tf_op | source)
XLA Modules:
  0.0 55.6 jit_solution(13598762107858049482)
XLA Ops:
  0.6 3.8 %shard_map.85 = (bf16[1312,128]{1,0:T(8,128)(2,1)}, bf16[1312,128]{1,0:T(8,128)(2,1)}, bf16[1312,128]{1,0:T(8,128)(2,1)}, bf16[1312,128]{1,0:T(8,128)(2,1)}, bf16[128,256]{1,0:T(8,128)(2,1)}) custom-call(s32[1]{0:T(128)} %bitcast.place_ref, bf16[128,2560]{1,0:T(8,128)(2,1)} %bitcast.19, bf16[128,2560]{1,0:T(8,128)(2,1)} %bitcast.20, ...), custom_call_target="tpu_custom_call" | custom-call | tf_op jit(solution)/shard_map/pallas_call | solution.py:282
  4.5 0.0 copy-start.1
  4.5 7.1 %collective-permute-start.4 = (bf16[128,256]{1,0:T(8,128)(2,1)}, bf16[128,256]{1,0:T(8,128)(2,1)S(1)}, u32[]{:S(2)}, u32[]{:S(2)}) collective-permute-start(bf16[128,256]{1,0:T(8,128)(2,1)} %get-tuple-element.24.refs_3_.refs_1_), channel_id=1, source_target_pairs={{0,6},{1,7},{8,14},{9,15},{16,22},{17,23},{24,30},{25,31}} | collective-permute-start | bytes 196616 | tf_op jit(solution)/shard_map/ppermute | solution.py:265
  11.6 1.3 %collective-permute-start.3 = (bf16[128,256]{1,0:T(8,128)(2,1)}, bf16[128,256]{1,0:T(8,128)(2,1)S(1)}, u32[]{:S(2)}, u32[]{:S(2)}) collective-permute-start(bf16[128,256]{1,0:T(8,128)(2,1)} %get-tuple-element.24.refs_3_.refs_1_), channel_id=1, source_target_pairs={{0,4},{1,5},{2,6},{3,7},{8,12},{9,13},{10,14},{11,15},{16,20},{17,... | collective-permute-start | bytes 196616 | tf_op jit(solution)/shard_map/ppermute | solution.py:265
  12.9 2.5 %collective-permute-start.2 = (bf16[128,256]{1,0:T(8,128)(2,1)}, bf16[128,256]{1,0:T(8,128)(2,1)S(1)}, u32[]{:S(2)}, u32[]{:S(2)}) collective-permute-start(bf16[128,256]{1,0:T(8,128)(2,1)} %get-tuple-element.24.refs_3_.refs_1_), channel_id=1, source_target_pairs={{0,2},{1,3},{2,4},{3,5},{4,6},{5,7},{8,10},{9,11},{10,12},{11,13},... | collective-permute-start | bytes 196616 | tf_op jit(solution)/shard_map/ppermute | solution.py:265
  15.3 0.1 collective-permute-start
  15.4 1.6 %collective-permute-start.1 = (bf16[1312,128]{1,0:T(8,128)(2,1)}, bf16[1312,128]{1,0:T(8,128)(2,1)S(1)}, u32[]{:S(2)}, u32[]{:S(2)}) collective-permute-start(bf16[1312,128]{1,0:T(8,128)(2,1)} %get-tuple-element.23), channel_id=1, source_target_pairs={{0,16},{8,24},{16,0},{24,8},{1,17},{9,25},{17,1},{25,9},{2,18},{10... | collective-permute-start | bytes 1007624 | tf_op jit(solution)/shard_map/ppermute | solution.py:260
  17.0 0.0 collective-permute-done.4.refs_6_.refs_4_
  17.0 0.3 collective-permute-start.8
  17.3 0.0 collective-permute-done.3.refs_5_.refs_3_
  17.3 0.3 collective-permute-done.2.refs_4_.refs_2_
  17.5 0.0 copy-start
  17.6 0.9 %pad_maximum_fusion = bf16[4,128,256]{2,1,0:T(8,128)(2,1)S(1)} fusion(bf16[1,128,256]{2,1,0:T(8,128)(2,1)S(1)} %bitcast.15, bf16[1,128,256]{2,1,0:T(8,128)(2,1)S(1)} %bitcast.16, bf16[1,128,256]{2,1,0:T(8,128)(2,1)S(1)} %bitcast.17, bf16[1,128,256]{2,1,0:T(8,128)(2,1)} %bitcast.14), kind=kLoop, calls=%fused_computation | loop fusion | flops 393216 | bytes 524288 | tf_op jit(solution)/shard_map/stack | solution.py:299
  18.5 1.6 %collective-permute-start.5 = (bf16[4,128,256]{2,1,0:T(8,128)(2,1)S(1)}, bf16[4,128,256]{2,1,0:T(8,128)(2,1)S(1)}, u32[]{:S(2)}, u32[]{:S(2)}) collective-permute-start(bf16[4,128,256]{2,1,0:T(8,128)(2,1)S(1)} %pad_maximum_fusion), channel_id=1, source_target_pairs={{0,1},{1,0},{2,3},{3,2},{4,5},{5,4},{6,7},{7,6},{8,9},{9,8},{10,11... | collective-permute-start | bytes 786440 | tf_op jit(solution)/shard_map/ppermute | solution.py:260
  20.1 0.1 pad_add_fusion.info
  20.1 6.7 %collective-permute-done.5.refs_7_.refs_5_ = bf16[4,128,256]{2,1,0:T(8,128)(2,1)S(1)} collective-permute-done((bf16[4,128,256]{2,1,0:T(8,128)(2,1)S(1)}, bf16[4,128,256]{2,1,0:T(8,128)(2,1)S(1)}, u32[]{:S(2)}, u32[]{:S(2)}) %collective-permute-start.5) | collective-permute-done | bytes 262176 | tf_op jit(solution)/shard_map/ppermute | solution.py:260
  26.9 0.0 collective-permute-done.refs_1_
  26.9 0.0 collective-permute-done.1.refs_2_
  26.9 0.0 copy-done.1
  26.9 0.0 copy-done
  26.9 2.9 %shard_map.86 = (bf16[640,128]{1,0:T(8,128)(2,1)S(1)}, bf16[640,128]{1,0:T(8,128)(2,1)S(1)}, bf16[640,128]{1,0:T(8,128)(2,1)S(1)}, f32[4,128,512]{2,1,0:T(8,128)S(1)}) custom-call(s32[2]{0:T(128)S(1)} %pad_add_fusion.info, bf16[1312,128]{1,0:T(8,128)(2,1)S(1)} %copy-done.1, bf16[1312,128]{1,0:T(8,128)(2,1)S(1)} %collective-permute-done.refs_1_, ...), custom_call_target="tpu_custom_call" | custom-call | tf_op jit(solution)/shard_map/pallas_call | solution.py:311
  29.8 2.8 %collective-permute-done.8.refs_0_ = bf16[1312,128]{1,0:T(8,128)(2,1)S(1)} collective-permute-done((bf16[1312,128]{1,0:T(8,128)(2,1)}, bf16[1312,128]{1,0:T(8,128)(2,1)S(1)}, u32[]{:S(2)}, u32[]{:S(2)}) %collective-permute-start.8) | collective-permute-done | bytes 335904 | tf_op jit(solution)/shard_map/ppermute | solution.py:260
  32.7 1.8 %shard_map.87 = (bf16[640,128]{1,0:T(8,128)(2,1)S(1)}, bf16[4,128,256]{2,1,0:T(8,128)(2,1)S(1)}, bf16[4,128,256]{2,1,0:T(8,128)(2,1)S(1)}) custom-call(s32[2]{0:T(128)S(1)} %pad_add_fusion.info, bf16[1312,128]{1,0:T(8,128)(2,1)S(1)} %collective-permute-done.8.refs_0_, bf16[128,256]{1,0:T(8,128)(2,1)S(1)} %copy-done, ...), custom_call_target="tpu_custom_call" | custom-call | tf_op jit(solution)/shard_map/pallas_call | solution.py:311
  34.5 1.6 %collective-permute-start.10 = (bf16[4,128,256]{2,1,0:T(8,128)(2,1)S(1)}, bf16[4,128,256]{2,1,0:T(8,128)(2,1)S(1)}, u32[]{:S(2)}, u32[]{:S(2)}) collective-permute-start(bf16[4,128,256]{2,1,0:T(8,128)(2,1)S(1)} %get-tuple-element.32), channel_id=1, source_target_pairs={{0,1},{1,0},{2,3},{3,2},{4,5},{5,4},{6,7},{7,6},{8,9},{9,8},{10,11... | collective-permute-start | bytes 786440 | tf_op jit(solution)/shard_map/ppermute | solution.py:260
  36.1 0.0 collective-permute-start.6
  36.1 1.5 %collective-permute-start.7 = (bf16[640,128]{1,0:T(8,128)(2,1)S(1)}, bf16[640,128]{1,0:T(8,128)(2,1)S(1)}, u32[]{:S(2)}, u32[]{:S(2)}) collective-permute-start(bf16[640,128]{1,0:T(8,128)(2,1)S(1)} %get-tuple-element.27), channel_id=1, source_target_pairs={{0,16},{8,24},{16,0},{24,8},{1,17},{9,25},{17,1},{25,9},{2,18},{10... | collective-permute-start | bytes 491528 | tf_op jit(solution)/shard_map/ppermute | solution.py:260
  37.6 0.3 collective-permute-start.9
  37.9 5.1 %collective-permute-done.10.theirs = bf16[4,128,256]{2,1,0:T(8,128)(2,1)S(1)} collective-permute-done((bf16[4,128,256]{2,1,0:T(8,128)(2,1)S(1)}, bf16[4,128,256]{2,1,0:T(8,128)(2,1)S(1)}, u32[]{:S(2)}, u32[]{:S(2)}) %collective-permute-start.10) | collective-permute-done | bytes 262176 | tf_op jit(solution)/shard_map/ppermute | solution.py:260
  43.1 0.1 shard_map.89
  43.1 1.3 %collective-permute-start.11 = (bf16[128,256]{1,0:T(8,128)(2,1)S(1)}, bf16[128,256]{1,0:T(8,128)(2,1)S(1)}, u32[]{:S(2)}, u32[]{:S(2)}) collective-permute-start(bf16[128,256]{1,0:T(8,128)(2,1)S(1)} %get-tuple-element.34), channel_id=1, source_target_pairs={{2,0},{3,1},{4,2},{5,3},{6,4},{7,5},{10,8},{11,9},{12,10},{13,11},... | collective-permute-start | bytes 196616 | tf_op jit(solution)/shard_map/ppermute | solution.py:265
  44.4 1.3 %collective-permute-start.12 = (bf16[128,256]{1,0:T(8,128)(2,1)S(1)}, bf16[128,256]{1,0:T(8,128)(2,1)S(1)}, u32[]{:S(2)}, u32[]{:S(2)}) collective-permute-start(bf16[128,256]{1,0:T(8,128)(2,1)S(1)} %get-tuple-element.35), channel_id=1, source_target_pairs={{4,0},{5,1},{6,2},{7,3},{12,8},{13,9},{14,10},{15,11},{20,16},{21,... | collective-permute-start | bytes 196616 | tf_op jit(solution)/shard_map/ppermute | solution.py:265
  45.7 0.0 collective-permute-done.6.refs_1_
  45.8 1.3 %collective-permute-start.13 = (bf16[128,256]{1,0:T(8,128)(2,1)S(1)}, bf16[128,256]{1,0:T(8,128)(2,1)S(1)}, u32[]{:S(2)}, u32[]{:S(2)}) collective-permute-start(bf16[128,256]{1,0:T(8,128)(2,1)S(1)} %get-tuple-element.36), channel_id=1, source_target_pairs={{6,0},{7,1},{14,8},{15,9},{22,16},{23,17},{30,24},{31,25}} | collective-permute-start | bytes 196616 | tf_op jit(solution)/shard_map/ppermute | solution.py:265
  47.1 0.0 collective-permute-done.7.refs_2_
  47.1 0.0 collective-permute-done.9.refs_3_
  47.1 1.0 %shard_map.88 = bf16[128,2560]{1,0:T(8,128)(2,1)} custom-call(s32[1]{0:T(128)} %bitcast.place_ref, bf16[640,128]{1,0:T(8,128)(2,1)S(1)} %get-tuple-element.25.refs_0_, bf16[640,128]{1,0:T(8,128)(2,1)S(1)} %collective-permute-done.6.refs_1_, bf16[640,128]{1,0:T(8,128)(2,1)S(1)} %collective-permute-done.7.refs_2_, ...), custom_call_target="tpu_custom_call" | custom-call | tf_op jit(solution)/shard_map/pallas_call | solution.py:335
  48.0 1.3 %collective-permute-done.11.refs_1_ = bf16[128,256]{1,0:T(8,128)(2,1)S(1)} collective-permute-done((bf16[128,256]{1,0:T(8,128)(2,1)S(1)}, bf16[128,256]{1,0:T(8,128)(2,1)S(1)}, u32[]{:S(2)}, u32[]{:S(2)}) %collective-permute-start.11) | collective-permute-done | bytes 65568 | tf_op jit(solution)/shard_map/ppermute | solution.py:265
  49.3 2.9 %collective-permute-done.12.refs_2_ = bf16[128,256]{1,0:T(8,128)(2,1)S(1)} collective-permute-done((bf16[128,256]{1,0:T(8,128)(2,1)S(1)}, bf16[128,256]{1,0:T(8,128)(2,1)S(1)}, u32[]{:S(2)}, u32[]{:S(2)}) %collective-permute-start.12) | collective-permute-done | bytes 65568 | tf_op jit(solution)/shard_map/ppermute | solution.py:265
  52.2 2.7 %collective-permute-done.13.refs_3_ = bf16[128,256]{1,0:T(8,128)(2,1)S(1)} collective-permute-done((bf16[128,256]{1,0:T(8,128)(2,1)S(1)}, bf16[128,256]{1,0:T(8,128)(2,1)S(1)}, u32[]{:S(2)}, u32[]{:S(2)}) %collective-permute-start.13) | collective-permute-done | bytes 65568 | tf_op jit(solution)/shard_map/ppermute | solution.py:265
  54.9 0.7 %shard_map.90 = (bf16[128,128]{1,0:T(8,128)(2,1)}, bf16[128,128]{1,0:T(8,128)(2,1)}) custom-call(bf16[128,256]{1,0:T(8,128)(2,1)S(1)} %get-tuple-element.33.refs_0_, bf16[128,256]{1,0:T(8,128)(2,1)S(1)} %collective-permute-done.11.refs_1_, bf16[128,256]{1,0:T(8,128)(2,1)S(1)} %collective-permute-done.12.refs_2_, ...), custom_call_target="tpu_custom_call" | custom-call | tf_op jit(solution)/shard_map/pallas_call | solution.py:332
Async XLA Ops:
  4.5 22.4 %copy-start.1 = (bf16[1312,128]{1,0:T(8,128)(2,1)S(1)}, bf16[1312,128]{1,0:T(8,128)(2,1)}, u32[]{:S(2)}) copy-start(bf16[1312,128]{1,0:T(8,128)(2,1)} %get-tuple-element.21.refs_0_) | copy-start | bytes 1007620
  4.5 12.5 %collective-permute-start.4 = (bf16[128,256]{1,0:T(8,128)(2,1)}, bf16[128,256]{1,0:T(8,128)(2,1)S(1)}, u32[]{:S(2)}, u32[]{:S(2)}) collective-permute-start(bf16[128,256]{1,0:T(8,128)(2,1)} %get-tuple-element.24.refs_3_.refs_1_), channel_id=1, source_target_pairs={{0,6},{1,7},{8,14},{9,15},{16,22},{17,23},{24,30},{25,31}} | collective-permute-start | bytes 196616 | tf_op jit(solution)/shard_map/ppermute | solution.py:265
  11.6 5.7 %collective-permute-start.3 = (bf16[128,256]{1,0:T(8,128)(2,1)}, bf16[128,256]{1,0:T(8,128)(2,1)S(1)}, u32[]{:S(2)}, u32[]{:S(2)}) collective-permute-start(bf16[128,256]{1,0:T(8,128)(2,1)} %get-tuple-element.24.refs_3_.refs_1_), channel_id=1, source_target_pairs={{0,4},{1,5},{2,6},{3,7},{8,12},{9,13},{10,14},{11,15},{16,20},{17,... | collective-permute-start | bytes 196616 | tf_op jit(solution)/shard_map/ppermute | solution.py:265
  12.9 4.7 %collective-permute-start.2 = (bf16[128,256]{1,0:T(8,128)(2,1)}, bf16[128,256]{1,0:T(8,128)(2,1)S(1)}, u32[]{:S(2)}, u32[]{:S(2)}) collective-permute-start(bf16[128,256]{1,0:T(8,128)(2,1)} %get-tuple-element.24.refs_3_.refs_1_), channel_id=1, source_target_pairs={{0,2},{1,3},{2,4},{3,5},{4,6},{5,7},{8,10},{9,11},{10,12},{11,13},... | collective-permute-start | bytes 196616 | tf_op jit(solution)/shard_map/ppermute | solution.py:265
  15.3 11.5 %collective-permute-start = (bf16[1312,128]{1,0:T(8,128)(2,1)}, bf16[1312,128]{1,0:T(8,128)(2,1)S(1)}, u32[]{:S(2)}, u32[]{:S(2)}) collective-permute-start(bf16[1312,128]{1,0:T(8,128)(2,1)} %get-tuple-element.22), channel_id=1, source_target_pairs={{0,8},{8,0},{16,24},{24,16},{1,9},{9,1},{17,25},{25,17},{2,10},{10... | collective-permute-start | bytes 1007624 | tf_op jit(solution)/shard_map/ppermute | solution.py:260
  15.4 11.5 %collective-permute-start.1 = (bf16[1312,128]{1,0:T(8,128)(2,1)}, bf16[1312,128]{1,0:T(8,128)(2,1)S(1)}, u32[]{:S(2)}, u32[]{:S(2)}) collective-permute-start(bf16[1312,128]{1,0:T(8,128)(2,1)} %get-tuple-element.23), channel_id=1, source_target_pairs={{0,16},{8,24},{16,0},{24,8},{1,17},{9,25},{17,1},{25,9},{2,18},{10... | collective-permute-start | bytes 1007624 | tf_op jit(solution)/shard_map/ppermute | solution.py:260
  17.0 15.7 %collective-permute-start.8 = (bf16[1312,128]{1,0:T(8,128)(2,1)}, bf16[1312,128]{1,0:T(8,128)(2,1)S(1)}, u32[]{:S(2)}, u32[]{:S(2)}) collective-permute-start(bf16[1312,128]{1,0:T(8,128)(2,1)} %get-tuple-element.28), channel_id=1, source_target_pairs={{0,24},{8,16},{16,8},{24,0},{1,25},{9,17},{17,9},{25,1},{2,26},{10... | collective-permute-start | bytes 1007624 | tf_op jit(solution)/shard_map/ppermute | solution.py:260
  17.5 9.3 %copy-start = (bf16[128,256]{1,0:T(8,128)(2,1)S(1)}, bf16[128,256]{1,0:T(8,128)(2,1)}, u32[]{:S(2)}) copy-start(bf16[128,256]{1,0:T(8,128)(2,1)} %get-tuple-element.24.refs_3_.refs_1_) | copy-start | bytes 196612
  18.5 8.4 %collective-permute-start.5 = (bf16[4,128,256]{2,1,0:T(8,128)(2,1)S(1)}, bf16[4,128,256]{2,1,0:T(8,128)(2,1)S(1)}, u32[]{:S(2)}, u32[]{:S(2)}) collective-permute-start(bf16[4,128,256]{2,1,0:T(8,128)(2,1)S(1)} %pad_maximum_fusion), channel_id=1, source_target_pairs={{0,1},{1,0},{2,3},{3,2},{4,5},{5,4},{6,7},{7,6},{8,9},{9,8},{10,11... | collective-permute-start | bytes 786440 | tf_op jit(solution)/shard_map/ppermute | solution.py:260
  34.5 8.6 %collective-permute-start.10 = (bf16[4,128,256]{2,1,0:T(8,128)(2,1)S(1)}, bf16[4,128,256]{2,1,0:T(8,128)(2,1)S(1)}, u32[]{:S(2)}, u32[]{:S(2)}) collective-permute-start(bf16[4,128,256]{2,1,0:T(8,128)(2,1)S(1)} %get-tuple-element.32), channel_id=1, source_target_pairs={{0,1},{1,0},{2,3},{3,2},{4,5},{5,4},{6,7},{7,6},{8,9},{9,8},{10,11... | collective-permute-start | bytes 786440 | tf_op jit(solution)/shard_map/ppermute | solution.py:260
  36.1 9.7 %collective-permute-start.6 = (bf16[640,128]{1,0:T(8,128)(2,1)S(1)}, bf16[640,128]{1,0:T(8,128)(2,1)S(1)}, u32[]{:S(2)}, u32[]{:S(2)}) collective-permute-start(bf16[640,128]{1,0:T(8,128)(2,1)S(1)} %get-tuple-element.26), channel_id=1, source_target_pairs={{0,8},{8,0},{16,24},{24,16},{1,9},{9,1},{17,25},{25,17},{2,10},{10... | collective-permute-start | bytes 491528 | tf_op jit(solution)/shard_map/ppermute | solution.py:260
  36.1 11.0 %collective-permute-start.7 = (bf16[640,128]{1,0:T(8,128)(2,1)S(1)}, bf16[640,128]{1,0:T(8,128)(2,1)S(1)}, u32[]{:S(2)}, u32[]{:S(2)}) collective-permute-start(bf16[640,128]{1,0:T(8,128)(2,1)S(1)} %get-tuple-element.27), channel_id=1, source_target_pairs={{0,16},{8,24},{16,0},{24,8},{1,17},{9,25},{17,1},{25,9},{2,18},{10... | collective-permute-start | bytes 491528 | tf_op jit(solution)/shard_map/ppermute | solution.py:260
  37.6 9.5 %collective-permute-start.9 = (bf16[640,128]{1,0:T(8,128)(2,1)S(1)}, bf16[640,128]{1,0:T(8,128)(2,1)S(1)}, u32[]{:S(2)}, u32[]{:S(2)}) collective-permute-start(bf16[640,128]{1,0:T(8,128)(2,1)S(1)} %get-tuple-element.30), channel_id=1, source_target_pairs={{0,24},{8,16},{16,8},{24,0},{1,25},{9,17},{17,9},{25,1},{2,26},{10... | collective-permute-start | bytes 491528 | tf_op jit(solution)/shard_map/ppermute | solution.py:260
  43.1 6.2 %collective-permute-start.11 = (bf16[128,256]{1,0:T(8,128)(2,1)S(1)}, bf16[128,256]{1,0:T(8,128)(2,1)S(1)}, u32[]{:S(2)}, u32[]{:S(2)}) collective-permute-start(bf16[128,256]{1,0:T(8,128)(2,1)S(1)} %get-tuple-element.34), channel_id=1, source_target_pairs={{2,0},{3,1},{4,2},{5,3},{6,4},{7,5},{10,8},{11,9},{12,10},{13,11},... | collective-permute-start | bytes 196616 | tf_op jit(solution)/shard_map/ppermute | solution.py:265
  44.4 7.8 %collective-permute-start.12 = (bf16[128,256]{1,0:T(8,128)(2,1)S(1)}, bf16[128,256]{1,0:T(8,128)(2,1)S(1)}, u32[]{:S(2)}, u32[]{:S(2)}) collective-permute-start(bf16[128,256]{1,0:T(8,128)(2,1)S(1)} %get-tuple-element.35), channel_id=1, source_target_pairs={{4,0},{5,1},{6,2},{7,3},{12,8},{13,9},{14,10},{15,11},{20,16},{21,... | collective-permute-start | bytes 196616 | tf_op jit(solution)/shard_map/ppermute | solution.py:265
  45.8 9.1 %collective-permute-start.13 = (bf16[128,256]{1,0:T(8,128)(2,1)S(1)}, bf16[128,256]{1,0:T(8,128)(2,1)S(1)}, u32[]{:S(2)}, u32[]{:S(2)}) collective-permute-start(bf16[128,256]{1,0:T(8,128)(2,1)S(1)} %get-tuple-element.36), channel_id=1, source_target_pairs={{6,0},{7,1},{14,8},{15,9},{22,16},{23,17},{30,24},{31,25}} | collective-permute-start | bytes 196616 | tf_op jit(solution)/shard_map/ppermute | solution.py:265

commit v3 on v2

v3 whole, which is shorter than its diff:
```python
import functools
import math

import jax
import jax.numpy as jnp
from jax import lax
from jax.experimental import pallas as pl
from jax.experimental.pallas import tpu as pltpu
from jax.sharding import PartitionSpec as P

NT_DIMS = (((1,), (1,)), ((), ()))
UNROLLED = 4
EXTRA = 4
VMEM_LIMIT = 32 * 1024 * 1024
PACK_LIMIT = 62 * 1024 * 1024
LOG2E = math.log2(math.e)
SMEM = pl.BlockSpec(memory_space=pltpu.SMEM)
VMEM = pl.BlockSpec(memory_space=pltpu.VMEM)
HBM = pl.BlockSpec(memory_space=pltpu.HBM)


def up16(rows):
    return -(-rows // 16) * 16


def pack_kernel(heads, head, which, cached, after, place_ref, queries, grads, saved, totals, *refs):
    cache, refs = refs[:cached], refs[cached + after :]
    outs, refs = refs[: len(which)], refs[len(which) :]
    block, refs = (refs[0], refs[1:]) if cached else (None, refs)
    here, totals_here, ready, sems = refs
    rows = queries.shape[0]
    width = heads * head
    groups = queries.shape[1] // width
    ends = []
    for m, k in enumerate(which):
        columns = pl.ds(pl.multiple_of((place_ref[0] ^ k) * width, 128), width)
        for i, source in enumerate((grads, saved, queries)):
            ends.append((source.at[:, columns], here.at[m, i]))
    ends.append((totals, totals_here))
    for i, source in enumerate(cache):
        ends.append((source, block.at[:, pl.ds(i * head, head)]))
    loads = [pltpu.make_async_copy(*pair, sems.at[i]) for i, pair in enumerate(ends)]
    stores = [
        pltpu.make_async_copy(ready.at[m], out, sems.at[len(loads) + m])
        for m, out in enumerate(outs)
    ]
    for load in loads:
        load.start()
    lanes = lax.broadcasted_iota(jnp.int32, (rows, 128), 1)
    for m, k in enumerate(which):
        message = ready.at[m]
        for load in loads[3 * m : 3 * m + 3]:
            load.wait()
        dots = jnp.zeros((rows, 128), jnp.float32)
        for h in range(heads):
            columns = slice(h * head, (h + 1) * head)
            grad = here[m, 0, :, columns]
            out = here[m, 1, :, columns].astype(jnp.float32)
            product = grad.astype(jnp.float32) * out
            dots = jnp.where(lanes == h, jnp.sum(product, axis=1, keepdims=True), dots)
            message[h * rows : (h + 1) * rows, :] = here[m, 2, :, columns]
            message[(heads + h) * rows : (heads + h + 1) * rows, :] = grad
        dots = jnp.transpose(dots)[:heads]
        high = dots.astype(jnp.bfloat16).astype(jnp.float32)
        rest = dots - high
        middle = rest.astype(jnp.bfloat16).astype(jnp.float32)
        low = rest - middle
        if m == 0:
            loads[3 * len(which)].wait()
        chosen = totals_here[0:heads, :].astype(jnp.float32)
        for group in range(1, groups):
            part = totals_here[group * heads : (group + 1) * heads, :].astype(jnp.float32)
            chosen = jnp.where((place_ref[0] ^ k) == group, part, chosen)
        spare = jnp.zeros((message.shape[0] - 2 * heads * rows - EXTRA * heads, 128), jnp.float32)
        extra = jnp.concatenate([chosen, high, middle, low, spare], axis=0)
        message[2 * heads * rows :, :] = extra.astype(jnp.bfloat16)
        stores[m].start()
    for copy in loads[3 * len(which) + 1 :] + stores:
        copy.wait()


def attend_kernel(layers, heads, head, outer, inv_root, info, *refs):
    messages = refs[:layers]
    own, own_swapped, further, others = refs[layers : layers + 4]
    refs = refs[layers + 4 :]
    halves, refs = refs[:4], refs[4:]
    query_outs, refs = refs[:layers], refs[layers:]
    keys, values, query_turned, grad_turned, totals, dots, weights_all, score_all, query_acc = refs
    rows = own.shape[0]
    pair = 2 * rows
    z, x = info[0], info[1]
    near = outer // 2
    per_layer = heads * rows
    every = layers * per_layer
    for k in range(outer):
        at = pl.multiple_of((z ^ k) * pair, pair)
        here, there = (further.at[k - 1], others.at[k - 1]) if k else (own, own_swapped)
        for block, half in ((here, x), (there, 1 - x)):
            keys[pl.ds(at + half * rows, rows), :] = block[:, :head]
            values[pl.ds(at + half * rows, rows), :] = block[:, head:]

    for layer in range(layers):
        there = slice(layer * per_layer, (layer + 1) * per_layer)
        query_turned[:, there] = jnp.transpose(messages[layer][:per_layer, :])
        grad_turned[:, there] = jnp.transpose(messages[layer][per_layer : 2 * per_layer, :])
        extra = messages[layer][2 * per_layer :, :].astype(jnp.float32)
        high, middle, low = (extra[i * heads : (i + 1) * heads] for i in (1, 2, 3))
        spare = jnp.zeros((128 - 2 * heads, 128), jnp.float32)
        columns = jnp.transpose(
            jnp.concatenate([extra[:heads] * LOG2E, high + (middle + low), spare], axis=0)
        )
        for h in range(heads):
            at = layer * per_layer + h * rows
            totals[at : at + rows, :] = jnp.broadcast_to(columns[:, h : h + 1], (rows, 128))
            dots[at : at + rows, :] = jnp.broadcast_to(
                columns[:, heads + h : heads + h + 1], (rows, 128)
            )
    chunks = [
        (layer, h, min(2, heads - h)) for layer in range(layers) for h in range(0, heads, 2)
    ]

    def tiles(at, columns, masked):
        key_tile = keys[pl.ds(at, pair), :]
        value_tile = values[pl.ds(at, pair), :]
        for layer, h, count in chunks:
            tall = count * rows
            top = layer * per_layer + h * rows
            here = slice(top, top + tall)
            query = messages[layer][h * rows : h * rows + tall, :]
            grad = messages[layer][per_layer + h * rows : per_layer + h * rows + tall, :]
            total = jnp.concatenate([totals[here, :]] * (pair // 128), axis=1)
            dot = jnp.concatenate([dots[here, :]] * (pair // 128), axis=1)
            scores = lax.dot_general(query, key_tile, NT_DIMS, preferred_element_type=jnp.float32)
            weights = jnp.exp2(scores * (inv_root * LOG2E) - total)
            if masked:
                key_pos = lax.broadcasted_iota(jnp.int32, (1, pair), 1)
                query_pos = lax.broadcasted_iota(jnp.int32, (tall, 1), 0) % rows + x * rows
                weights = jnp.where(key_pos <= query_pos, weights, 0.0)
            weight_grads = lax.dot_general(
                grad, value_tile, NT_DIMS, preferred_element_type=jnp.float32
            )
            score_grads = weights * (weight_grads - dot) * inv_root
            weights_all[here, columns] = weights.astype(jnp.bfloat16)
            score_all[here, columns] = score_grads.astype(jnp.bfloat16)

    def leave(j, key_sum, value_sum):
        both = (jnp.transpose(key_sum), jnp.transpose(value_sum))
        step = z - j
        for half in range(2):
            chosen = jnp.concatenate(
                [jnp.where(x == half, total[:rows], total[rows:]) for total in both], axis=1
            ).astype(jnp.bfloat16)

            @pl.when(step < near)
            def _():
                halves[2 * half][step] = chosen

            @pl.when(step >= near)
            def _():
                halves[2 * half + 1][step - near] = chosen

    def sweep(j, masked):
        at = pl.multiple_of(j * pair, pair)
        here = slice(0, pair)
        tiles(at, here, masked)
        query_acc[...] += jnp.dot(
            score_all[:, here], keys[pl.ds(at, pair), :], preferred_element_type=jnp.float32
        )
        leave(
            j,
            jnp.dot(query_turned[...], score_all[:, here], preferred_element_type=jnp.float32),
            jnp.dot(grad_turned[...], weights_all[:, here], preferred_element_type=jnp.float32),
        )

    def full(j, carry):
        sweep(j, False)
        return carry

    def stepwise():
        query_acc[...] = jnp.zeros_like(query_acc)
        lax.fori_loop(0, z, full, 0)
        sweep(z, True)
        for layer in range(layers):
            query_outs[layer][...] = query_acc[
                layer * per_layer : (layer + 1) * per_layer, :
            ].astype(jnp.bfloat16)

    def whole():
        for j in range(outer):
            here = slice(j * pair, (j + 1) * pair)
            tiles(j * pair, here, j == outer - 1)
        key_sum = jnp.dot(query_turned[...], score_all[...], preferred_element_type=jnp.float32)
        value_sum = jnp.dot(grad_turned[...], weights_all[...], preferred_element_type=jnp.float32)
        for j in range(outer):
            here = slice(j * pair, (j + 1) * pair)
            leave(j, key_sum[:, here], value_sum[:, here])
        for layer in range(layers):
            there = slice(layer * per_layer, (layer + 1) * per_layer)
            query_outs[layer][...] = jnp.dot(
                score_all[there, :], keys[...], preferred_element_type=jnp.float32
            ).astype(jnp.bfloat16)

    if outer <= UNROLLED:
        pl.when(z == outer - 1)(whole)
        pl.when(z < outer - 1)(stepwise)
    else:
        stepwise()

    def blank(out, first):
        def body(k, carry):
            out[k - first] = jnp.zeros(out.shape[1:], jnp.bfloat16)
            return carry

        lax.fori_loop(jnp.maximum(z + 1, first), first + out.shape[0], body, 0)

    for half in range(2):
        blank(halves[2 * half], 0)
        blank(halves[2 * half + 1], near)


def add_kernel(mine, theirs, *outs):
    for k, out in enumerate(outs):
        out[...] = (mine[k].astype(jnp.float32) + theirs[k].astype(jnp.float32)).astype(
            jnp.bfloat16
        )


def place_kernel(heads, head, place_ref, *refs):
    messages, out = refs[:-1], refs[-1]
    rows = out.shape[0]
    for k, message in enumerate(messages):
        start = pl.multiple_of((place_ref[0] ^ k) * heads * head, 128)
        for h in range(heads):
            at = pl.multiple_of(start + h * head, 128)
            out[:, pl.ds(at, head)] = message[h * rows : (h + 1) * rows, :]


def total_kernel(*refs):
    blocks, key_out, value_out = refs[:-2], refs[-2], refs[-1]
    total = blocks[0][...].astype(jnp.float32)
    for block in blocks[1:]:
        total = total + block[...].astype(jnp.float32)
    head = key_out.shape[1]
    key_out[...] = total[:, :head].astype(jnp.bfloat16)
    value_out[...] = total[:, head:].astype(jnp.bfloat16)


def call(kernel, outs, in_specs, scratch=(), limit=VMEM_LIMIT, out_specs=None):
    return pl.pallas_call(
        kernel,
        out_shape=[jax.ShapeDtypeStruct(shape, jnp.bfloat16) for shape in outs],
        in_specs=in_specs,
        out_specs=out_specs or [VMEM] * len(outs),
        scratch_shapes=list(scratch),
        compiler_params=pltpu.CompilerParams(vmem_limit_bytes=limit),
    )


def swap(array, axis, bits):
    size = lax.axis_size(axis)
    return lax.ppermute(array, axis, [(i, i ^ bits) for i in range(size)])


def move(array, step):
    size = lax.axis_size("seq")
    return lax.ppermute(
        array, "seq", [(i, i + step) for i in range(size) if 0 <= i + step < size]
    )


def local(queries, cache_keys, cache_values, saved_out, out_grads, log_sums):
    sections = lax.axis_size("section")
    seq = lax.axis_size("seq")
    outer = seq // 2
    section_at = lax.axis_index("section").astype(jnp.int32).reshape(1)
    seq_at = lax.axis_index("seq").astype(jnp.int32)
    rows, head = cache_keys.shape
    heads = log_sums.shape[2] // sections
    inv_root = 1.0 / math.sqrt(head)
    info = jnp.stack([seq_at // 2, seq_at % 2])
    lines = 2 * heads * rows + up16(EXTRA * heads)

    totals = jnp.transpose(log_sums[0])

    half = sections // 2
    *sent, own = call(
        functools.partial(pack_kernel, heads, head, tuple(range(sections)), 2, 0),
        [(lines, 128)] * sections + [(rows, 2 * head)],
        [SMEM] + [HBM] * 6,
        [
            pltpu.VMEM((sections, 3, rows, heads * head), jnp.bfloat16),
            pltpu.VMEM(totals.shape, jnp.bfloat16),
            pltpu.VMEM((sections, lines, 128), jnp.bfloat16),
            pltpu.SemaphoreType.DMA((4 * sections + 3,)),
        ],
        limit=PACK_LIMIT,
        out_specs=[HBM] * (sections + 1),
    )(section_at, queries[0], out_grads[0], saved_out[0], totals, cache_keys, cache_values)
    passed = swap(sent[half + 1], "section", 1)
    messages = [sent[0], swap(sent[1], "section", 1), swap(sent[half], "section", half)]
    passed, tied = lax.optimization_barrier((passed, own))
    messages.append(swap(passed, "section", half))

    def exchange(own):
        far = {k: swap(own, "seq", 2 * k) for k in reversed(range(1, outer))}
        return jnp.stack([far[k] for k in range(1, outer)])

    def nothing(own):
        return jnp.zeros((outer - 1, *own.shape), own.dtype)

    further = lax.cond(seq_at >= 0, exchange, nothing, tied)
    blocks_here = [own, swap(own, "seq", 1), further, swap(further, "seq", 1)]

    every = sections * heads * rows
    across = 2 * rows * (outer if outer <= UNROLLED else 1)
    bf16 = functools.partial(pltpu.VMEM, dtype=jnp.bfloat16)
    mine_near, mine_far, theirs_near, theirs_far, *back = call(
        functools.partial(attend_kernel, sections, heads, head, outer, inv_root),
        [(outer // 2, rows, 2 * head), (outer - outer // 2, rows, 2 * head)] * 2
        + [(heads * rows, head)] * sections,
        [SMEM] + [VMEM] * (sections + 4),
        [bf16((seq * rows, head))] * 2
        + [bf16((head, every))] * 2
        + [pltpu.VMEM((every, 128), jnp.float32)] * 2
        + [bf16((every, across))] * 2
        + [pltpu.VMEM((every, head), jnp.float32)],
    )(info, *messages, *blocks_here)

    def reduced(mine, theirs):
        count = mine.shape[0]
        return call(add_kernel, [(rows, 2 * head)] * count, [VMEM] * 2)(
            mine, swap(theirs, "seq", 1)
        )

    far_sums = reduced(mine_far, theirs_far)
    summed = [*reduced(mine_near, theirs_near), *far_sums]
    blocks = [move(summed[k], -2 * k) for k in reversed(range(1, outer))] + [summed[0]]
    key_grads, value_grads = call(total_kernel, [(rows, head)] * 2, [VMEM] * outer)(*blocks)

    back = [back[0]] + [swap(back[k], "section", k) for k in range(1, sections)]
    (query_grads,) = call(
        functools.partial(place_kernel, heads, head),
        [queries.shape[1:]],
        [SMEM] + [VMEM] * sections,
    )(section_at, *back)
    return (query_grads[None], key_grads, value_grads)


def solution(mesh):
    placed = (
        P("section", "seq", None),
        P("seq", "section"),
        P("seq", "section"),
        P("section", "seq", None),
        P("section", "seq", None),
        P("section", "seq", None),
    )
    return jax.shard_map(
        local,
        mesh=mesh,
        in_specs=placed,
        out_specs=(P("section", "seq", None), P("seq", "section"), P("seq", "section")),
        check_vma=False,
    )
```

time: 55.9 us -> 49 us (0.88)
  starting transfers between devices: 21.6 us -> 19 us
  Pallas kernels: 10.3 us -> 8.38 us
  waiting for transfers between devices: 21.8 us -> 20.6 us
  other arithmetic: 1.02 us -> 0.1 us
    ppermute x6 -> x3, starting transfers between devices: 14.7 us -> 3.86 us  [move(): lax.ppermute(array, 'seq', [(i, i + step) for i in range(size) if 0 <= i...]
    ppermute x8 -> x14, starting transfers between devices: 6.91 us -> 15.2 us  [swap(): return lax.ppermute(array, axis, [(i, i ^ bits) for i in range(size)])]
    pallas_call x4, Pallas kernels: 8.66 us -> 6.77 us  [the longest x1 3.73 us: local(): call(functools.partial(attend_kernel, sections, heads, head, outer, inv_r...]
    ppermute x6 -> x3, waiting for transfers between devices: 7.11 us -> 5.9 us  [move(): lax.ppermute(array, 'seq', [(i, i + step) for i in range(size) if 0 <= i...]
    another operation x1, other arithmetic: 0.95 us -> 0.02 us  [exchange(): return jnp.stack([far[k] for k in range(1, outer)])]
    ppermute x8 -> x14, waiting for transfers between devices: 14.7 us -> 14.7 us  [swap(): return lax.ppermute(array, axis, [(i, i ^ bits) for i in range(size)])]
  transfers between devices with their start and end apart: 14 -> 17, of which waited for: 7 -> 9; matrix products, arithmetic and copies ran while one was open for 2% -> 0% of each run, Pallas kernels for 7% -> 2%
where the time goes in v3:
time: 49 us; the launch traced here: 48.8 us
  waiting for transfers between devices  20.6 us (42%)
  starting transfers between devices  19 us (39%)
  Pallas kernels  8.38 us (17%)
  between operations  0.75 us (2%)
    ppermute x14, starting transfers between devices, swap(): return lax.ppermute(array, axis, [(i, i ^ bits) for i in range(size)])  15.2 us
    ppermute x14, waiting for transfers between devices, swap(): return lax.ppermute(array, axis, [(i, i ^ bits) for i in range(size)])  14.7 us
    ppermute x3, waiting for transfers between devices, move(): lax.ppermute(array, 'seq', [(i, i + step) for i in range(size) if 0 <= i...  5.9 us
    ppermute x3, starting transfers between devices, move(): lax.ppermute(array, 'seq', [(i, i + step) for i in range(size) if 0 <= i...  3.86 us
    pallas_call x1, Pallas kernels, local(): call(functools.partial(attend_kernel, sections, heads, head, outer, inv_r...  3.73 us
    pallas_call x1, Pallas kernels, local(): call(functools.partial(pack_kernel, heads, head, tuple(range(sections)),...  2.97 us
  transfers between devices with their start and end apart: 17, of which 9 were waited for; matrix products, arithmetic and copies ran while one was open for 0% of the time, Pallas kernels for 2%

profile of v3, /device:TPU:0, one launch (start us, length us, event | category | flops | bytes accessed | tf_op | source)
XLA Modules:
  0.0 48.8 jit_solution(12738186793617985375)
XLA Ops:
  0.6 3.0 %shard_map.85 = (bf16[1312,128]{1,0:T(8,128)(2,1)}, bf16[1312,128]{1,0:T(8,128)(2,1)}, bf16[1312,128]{1,0:T(8,128)(2,1)}, bf16[1312,128]{1,0:T(8,128)(2,1)}, bf16[128,256]{1,0:T(8,128)(2,1)S(1)}) custom-call(s32[1]{0:T(128)} %bitcast.3.place_ref, bf16[128,2560]{1,0:T(8,128)(2,1)} %bitcast.14, bf16[128,2560]{1,0:T(8,128)(2,1)} %bitcast.15, ...), custom_call_target="tpu_custom_call" | custom-call | tf_op jit(solution)/shard_map/pallas_call | solution.py:286
  3.6 0.0 copy-start
  3.6 0.5 %collective-permute-start.5 = (bf16[1312,128]{1,0:T(8,128)(2,1)}, bf16[1312,128]{1,0:T(8,128)(2,1)S(1)}, u32[]{:S(2)}, u32[]{:S(2)}) collective-permute-start(bf16[1312,128]{1,0:T(8,128)(2,1)} %get-tuple-element.31), channel_id=1, source_target_pairs={{0,8},{8,0},{16,24},{24,16},{1,9},{9,1},{17,25},{25,17},{2,10},{10... | collective-permute-start | bytes 1007624 | tf_op jit(solution)/shard_map/ppermute | solution.py:261
  4.2 0.1 collective-permute-start.3
  4.2 2.9 %collective-permute-start.4 = (bf16[1312,128]{1,0:T(8,128)(2,1)}, bf16[1312,128]{1,0:T(8,128)(2,1)S(1)}, u32[]{:S(2)}, u32[]{:S(2)}) collective-permute-start(bf16[1312,128]{1,0:T(8,128)(2,1)} %get-tuple-element.30), channel_id=1, source_target_pairs={{0,16},{8,24},{16,0},{24,8},{1,17},{9,25},{17,1},{25,9},{2,18},{10... | collective-permute-start | bytes 1007624 | tf_op jit(solution)/shard_map/ppermute | solution.py:261
  7.2 0.0 collective-permute-done.5
  7.2 9.4 %conditional.1 = (bf16[3,128,256]{2,1,0:T(8,128)(2,1)S(1)}) conditional(s32[]{:T(128)} %convert_element_type.3, () %tuple.16, bf16[128,256]{1,0:T(8,128)(2,1)S(1)} %get-tuple-element.34.refs_4_), branch_computations={%region_0.1_spmd, %region_1.2_spmd} | conditional | flops 196608 | bytes 1179776 | solution.py:311
  7.2 3.6 %collective-permute-start.2 = (bf16[128,256]{1,0:T(8,128)(2,1)S(1)}, bf16[128,256]{1,0:T(8,128)(2,1)S(1)}, u32[]{:S(2)}, u32[]{:S(2)}) collective-permute-start(bf16[128,256]{1,0:T(8,128)(2,1)S(1)} %param.1), channel_id=1, source_target_pairs={{0,6},{1,7},{2,4},{3,5},{4,2},{5,3},{6,0},{7,1},{8,14},{9,15},{10,... | collective-permute-start | bytes 196616 | tf_op jit(solution)/shard_map/cond/branch_1_fun/ppermute | solution.py:261
  10.8 0.0 collective-permute-start.1
  10.8 0.8 %collective-permute-start = (bf16[128,256]{1,0:T(8,128)(2,1)S(1)}, bf16[128,256]{1,0:T(8,128)(2,1)S(1)}, u32[]{:S(2)}, u32[]{:S(2)}) collective-permute-start(bf16[128,256]{1,0:T(8,128)(2,1)S(1)} %param.1), channel_id=1, source_target_pairs={{0,2},{1,3},{2,0},{3,1},{4,6},{5,7},{6,4},{7,5},{8,10},{9,11},{10,... | collective-permute-start | bytes 196616 | tf_op jit(solution)/shard_map/cond/branch_1_fun/ppermute | solution.py:261
  11.6 2.1 %collective-permute-done.2 = bf16[128,256]{1,0:T(8,128)(2,1)S(1)} collective-permute-done((bf16[128,256]{1,0:T(8,128)(2,1)S(1)}, bf16[128,256]{1,0:T(8,128)(2,1)S(1)}, u32[]{:S(2)}, u32[]{:S(2)}) %collective-permute-start.2) | collective-permute-done | bytes 65568 | tf_op jit(solution)/shard_map/cond/branch_1_fun/ppermute | solution.py:261
  13.7 2.8 %collective-permute-done.1 = bf16[128,256]{1,0:T(8,128)(2,1)S(1)} collective-permute-done((bf16[128,256]{1,0:T(8,128)(2,1)S(1)}, bf16[128,256]{1,0:T(8,128)(2,1)S(1)}, u32[]{:S(2)}, u32[]{:S(2)}) %collective-permute-start.1) | collective-permute-done | bytes 65568 | tf_op jit(solution)/shard_map/cond/branch_1_fun/ppermute | solution.py:261
  16.5 0.0 collective-permute-done
  16.5 1.6 %collective-permute-start.6 = (bf16[1312,128]{1,0:T(8,128)(2,1)S(1)}, bf16[1312,128]{1,0:T(8,128)(2,1)S(1)}, u32[]{:S(2)}, u32[]{:S(2)}) collective-permute-start(bf16[1312,128]{1,0:T(8,128)(2,1)S(1)} %collective-permute-done.5), channel_id=1, source_target_pairs={{0,16},{8,24},{16,0},{24,8},{1,17},{9,25},{17,1},{25,9},{2,18},{10... | collective-permute-start | bytes 1007624 | tf_op jit(solution)/shard_map/ppermute | solution.py:261
  18.1 1.5 %collective-permute-start.8 = (bf16[3,128,256]{2,1,0:T(8,128)(2,1)S(1)}, bf16[3,128,256]{2,1,0:T(8,128)(2,1)S(1)}, u32[]{:S(2)}, u32[]{:S(2)}) collective-permute-start(bf16[3,128,256]{2,1,0:T(8,128)(2,1)S(1)} %get-tuple-element.49.refs_6_), channel_id=1, source_target_pairs={{0,1},{1,0},{2,3},{3,2},{4,5},{5,4},{6,7},{7,6},{8,9},{9,8},{10,11... | collective-permute-start | bytes 589832 | tf_op jit(solution)/shard_map/ppermute | solution.py:261
  19.6 0.5 %collective-permute-start.7 = (bf16[128,256]{1,0:T(8,128)(2,1)S(1)}, bf16[128,256]{1,0:T(8,128)(2,1)S(1)}, u32[]{:S(2)}, u32[]{:S(2)}) collective-permute-start(bf16[128,256]{1,0:T(8,128)(2,1)S(1)} %get-tuple-element.34.refs_4_), channel_id=1, source_target_pairs={{0,1},{1,0},{2,3},{3,2},{4,5},{5,4},{6,7},{7,6},{8,9},{9,8},{10,11... | collective-permute-start | bytes 196616 | tf_op jit(solution)/shard_map/ppermute | solution.py:261
  20.1 0.1 pad_add_fusion.info
  20.2 5.5 %collective-permute-done.7.refs_5_ = bf16[128,256]{1,0:T(8,128)(2,1)S(1)} collective-permute-done((bf16[128,256]{1,0:T(8,128)(2,1)S(1)}, bf16[128,256]{1,0:T(8,128)(2,1)S(1)}, u32[]{:S(2)}, u32[]{:S(2)}) %collective-permute-start.7) | collective-permute-done | bytes 65568 | tf_op jit(solution)/shard_map/ppermute | solution.py:261
  25.7 0.0 collective-permute-done.3.refs_1_
  25.7 0.0 collective-permute-done.4.refs_2_
  25.7 0.0 collective-permute-done.8.refs_7_
  25.7 0.4 collective-permute-done.6.refs_3_
  26.1 0.0 copy-done
  26.1 3.7 %shard_map.86 = (bf16[2,128,256]{2,1,0:T(8,128)(2,1)S(1)}, bf16[2,128,256]{2,1,0:T(8,128)(2,1)S(1)}, bf16[2,128,256]{2,1,0:T(8,128)(2,1)S(1)}, bf16[2,128,256]{2...) custom-call(s32[2]{0:T(128)S(1)} %pad_add_fusion.info, ...), custom_call_target="tpu_custom_call" | custom-call | tf_op jit(solution)/shard_map/pallas_call | solution.py:317
  29.8 0.1 collective-permute-start.9
  29.9 1.6 %collective-permute-start.12 = (bf16[2,128,256]{2,1,0:T(8,128)(2,1)S(1)}, bf16[2,128,256]{2,1,0:T(8,128)(2,1)S(1)}, u32[]{:S(2)}, u32[]{:S(2)}) collective-permute-start(bf16[2,128,256]{2,1,0:T(8,128)(2,1)S(1)} %get-tuple-element.40), channel_id=1, source_target_pairs={{0,1},{1,0},{2,3},{3,2},{4,5},{5,4},{6,7},{7,6},{8,9},{9,8},{10,11... | collective-permute-start | bytes 393224 | tf_op jit(solution)/shard_map/ppermute | solution.py:261
  31.5 0.5 %collective-permute-start.15 = (bf16[2,128,256]{2,1,0:T(8,128)(2,1)S(1)}, bf16[2,128,256]{2,1,0:T(8,128)(2,1)S(1)}, u32[]{:S(2)}, u32[]{:S(2)}) collective-permute-start(bf16[2,128,256]{2,1,0:T(8,128)(2,1)S(1)} %get-tuple-element.44), channel_id=1, source_target_pairs={{0,1},{1,0},{2,3},{3,2},{4,5},{5,4},{6,7},{7,6},{8,9},{9,8},{10,11... | collective-permute-start | bytes 393224 | tf_op jit(solution)/shard_map/ppermute | solution.py:261
  32.0 1.5 %collective-permute-start.10 = (bf16[640,128]{1,0:T(8,128)(2,1)S(1)}, bf16[640,128]{1,0:T(8,128)(2,1)S(1)}, u32[]{:S(2)}, u32[]{:S(2)}) collective-permute-start(bf16[640,128]{1,0:T(8,128)(2,1)S(1)} %get-tuple-element.37), channel_id=1, source_target_pairs={{0,16},{8,24},{16,0},{24,8},{1,17},{9,25},{17,1},{25,9},{2,18},{10... | collective-permute-start | bytes 491528 | tf_op jit(solution)/shard_map/ppermute | solution.py:261
  33.5 0.0 collective-permute-start.11
  33.5 2.8 %collective-permute-done.12.theirs = bf16[2,128,256]{2,1,0:T(8,128)(2,1)S(1)} collective-permute-done((bf16[2,128,256]{2,1,0:T(8,128)(2,1)S(1)}, bf16[2,128,256]{2,1,0:T(8,128)(2,1)S(1)}, u32[]{:S(2)}, u32[]{:S(2)}) %collective-permute-start.12) | collective-permute-done | bytes 131104 | tf_op jit(solution)/shard_map/ppermute | solution.py:261
  36.3 1.3 %collective-permute-start.13 = (bf16[128,256]{1,0:T(8,128)(2,1)S(1)}, bf16[128,256]{1,0:T(8,128)(2,1)S(1)}, u32[]{:S(2)}, u32[]{:S(2)}) collective-permute-start(bf16[128,256]{1,0:T(8,128)(2,1)S(1)} %get-tuple-element.41), channel_id=1, source_target_pairs={{6,0},{7,1},{14,8},{15,9},{22,16},{23,17},{30,24},{31,25}} | collective-permute-start | bytes 196616 | tf_op jit(solution)/shard_map/ppermute | solution.py:266
  37.6 1.0 %collective-permute-done.15.theirs = bf16[2,128,256]{2,1,0:T(8,128)(2,1)S(1)} collective-permute-done((bf16[2,128,256]{2,1,0:T(8,128)(2,1)S(1)}, bf16[2,128,256]{2,1,0:T(8,128)(2,1)S(1)}, u32[]{:S(2)}, u32[]{:S(2)}) %collective-permute-start.15) | collective-permute-done | bytes 131104 | tf_op jit(solution)/shard_map/ppermute | solution.py:261
  38.6 1.3 %collective-permute-start.14 = (bf16[128,256]{1,0:T(8,128)(2,1)S(1)}, bf16[128,256]{1,0:T(8,128)(2,1)S(1)}, u32[]{:S(2)}, u32[]{:S(2)}) collective-permute-start(bf16[128,256]{1,0:T(8,128)(2,1)S(1)} %get-tuple-element.42), channel_id=1, source_target_pairs={{4,0},{5,1},{6,2},{7,3},{12,8},{13,9},{14,10},{15,11},{20,16},{21,... | collective-permute-start | bytes 196616 | tf_op jit(solution)/shard_map/ppermute | solution.py:266
  40.0 0.0 collective-permute-done.9.refs_1_
  40.0 1.3 %collective-permute-start.16 = (bf16[128,256]{1,0:T(8,128)(2,1)S(1)}, bf16[128,256]{1,0:T(8,128)(2,1)S(1)}, u32[]{:S(2)}, u32[]{:S(2)}) collective-permute-start(bf16[128,256]{1,0:T(8,128)(2,1)S(1)} %get-tuple-element.45), channel_id=1, source_target_pairs={{2,0},{3,1},{4,2},{5,3},{6,4},{7,5},{10,8},{11,9},{12,10},{13,11},... | collective-permute-start | bytes 196616 | tf_op jit(solution)/shard_map/ppermute | solution.py:266
  41.3 0.0 collective-permute-done.10.refs_2_
  41.3 0.0 collective-permute-done.11.refs_3_
  41.3 1.0 %shard_map.87 = bf16[128,2560]{1,0:T(8,128)(2,1)} custom-call(s32[1]{0:T(128)} %bitcast.3.place_ref, bf16[640,128]{1,0:T(8,128)(2,1)S(1)} %get-tuple-element.35.refs_0_, bf16[640,128]{1,0:T(8,128)(2,1)S(1)} %collective-permute-done.9.refs_1_, bf16[640,128]{1,0:T(8,128)(2,1)S(1)} %collective-permute-done.10.refs_2_, ...), custom_call_target="tpu_custom_call" | custom-call | tf_op jit(solution)/shard_map/pallas_call | solution.py:341
  42.3 4.2 %collective-permute-done.13.refs_0_ = bf16[128,256]{1,0:T(8,128)(2,1)S(1)} collective-permute-done((bf16[128,256]{1,0:T(8,128)(2,1)S(1)}, bf16[128,256]{1,0:T(8,128)(2,1)S(1)}, u32[]{:S(2)}, u32[]{:S(2)}) %collective-permute-start.13) | collective-permute-done | bytes 65568 | tf_op jit(solution)/shard_map/ppermute | solution.py:266
  46.5 1.3 %collective-permute-done.14.refs_1_ = bf16[128,256]{1,0:T(8,128)(2,1)S(1)} collective-permute-done((bf16[128,256]{1,0:T(8,128)(2,1)S(1)}, bf16[128,256]{1,0:T(8,128)(2,1)S(1)}, u32[]{:S(2)}, u32[]{:S(2)}) %collective-permute-start.14) | collective-permute-done | bytes 65568 | tf_op jit(solution)/shard_map/ppermute | solution.py:266
  47.8 0.3 collective-permute-done.16.refs_2_
  48.2 0.7 %shard_map.90 = (bf16[128,128]{1,0:T(8,128)(2,1)}, bf16[128,128]{1,0:T(8,128)(2,1)}) custom-call(bf16[128,256]{1,0:T(8,128)(2,1)S(1)} %collective-permute-done.13.refs_0_, bf16[128,256]{1,0:T(8,128)(2,1)S(1)} %collective-permute-done.14.refs_1_, bf16[128,256]{1,0:T(8,128)(2,1)S(1)} %collective-permute-done.16.refs_2_, ...), custom_call_target="tpu_custom_call" | custom-call | tf_op jit(solution)/shard_map/pallas_call | solution.py:338
  (3 shorter events, 0.1 us)
Async XLA Ops:
  3.6 22.5 %copy-start = (bf16[1312,128]{1,0:T(8,128)(2,1)S(1)}, bf16[1312,128]{1,0:T(8,128)(2,1)}, u32[]{:S(2)}) copy-start(bf16[1312,128]{1,0:T(8,128)(2,1)} %get-tuple-element.28.refs_0_) | copy-start | bytes 1007620
  3.6 3.5 %collective-permute-start.5 = (bf16[1312,128]{1,0:T(8,128)(2,1)}, bf16[1312,128]{1,0:T(8,128)(2,1)S(1)}, u32[]{:S(2)}, u32[]{:S(2)}) collective-permute-start(bf16[1312,128]{1,0:T(8,128)(2,1)} %get-tuple-element.31), channel_id=1, source_target_pairs={{0,8},{8,0},{16,24},{24,16},{1,9},{9,1},{17,25},{25,17},{2,10},{10... | collective-permute-start | bytes 1007624 | tf_op jit(solution)/shard_map/ppermute | solution.py:261
  4.2 21.6 %collective-permute-start.3 = (bf16[1312,128]{1,0:T(8,128)(2,1)}, bf16[1312,128]{1,0:T(8,128)(2,1)S(1)}, u32[]{:S(2)}, u32[]{:S(2)}) collective-permute-start(bf16[1312,128]{1,0:T(8,128)(2,1)} %get-tuple-element.29), channel_id=1, source_target_pairs={{0,8},{8,0},{16,24},{24,16},{1,9},{9,1},{17,25},{25,17},{2,10},{10... | collective-permute-start | bytes 1007624 | tf_op jit(solution)/shard_map/ppermute | solution.py:261
  4.2 21.5 %collective-permute-start.4 = (bf16[1312,128]{1,0:T(8,128)(2,1)}, bf16[1312,128]{1,0:T(8,128)(2,1)S(1)}, u32[]{:S(2)}, u32[]{:S(2)}) collective-permute-start(bf16[1312,128]{1,0:T(8,128)(2,1)} %get-tuple-element.30), channel_id=1, source_target_pairs={{0,16},{8,24},{16,0},{24,8},{1,17},{9,25},{17,1},{25,9},{2,18},{10... | collective-permute-start | bytes 1007624 | tf_op jit(solution)/shard_map/ppermute | solution.py:261
  7.2 6.5 %collective-permute-start.2 = (bf16[128,256]{1,0:T(8,128)(2,1)S(1)}, bf16[128,256]{1,0:T(8,128)(2,1)S(1)}, u32[]{:S(2)}, u32[]{:S(2)}) collective-permute-start(bf16[128,256]{1,0:T(8,128)(2,1)S(1)} %param.1), channel_id=1, source_target_pairs={{0,6},{1,7},{2,4},{3,5},{4,2},{5,3},{6,0},{7,1},{8,14},{9,15},{10,... | collective-permute-start | bytes 196616 | tf_op jit(solution)/shard_map/cond/branch_1_fun/ppermute | solution.py:261
  10.8 5.7 %collective-permute-start.1 = (bf16[128,256]{1,0:T(8,128)(2,1)S(1)}, bf16[128,256]{1,0:T(8,128)(2,1)S(1)}, u32[]{:S(2)}, u32[]{:S(2)}) collective-permute-start(bf16[128,256]{1,0:T(8,128)(2,1)S(1)} %param.1), channel_id=1, source_target_pairs={{0,4},{1,5},{2,6},{3,7},{4,0},{5,1},{6,2},{7,3},{8,12},{9,13},{10,... | collective-permute-start | bytes 196616 | tf_op jit(solution)/shard_map/cond/branch_1_fun/ppermute | solution.py:261
  10.8 5.7 %collective-permute-start = (bf16[128,256]{1,0:T(8,128)(2,1)S(1)}, bf16[128,256]{1,0:T(8,128)(2,1)S(1)}, u32[]{:S(2)}, u32[]{:S(2)}) collective-permute-start(bf16[128,256]{1,0:T(8,128)(2,1)S(1)} %param.1), channel_id=1, source_target_pairs={{0,2},{1,3},{2,0},{3,1},{4,6},{5,7},{6,4},{7,5},{8,10},{9,11},{10,... | collective-permute-start | bytes 196616 | tf_op jit(solution)/shard_map/cond/branch_1_fun/ppermute | solution.py:261
  16.5 9.6 %collective-permute-start.6 = (bf16[1312,128]{1,0:T(8,128)(2,1)S(1)}, bf16[1312,128]{1,0:T(8,128)(2,1)S(1)}, u32[]{:S(2)}, u32[]{:S(2)}) collective-permute-start(bf16[1312,128]{1,0:T(8,128)(2,1)S(1)} %collective-permute-done.5), channel_id=1, source_target_pairs={{0,16},{8,24},{16,0},{24,8},{1,17},{9,25},{17,1},{25,9},{2,18},{10... | collective-permute-start | bytes 1007624 | tf_op jit(solution)/shard_map/ppermute | solution.py:261
  18.1 7.6 %collective-permute-start.8 = (bf16[3,128,256]{2,1,0:T(8,128)(2,1)S(1)}, bf16[3,128,256]{2,1,0:T(8,128)(2,1)S(1)}, u32[]{:S(2)}, u32[]{:S(2)}) collective-permute-start(bf16[3,128,256]{2,1,0:T(8,128)(2,1)S(1)} %get-tuple-element.49.refs_6_), channel_id=1, source_target_pairs={{0,1},{1,0},{2,3},{3,2},{4,5},{5,4},{6,7},{7,6},{8,9},{9,8},{10,11... | collective-permute-start | bytes 589832 | tf_op jit(solution)/shard_map/ppermute | solution.py:261
  19.6 6.1 %collective-permute-start.7 = (bf16[128,256]{1,0:T(8,128)(2,1)S(1)}, bf16[128,256]{1,0:T(8,128)(2,1)S(1)}, u32[]{:S(2)}, u32[]{:S(2)}) collective-permute-start(bf16[128,256]{1,0:T(8,128)(2,1)S(1)} %get-tuple-element.34.refs_4_), channel_id=1, source_target_pairs={{0,1},{1,0},{2,3},{3,2},{4,5},{5,4},{6,7},{7,6},{8,9},{9,8},{10,11... | collective-permute-start | bytes 196616 | tf_op jit(solution)/shard_map/ppermute | solution.py:261
  29.8 10.1 %collective-permute-start.9 = (bf16[640,128]{1,0:T(8,128)(2,1)S(1)}, bf16[640,128]{1,0:T(8,128)(2,1)S(1)}, u32[]{:S(2)}, u32[]{:S(2)}) collective-permute-start(bf16[640,128]{1,0:T(8,128)(2,1)S(1)} %get-tuple-element.36), channel_id=1, source_target_pairs={{0,8},{8,0},{16,24},{24,16},{1,9},{9,1},{17,25},{25,17},{2,10},{10... | collective-permute-start | bytes 491528 | tf_op jit(solution)/shard_map/ppermute | solution.py:261
  29.9 6.4 %collective-permute-start.12 = (bf16[2,128,256]{2,1,0:T(8,128)(2,1)S(1)}, bf16[2,128,256]{2,1,0:T(8,128)(2,1)S(1)}, u32[]{:S(2)}, u32[]{:S(2)}) collective-permute-start(bf16[2,128,256]{2,1,0:T(8,128)(2,1)S(1)} %get-tuple-element.40), channel_id=1, source_target_pairs={{0,1},{1,0},{2,3},{3,2},{4,5},{5,4},{6,7},{7,6},{8,9},{9,8},{10,11... | collective-permute-start | bytes 393224 | tf_op jit(solution)/shard_map/ppermute | solution.py:261
  31.5 7.2 %collective-permute-start.15 = (bf16[2,128,256]{2,1,0:T(8,128)(2,1)S(1)}, bf16[2,128,256]{2,1,0:T(8,128)(2,1)S(1)}, u32[]{:S(2)}, u32[]{:S(2)}) collective-permute-start(bf16[2,128,256]{2,1,0:T(8,128)(2,1)S(1)} %get-tuple-element.44), channel_id=1, source_target_pairs={{0,1},{1,0},{2,3},{3,2},{4,5},{5,4},{6,7},{7,6},{8,9},{9,8},{10,11... | collective-permute-start | bytes 393224 | tf_op jit(solution)/shard_map/ppermute | solution.py:261
  32.0 9.3 %collective-permute-start.10 = (bf16[640,128]{1,0:T(8,128)(2,1)S(1)}, bf16[640,128]{1,0:T(8,128)(2,1)S(1)}, u32[]{:S(2)}, u32[]{:S(2)}) collective-permute-start(bf16[640,128]{1,0:T(8,128)(2,1)S(1)} %get-tuple-element.37), channel_id=1, source_target_pairs={{0,16},{8,24},{16,0},{24,8},{1,17},{9,25},{17,1},{25,9},{2,18},{10... | collective-permute-start | bytes 491528 | tf_op jit(solution)/shard_map/ppermute | solution.py:261
  33.5 7.8 %collective-permute-start.11 = (bf16[640,128]{1,0:T(8,128)(2,1)S(1)}, bf16[640,128]{1,0:T(8,128)(2,1)S(1)}, u32[]{:S(2)}, u32[]{:S(2)}) collective-permute-start(bf16[640,128]{1,0:T(8,128)(2,1)S(1)} %get-tuple-element.38), channel_id=1, source_target_pairs={{0,24},{8,16},{16,8},{24,0},{1,25},{9,17},{17,9},{25,1},{2,26},{10... | collective-permute-start | bytes 491528 | tf_op jit(solution)/shard_map/ppermute | solution.py:261
  36.3 10.2 %collective-permute-start.13 = (bf16[128,256]{1,0:T(8,128)(2,1)S(1)}, bf16[128,256]{1,0:T(8,128)(2,1)S(1)}, u32[]{:S(2)}, u32[]{:S(2)}) collective-permute-start(bf16[128,256]{1,0:T(8,128)(2,1)S(1)} %get-tuple-element.41), channel_id=1, source_target_pairs={{6,0},{7,1},{14,8},{15,9},{22,16},{23,17},{30,24},{31,25}} | collective-permute-start | bytes 196616 | tf_op jit(solution)/shard_map/ppermute | solution.py:266
  38.6 9.2 %collective-permute-start.14 = (bf16[128,256]{1,0:T(8,128)(2,1)S(1)}, bf16[128,256]{1,0:T(8,128)(2,1)S(1)}, u32[]{:S(2)}, u32[]{:S(2)}) collective-permute-start(bf16[128,256]{1,0:T(8,128)(2,1)S(1)} %get-tuple-element.42), channel_id=1, source_target_pairs={{4,0},{5,1},{6,2},{7,3},{12,8},{13,9},{14,10},{15,11},{20,16},{21,... | collective-permute-start | bytes 196616 | tf_op jit(solution)/shard_map/ppermute | solution.py:266
  40.0 8.2 %collective-permute-start.16 = (bf16[128,256]{1,0:T(8,128)(2,1)S(1)}, bf16[128,256]{1,0:T(8,128)(2,1)S(1)}, u32[]{:S(2)}, u32[]{:S(2)}) collective-permute-start(bf16[128,256]{1,0:T(8,128)(2,1)S(1)} %get-tuple-element.45), channel_id=1, source_target_pairs={{2,0},{3,1},{4,2},{5,3},{6,4},{7,5},{10,8},{11,9},{12,10},{13,11},... | collective-permute-start | bytes 196616 | tf_op jit(solution)/shard_map/ppermute | solution.py:266

commit v4 on v3

--- a/solution.py
+++ b/solution.py
@@ -85,7 +85,7 @@
     refs = refs[layers + 4 :]
     halves, refs = refs[:4], refs[4:]
     query_outs, refs = refs[:layers], refs[layers:]
-    keys, values, query_turned, grad_turned, totals, dots, weights_all, score_all, query_acc = refs
+    keys, values, query_turned, grad_turned, totals, dots, weights_all, score_all, *refs = refs
     rows = own.shape[0]
     pair = 2 * rows
     z, x = info[0], info[1]
@@ -119,7 +119,7 @@
         (layer, h, min(2, heads - h)) for layer in range(layers) for h in range(0, heads, 2)
     ]
 
-    def tiles(at, columns, masked):
+    def tiles(at, columns, masked, turned=None):
         key_tile = keys[pl.ds(at, pair), :]
         value_tile = values[pl.ds(at, pair), :]
         for layer, h, count in chunks:
@@ -141,15 +141,18 @@
             )
             score_grads = weights * (weight_grads - dot) * inv_root
             weights_all[here, columns] = weights.astype(jnp.bfloat16)
-            score_all[here, columns] = score_grads.astype(jnp.bfloat16)
+            score_grads = score_grads.astype(jnp.bfloat16)
+            score_all[here, columns] = score_grads
+            if turned is not None:
+                turned[columns, here] = jnp.transpose(score_grads)
 
     def leave(j, key_sum, value_sum):
-        both = (jnp.transpose(key_sum), jnp.transpose(value_sum))
+        both = [jnp.transpose(total.astype(jnp.bfloat16)) for total in (key_sum, value_sum)]
         step = z - j
         for half in range(2):
             chosen = jnp.concatenate(
                 [jnp.where(x == half, total[:rows], total[rows:]) for total in both], axis=1
-            ).astype(jnp.bfloat16)
+            )
 
             @pl.when(step < near)
             def _():
@@ -159,7 +162,7 @@
             def _():
                 halves[2 * half + 1][step - near] = chosen
 
-    def sweep(j, masked):
+    def sweep(j, masked, query_acc):
         at = pl.multiple_of(j * pair, pair)
         here = slice(0, pair)
         tiles(at, here, masked)
@@ -172,33 +175,38 @@
             jnp.dot(grad_turned[...], weights_all[:, here], preferred_element_type=jnp.float32),
         )
 
-    def full(j, carry):
-        sweep(j, False)
-        return carry
-
     def stepwise():
+        query_acc = refs[0]
         query_acc[...] = jnp.zeros_like(query_acc)
+
+        def full(j, carry):
+            sweep(j, False, query_acc)
+            return carry
+
         lax.fori_loop(0, z, full, 0)
-        sweep(z, True)
+        sweep(z, True, query_acc)
         for layer in range(layers):
             query_outs[layer][...] = query_acc[
                 layer * per_layer : (layer + 1) * per_layer, :
             ].astype(jnp.bfloat16)
 
     def whole():
+        score_turned = refs[1]
         for j in range(outer):
             here = slice(j * pair, (j + 1) * pair)
-            tiles(j * pair, here, j == outer - 1)
+            tiles(j * pair, here, j == outer - 1, score_turned)
         key_sum = jnp.dot(query_turned[...], score_all[...], preferred_element_type=jnp.float32)
         value_sum = jnp.dot(grad_turned[...], weights_all[...], preferred_element_type=jnp.float32)
         for j in range(outer):
             here = slice(j * pair, (j + 1) * pair)
             leave(j, key_sum[:, here], value_sum[:, here])
+        key_turned = jnp.transpose(keys[...])
         for layer in range(layers):
             there = slice(layer * per_layer, (layer + 1) * per_layer)
-            query_outs[layer][...] = jnp.dot(
-                score_all[there, :], keys[...], preferred_element_type=jnp.float32
-            ).astype(jnp.bfloat16)
+            total = jnp.dot(
+                key_turned, score_turned[:, there], preferred_element_type=jnp.float32
+            )
+            query_outs[layer][...] = jnp.transpose(total.astype(jnp.bfloat16))
 
     if outer <= UNROLLED:
         pl.when(z == outer - 1)(whole)
@@ -323,7 +331,8 @@
         + [bf16((head, every))] * 2
         + [pltpu.VMEM((every, 128), jnp.float32)] * 2
         + [bf16((every, across))] * 2
-        + [pltpu.VMEM((every, head), jnp.float32)],
+        + [pltpu.VMEM((every, head), jnp.float32)]
+        + ([bf16((across, every))] if outer <= UNROLLED else []),
     )(info, *messages, *blocks_here)
 
     def reduced(mine, theirs):
@@ -335,14 +344,15 @@
     far_sums = reduced(mine_far, theirs_far)
     summed = [*reduced(mine_near, theirs_near), *far_sums]
     blocks = [move(summed[k], -2 * k) for k in reversed(range(1, outer))] + [summed[0]]
-    key_grads, value_grads = call(total_kernel, [(rows, head)] * 2, [VMEM] * outer)(*blocks)
-
-    back = [back[0]] + [swap(back[k], "section", k) for k in range(1, sections)]
+    back[1:] = lax.optimization_barrier((swap(back[1], "section", 1), *back[2:]))
+    back[2:] = [swap(back[k], "section", k) for k in range(2, sections)]
     (query_grads,) = call(
         functools.partial(place_kernel, heads, head),
         [queries.shape[1:]],
         [SMEM] + [VMEM] * sections,
     )(section_at, *back)
+    blocks[0], query_grads = lax.optimization_barrier((blocks[0], query_grads))
+    key_grads, value_grads = call(total_kernel, [(rows, head)] * 2, [VMEM] * outer)(*blocks)
     return (query_grads[None], key_grads, value_grads)
 
 

time: 49 us -> 48.5 us (0.990)
  waiting for transfers between devices: 20.6 us -> 20 us
    ppermute x14, waiting for transfers between devices: 14.7 us -> 13.9 us  [swap(): return lax.ppermute(array, axis, [(i, i ^ bits) for i in range(size)])]
  transfers between devices with their start and end apart: 17 -> 17, of which waited for: 9 -> 8; matrix products, arithmetic and copies ran while one was open for 0% -> 0% of each run, Pallas kernels for 2% -> 2%
where the time goes in v4:
time: 48.5 us; the launch traced here: 48.3 us
  waiting for transfers between devices  20 us (41%)
  starting transfers between devices  19 us (39%)
  Pallas kernels  8.36 us (17%)
  between operations  0.74 us (2%)
    ppermute x14, starting transfers between devices, swap(): return lax.ppermute(array, axis, [(i, i ^ bits) for i in range(size)])  15.2 us
    ppermute x14, waiting for transfers between devices, swap(): return lax.ppermute(array, axis, [(i, i ^ bits) for i in range(size)])  13.9 us
    ppermute x3, waiting for transfers between devices, move(): lax.ppermute(array, 'seq', [(i, i + step) for i in range(size) if 0 <= i...  6.19 us
    ppermute x3, starting transfers between devices, move(): lax.ppermute(array, 'seq', [(i, i + step) for i in range(size) if 0 <= i...  3.88 us
    pallas_call x1, Pallas kernels, local(): call(functools.partial(attend_kernel, sections, heads, head, outer, inv_r...  3.71 us
    pallas_call x1, Pallas kernels, local(): call(functools.partial(pack_kernel, heads, head, tuple(range(sections)),...  2.97 us
  transfers between devices with their start and end apart: 17, of which 8 were waited for; matrix products, arithmetic and copies ran while one was open for 0% of the time, Pallas kernels for 2%

profile of v4, /device:TPU:0, one launch (start us, length us, event | category | flops | bytes accessed | tf_op | source)
XLA Modules:
  0.0 48.3 jit_solution(11187659817627583611)
XLA Ops:
  0.6 3.0 %shard_map.85 = (bf16[1312,128]{1,0:T(8,128)(2,1)}, bf16[1312,128]{1,0:T(8,128)(2,1)}, bf16[1312,128]{1,0:T(8,128)(2,1)}, bf16[1312,128]{1,0:T(8,128)(2,1)}, bf16[128,256]{1,0:T(8,128)(2,1)S(1)}) custom-call(s32[1]{0:T(128)} %bitcast.5.place_ref, bf16[128,2560]{1,0:T(8,128)(2,1)} %bitcast.14, bf16[128,2560]{1,0:T(8,128)(2,1)} %bitcast.15, ...), custom_call_target="tpu_custom_call" | custom-call | tf_op jit(solution)/shard_map/pallas_call | solution.py:294
  3.6 0.0 copy-start
  3.6 0.5 %collective-permute-start.5 = (bf16[1312,128]{1,0:T(8,128)(2,1)}, bf16[1312,128]{1,0:T(8,128)(2,1)S(1)}, u32[]{:S(2)}, u32[]{:S(2)}) collective-permute-start(bf16[1312,128]{1,0:T(8,128)(2,1)} %get-tuple-element.36), channel_id=1, source_target_pairs={{0,8},{8,0},{16,24},{24,16},{1,9},{9,1},{17,25},{25,17},{2,10},{10... | collective-permute-start | bytes 1007624 | tf_op jit(solution)/shard_map/ppermute | solution.py:269
  4.2 0.1 collective-permute-start.3
  4.2 2.9 %collective-permute-start.4 = (bf16[1312,128]{1,0:T(8,128)(2,1)}, bf16[1312,128]{1,0:T(8,128)(2,1)S(1)}, u32[]{:S(2)}, u32[]{:S(2)}) collective-permute-start(bf16[1312,128]{1,0:T(8,128)(2,1)} %get-tuple-element.35), channel_id=1, source_target_pairs={{0,16},{8,24},{16,0},{24,8},{1,17},{9,25},{17,1},{25,9},{2,18},{10... | collective-permute-start | bytes 1007624 | tf_op jit(solution)/shard_map/ppermute | solution.py:269
  7.2 0.0 collective-permute-done.5
  7.2 9.4 %conditional.1 = (bf16[3,128,256]{2,1,0:T(8,128)(2,1)S(1)}) conditional(s32[]{:T(128)} %convert_element_type.3, () %tuple.18, bf16[128,256]{1,0:T(8,128)(2,1)S(1)} %get-tuple-element.39.refs_4_), branch_computations={%region_0.1_spmd, %region_1.2_spmd} | conditional | flops 196608 | bytes 1179776 | solution.py:319
  7.2 3.6 %collective-permute-start.2 = (bf16[128,256]{1,0:T(8,128)(2,1)S(1)}, bf16[128,256]{1,0:T(8,128)(2,1)S(1)}, u32[]{:S(2)}, u32[]{:S(2)}) collective-permute-start(bf16[128,256]{1,0:T(8,128)(2,1)S(1)} %param.1), channel_id=1, source_target_pairs={{0,6},{1,7},{2,4},{3,5},{4,2},{5,3},{6,0},{7,1},{8,14},{9,15},{10,... | collective-permute-start | bytes 196616 | tf_op jit(solution)/shard_map/cond/branch_1_fun/ppermute | solution.py:269
  10.8 0.0 collective-permute-start.1
  10.8 0.8 %collective-permute-start = (bf16[128,256]{1,0:T(8,128)(2,1)S(1)}, bf16[128,256]{1,0:T(8,128)(2,1)S(1)}, u32[]{:S(2)}, u32[]{:S(2)}) collective-permute-start(bf16[128,256]{1,0:T(8,128)(2,1)S(1)} %param.1), channel_id=1, source_target_pairs={{0,2},{1,3},{2,0},{3,1},{4,6},{5,7},{6,4},{7,5},{8,10},{9,11},{10,... | collective-permute-start | bytes 196616 | tf_op jit(solution)/shard_map/cond/branch_1_fun/ppermute | solution.py:269
  11.6 2.1 %collective-permute-done.2 = bf16[128,256]{1,0:T(8,128)(2,1)S(1)} collective-permute-done((bf16[128,256]{1,0:T(8,128)(2,1)S(1)}, bf16[128,256]{1,0:T(8,128)(2,1)S(1)}, u32[]{:S(2)}, u32[]{:S(2)}) %collective-permute-start.2) | collective-permute-done | bytes 65568 | tf_op jit(solution)/shard_map/cond/branch_1_fun/ppermute | solution.py:269
  13.7 2.8 %collective-permute-done.1 = bf16[128,256]{1,0:T(8,128)(2,1)S(1)} collective-permute-done((bf16[128,256]{1,0:T(8,128)(2,1)S(1)}, bf16[128,256]{1,0:T(8,128)(2,1)S(1)}, u32[]{:S(2)}, u32[]{:S(2)}) %collective-permute-start.1) | collective-permute-done | bytes 65568 | tf_op jit(solution)/shard_map/cond/branch_1_fun/ppermute | solution.py:269
  16.5 0.0 collective-permute-done
  16.5 1.6 %collective-permute-start.6 = (bf16[1312,128]{1,0:T(8,128)(2,1)S(1)}, bf16[1312,128]{1,0:T(8,128)(2,1)S(1)}, u32[]{:S(2)}, u32[]{:S(2)}) collective-permute-start(bf16[1312,128]{1,0:T(8,128)(2,1)S(1)} %collective-permute-done.5), channel_id=1, source_target_pairs={{0,16},{8,24},{16,0},{24,8},{1,17},{9,25},{17,1},{25,9},{2,18},{10... | collective-permute-start | bytes 1007624 | tf_op jit(solution)/shard_map/ppermute | solution.py:269
  18.1 1.5 %collective-permute-start.8 = (bf16[3,128,256]{2,1,0:T(8,128)(2,1)S(1)}, bf16[3,128,256]{2,1,0:T(8,128)(2,1)S(1)}, u32[]{:S(2)}, u32[]{:S(2)}) collective-permute-start(bf16[3,128,256]{2,1,0:T(8,128)(2,1)S(1)} %get-tuple-element.59.refs_6_), channel_id=1, source_target_pairs={{0,1},{1,0},{2,3},{3,2},{4,5},{5,4},{6,7},{7,6},{8,9},{9,8},{10,11... | collective-permute-start | bytes 589832 | tf_op jit(solution)/shard_map/ppermute | solution.py:269
  19.6 0.5 %collective-permute-start.7 = (bf16[128,256]{1,0:T(8,128)(2,1)S(1)}, bf16[128,256]{1,0:T(8,128)(2,1)S(1)}, u32[]{:S(2)}, u32[]{:S(2)}) collective-permute-start(bf16[128,256]{1,0:T(8,128)(2,1)S(1)} %get-tuple-element.39.refs_4_), channel_id=1, source_target_pairs={{0,1},{1,0},{2,3},{3,2},{4,5},{5,4},{6,7},{7,6},{8,9},{9,8},{10,11... | collective-permute-start | bytes 196616 | tf_op jit(solution)/shard_map/ppermute | solution.py:269
  20.1 0.1 pad_add_fusion.info
  20.2 5.5 %collective-permute-done.7.refs_5_ = bf16[128,256]{1,0:T(8,128)(2,1)S(1)} collective-permute-done((bf16[128,256]{1,0:T(8,128)(2,1)S(1)}, bf16[128,256]{1,0:T(8,128)(2,1)S(1)}, u32[]{:S(2)}, u32[]{:S(2)}) %collective-permute-start.7) | collective-permute-done | bytes 65568 | tf_op jit(solution)/shard_map/ppermute | solution.py:269
  25.7 0.0 collective-permute-done.3.refs_1_
  25.7 0.0 collective-permute-done.4.refs_2_
  25.7 0.0 collective-permute-done.8.refs_7_
  25.7 0.4 collective-permute-done.6.refs_3_
  26.1 0.0 copy-done
  26.1 3.7 %shard_map.86 = (bf16[2,128,256]{2,1,0:T(8,128)(2,1)S(1)}, bf16[2,128,256]{2,1,0:T(8,128)(2,1)S(1)}, bf16[2,128,256]{2,1,0:T(8,128)(2,1)S(1)}, bf16[2,128,256]{2...) custom-call(s32[2]{0:T(128)S(1)} %pad_add_fusion.info, ...), custom_call_target="tpu_custom_call" | custom-call | tf_op jit(solution)/shard_map/pallas_call | solution.py:325
  29.8 0.1 collective-permute-start.11
  29.9 1.6 %collective-permute-start.9 = (bf16[2,128,256]{2,1,0:T(8,128)(2,1)S(1)}, bf16[2,128,256]{2,1,0:T(8,128)(2,1)S(1)}, u32[]{:S(2)}, u32[]{:S(2)}) collective-permute-start(bf16[2,128,256]{2,1,0:T(8,128)(2,1)S(1)} %get-tuple-element.41), channel_id=1, source_target_pairs={{0,1},{1,0},{2,3},{3,2},{4,5},{5,4},{6,7},{7,6},{8,9},{9,8},{10,11... | collective-permute-start | bytes 393224 | tf_op jit(solution)/shard_map/ppermute | solution.py:269
  31.5 0.5 %collective-permute-start.15 = (bf16[2,128,256]{2,1,0:T(8,128)(2,1)S(1)}, bf16[2,128,256]{2,1,0:T(8,128)(2,1)S(1)}, u32[]{:S(2)}, u32[]{:S(2)}) collective-permute-start(bf16[2,128,256]{2,1,0:T(8,128)(2,1)S(1)} %get-tuple-element.54), channel_id=1, source_target_pairs={{0,1},{1,0},{2,3},{3,2},{4,5},{5,4},{6,7},{7,6},{8,9},{9,8},{10,11... | collective-permute-start | bytes 393224 | tf_op jit(solution)/shard_map/ppermute | solution.py:269
  32.0 0.0 collective-permute-done.11.refs_1_
  32.0 1.5 %collective-permute-start.12 = (bf16[640,128]{1,0:T(8,128)(2,1)S(1)}, bf16[640,128]{1,0:T(8,128)(2,1)S(1)}, u32[]{:S(2)}, u32[]{:S(2)}) collective-permute-start(bf16[640,128]{1,0:T(8,128)(2,1)S(1)} %get-tuple-element.48), channel_id=1, source_target_pairs={{0,16},{8,24},{16,0},{24,8},{1,17},{9,25},{17,1},{25,9},{2,18},{10... | collective-permute-start | bytes 491528 | tf_op jit(solution)/shard_map/ppermute | solution.py:269
  33.5 0.0 collective-permute-start.13
  33.5 2.8 %collective-permute-done.9.theirs = bf16[2,128,256]{2,1,0:T(8,128)(2,1)S(1)} collective-permute-done((bf16[2,128,256]{2,1,0:T(8,128)(2,1)S(1)}, bf16[2,128,256]{2,1,0:T(8,128)(2,1)S(1)}, u32[]{:S(2)}, u32[]{:S(2)}) %collective-permute-start.9) | collective-permute-done | bytes 131104 | tf_op jit(solution)/shard_map/ppermute | solution.py:269
  36.3 1.3 %collective-permute-start.10 = (bf16[128,256]{1,0:T(8,128)(2,1)S(1)}, bf16[128,256]{1,0:T(8,128)(2,1)S(1)}, u32[]{:S(2)}, u32[]{:S(2)}) collective-permute-start(bf16[128,256]{1,0:T(8,128)(2,1)S(1)} %get-tuple-element.42), channel_id=1, source_target_pairs={{6,0},{7,1},{14,8},{15,9},{22,16},{23,17},{30,24},{31,25}} | collective-permute-start | bytes 196616 | tf_op jit(solution)/shard_map/ppermute | solution.py:274
  37.6 1.3 %collective-permute-start.14 = (bf16[128,256]{1,0:T(8,128)(2,1)S(1)}, bf16[128,256]{1,0:T(8,128)(2,1)S(1)}, u32[]{:S(2)}, u32[]{:S(2)}) collective-permute-start(bf16[128,256]{1,0:T(8,128)(2,1)S(1)} %get-tuple-element.52), channel_id=1, source_target_pairs={{4,0},{5,1},{6,2},{7,3},{12,8},{13,9},{14,10},{15,11},{20,16},{21,... | collective-permute-start | bytes 196616 | tf_op jit(solution)/shard_map/ppermute | solution.py:274
  38.9 0.0 collective-permute-done.15.theirs
  39.0 1.3 %collective-permute-start.16 = (bf16[128,256]{1,0:T(8,128)(2,1)S(1)}, bf16[128,256]{1,0:T(8,128)(2,1)S(1)}, u32[]{:S(2)}, u32[]{:S(2)}) collective-permute-start(bf16[128,256]{1,0:T(8,128)(2,1)S(1)} %get-tuple-element.55), channel_id=1, source_target_pairs={{2,0},{3,1},{4,2},{5,3},{6,4},{7,5},{10,8},{11,9},{12,10},{13,11},... | collective-permute-start | bytes 196616 | tf_op jit(solution)/shard_map/ppermute | solution.py:274
  40.3 0.0 collective-permute-done.12.refs_2_
  40.3 0.2 collective-permute-done.13.refs_3_
  40.5 1.0 %shard_map.88 = bf16[128,2560]{1,0:T(8,128)(2,1)} custom-call(s32[1]{0:T(128)} %bitcast.5.place_ref, bf16[640,128]{1,0:T(8,128)(2,1)S(1)} %get-tuple-element.43.refs_0_, bf16[640,128]{1,0:T(8,128)(2,1)S(1)} %collective-permute-done.11.refs_1_, bf16[640,128]{1,0:T(8,128)(2,1)S(1)} %collective-permute-done.12.refs_2_, ...), custom_call_target="tpu_custom_call" | custom-call | tf_op jit(solution)/shard_map/pallas_call | solution.py:349
  41.4 5.1 %collective-permute-done.10.refs_0_ = bf16[128,256]{1,0:T(8,128)(2,1)S(1)} collective-permute-done((bf16[128,256]{1,0:T(8,128)(2,1)S(1)}, bf16[128,256]{1,0:T(8,128)(2,1)S(1)}, u32[]{:S(2)}, u32[]{:S(2)}) %collective-permute-start.10) | collective-permute-done | bytes 65568 | tf_op jit(solution)/shard_map/ppermute | solution.py:274
  46.5 1.1 %collective-permute-done.14.refs_1_ = bf16[128,256]{1,0:T(8,128)(2,1)S(1)} collective-permute-done((bf16[128,256]{1,0:T(8,128)(2,1)S(1)}, bf16[128,256]{1,0:T(8,128)(2,1)S(1)}, u32[]{:S(2)}, u32[]{:S(2)}) %collective-permute-start.14) | collective-permute-done | bytes 65568 | tf_op jit(solution)/shard_map/ppermute | solution.py:274
  47.6 0.0 collective-permute-done.16.refs_2_
  47.6 0.7 %shard_map.90 = (bf16[128,128]{1,0:T(8,128)(2,1)}, bf16[128,128]{1,0:T(8,128)(2,1)}) custom-call(bf16[128,256]{1,0:T(8,128)(2,1)S(1)} %collective-permute-done.10.refs_0_, bf16[128,256]{1,0:T(8,128)(2,1)S(1)} %collective-permute-done.14.refs_1_, bf16[128,256]{1,0:T(8,128)(2,1)S(1)} %collective-permute-done.16.refs_2_, ...), custom_call_target="tpu_custom_call" | custom-call | tf_op jit(solution)/shard_map/pallas_call | solution.py:355
  (3 shorter events, 0.1 us)
Async XLA Ops:
  3.6 22.5 %copy-start = (bf16[1312,128]{1,0:T(8,128)(2,1)S(1)}, bf16[1312,128]{1,0:T(8,128)(2,1)}, u32[]{:S(2)}) copy-start(bf16[1312,128]{1,0:T(8,128)(2,1)} %get-tuple-element.33.refs_0_) | copy-start | bytes 1007620
  3.6 3.5 %collective-permute-start.5 = (bf16[1312,128]{1,0:T(8,128)(2,1)}, bf16[1312,128]{1,0:T(8,128)(2,1)S(1)}, u32[]{:S(2)}, u32[]{:S(2)}) collective-permute-start(bf16[1312,128]{1,0:T(8,128)(2,1)} %get-tuple-element.36), channel_id=1, source_target_pairs={{0,8},{8,0},{16,24},{24,16},{1,9},{9,1},{17,25},{25,17},{2,10},{10... | collective-permute-start | bytes 1007624 | tf_op jit(solution)/shard_map/ppermute | solution.py:269
  4.2 21.6 %collective-permute-start.3 = (bf16[1312,128]{1,0:T(8,128)(2,1)}, bf16[1312,128]{1,0:T(8,128)(2,1)S(1)}, u32[]{:S(2)}, u32[]{:S(2)}) collective-permute-start(bf16[1312,128]{1,0:T(8,128)(2,1)} %get-tuple-element.34), channel_id=1, source_target_pairs={{0,8},{8,0},{16,24},{24,16},{1,9},{9,1},{17,25},{25,17},{2,10},{10... | collective-permute-start | bytes 1007624 | tf_op jit(solution)/shard_map/ppermute | solution.py:269
  4.2 21.5 %collective-permute-start.4 = (bf16[1312,128]{1,0:T(8,128)(2,1)}, bf16[1312,128]{1,0:T(8,128)(2,1)S(1)}, u32[]{:S(2)}, u32[]{:S(2)}) collective-permute-start(bf16[1312,128]{1,0:T(8,128)(2,1)} %get-tuple-element.35), channel_id=1, source_target_pairs={{0,16},{8,24},{16,0},{24,8},{1,17},{9,25},{17,1},{25,9},{2,18},{10... | collective-permute-start | bytes 1007624 | tf_op jit(solution)/shard_map/ppermute | solution.py:269
  7.2 6.5 %collective-permute-start.2 = (bf16[128,256]{1,0:T(8,128)(2,1)S(1)}, bf16[128,256]{1,0:T(8,128)(2,1)S(1)}, u32[]{:S(2)}, u32[]{:S(2)}) collective-permute-start(bf16[128,256]{1,0:T(8,128)(2,1)S(1)} %param.1), channel_id=1, source_target_pairs={{0,6},{1,7},{2,4},{3,5},{4,2},{5,3},{6,0},{7,1},{8,14},{9,15},{10,... | collective-permute-start | bytes 196616 | tf_op jit(solution)/shard_map/cond/branch_1_fun/ppermute | solution.py:269
  10.8 5.7 %collective-permute-start.1 = (bf16[128,256]{1,0:T(8,128)(2,1)S(1)}, bf16[128,256]{1,0:T(8,128)(2,1)S(1)}, u32[]{:S(2)}, u32[]{:S(2)}) collective-permute-start(bf16[128,256]{1,0:T(8,128)(2,1)S(1)} %param.1), channel_id=1, source_target_pairs={{0,4},{1,5},{2,6},{3,7},{4,0},{5,1},{6,2},{7,3},{8,12},{9,13},{10,... | collective-permute-start | bytes 196616 | tf_op jit(solution)/shard_map/cond/branch_1_fun/ppermute | solution.py:269
  10.8 5.7 %collective-permute-start = (bf16[128,256]{1,0:T(8,128)(2,1)S(1)}, bf16[128,256]{1,0:T(8,128)(2,1)S(1)}, u32[]{:S(2)}, u32[]{:S(2)}) collective-permute-start(bf16[128,256]{1,0:T(8,128)(2,1)S(1)} %param.1), channel_id=1, source_target_pairs={{0,2},{1,3},{2,0},{3,1},{4,6},{5,7},{6,4},{7,5},{8,10},{9,11},{10,... | collective-permute-start | bytes 196616 | tf_op jit(solution)/shard_map/cond/branch_1_fun/ppermute | solution.py:269
  16.5 9.6 %collective-permute-start.6 = (bf16[1312,128]{1,0:T(8,128)(2,1)S(1)}, bf16[1312,128]{1,0:T(8,128)(2,1)S(1)}, u32[]{:S(2)}, u32[]{:S(2)}) collective-permute-start(bf16[1312,128]{1,0:T(8,128)(2,1)S(1)} %collective-permute-done.5), channel_id=1, source_target_pairs={{0,16},{8,24},{16,0},{24,8},{1,17},{9,25},{17,1},{25,9},{2,18},{10... | collective-permute-start | bytes 1007624 | tf_op jit(solution)/shard_map/ppermute | solution.py:269
  18.1 7.6 %collective-permute-start.8 = (bf16[3,128,256]{2,1,0:T(8,128)(2,1)S(1)}, bf16[3,128,256]{2,1,0:T(8,128)(2,1)S(1)}, u32[]{:S(2)}, u32[]{:S(2)}) collective-permute-start(bf16[3,128,256]{2,1,0:T(8,128)(2,1)S(1)} %get-tuple-element.59.refs_6_), channel_id=1, source_target_pairs={{0,1},{1,0},{2,3},{3,2},{4,5},{5,4},{6,7},{7,6},{8,9},{9,8},{10,11... | collective-permute-start | bytes 589832 | tf_op jit(solution)/shard_map/ppermute | solution.py:269
  19.6 6.1 %collective-permute-start.7 = (bf16[128,256]{1,0:T(8,128)(2,1)S(1)}, bf16[128,256]{1,0:T(8,128)(2,1)S(1)}, u32[]{:S(2)}, u32[]{:S(2)}) collective-permute-start(bf16[128,256]{1,0:T(8,128)(2,1)S(1)} %get-tuple-element.39.refs_4_), channel_id=1, source_target_pairs={{0,1},{1,0},{2,3},{3,2},{4,5},{5,4},{6,7},{7,6},{8,9},{9,8},{10,11... | collective-permute-start | bytes 196616 | tf_op jit(solution)/shard_map/ppermute | solution.py:269
  29.8 2.2 %collective-permute-start.11 = (bf16[640,128]{1,0:T(8,128)(2,1)S(1)}, bf16[640,128]{1,0:T(8,128)(2,1)S(1)}, u32[]{:S(2)}, u32[]{:S(2)}) collective-permute-start(bf16[640,128]{1,0:T(8,128)(2,1)S(1)} %get-tuple-element.44), channel_id=1, source_target_pairs={{0,8},{8,0},{16,24},{24,16},{1,9},{9,1},{17,25},{25,17},{2,10},{10... | collective-permute-start | bytes 491528 | tf_op jit(solution)/shard_map/ppermute | solution.py:269
  29.9 6.4 %collective-permute-start.9 = (bf16[2,128,256]{2,1,0:T(8,128)(2,1)S(1)}, bf16[2,128,256]{2,1,0:T(8,128)(2,1)S(1)}, u32[]{:S(2)}, u32[]{:S(2)}) collective-permute-start(bf16[2,128,256]{2,1,0:T(8,128)(2,1)S(1)} %get-tuple-element.41), channel_id=1, source_target_pairs={{0,1},{1,0},{2,3},{3,2},{4,5},{5,4},{6,7},{7,6},{8,9},{9,8},{10,11... | collective-permute-start | bytes 393224 | tf_op jit(solution)/shard_map/ppermute | solution.py:269
  31.5 7.4 %collective-permute-start.15 = (bf16[2,128,256]{2,1,0:T(8,128)(2,1)S(1)}, bf16[2,128,256]{2,1,0:T(8,128)(2,1)S(1)}, u32[]{:S(2)}, u32[]{:S(2)}) collective-permute-start(bf16[2,128,256]{2,1,0:T(8,128)(2,1)S(1)} %get-tuple-element.54), channel_id=1, source_target_pairs={{0,1},{1,0},{2,3},{3,2},{4,5},{5,4},{6,7},{7,6},{8,9},{9,8},{10,11... | collective-permute-start | bytes 393224 | tf_op jit(solution)/shard_map/ppermute | solution.py:269
  32.0 8.3 %collective-permute-start.12 = (bf16[640,128]{1,0:T(8,128)(2,1)S(1)}, bf16[640,128]{1,0:T(8,128)(2,1)S(1)}, u32[]{:S(2)}, u32[]{:S(2)}) collective-permute-start(bf16[640,128]{1,0:T(8,128)(2,1)S(1)} %get-tuple-element.48), channel_id=1, source_target_pairs={{0,16},{8,24},{16,0},{24,8},{1,17},{9,25},{17,1},{25,9},{2,18},{10... | collective-permute-start | bytes 491528 | tf_op jit(solution)/shard_map/ppermute | solution.py:269
  33.5 7.0 %collective-permute-start.13 = (bf16[640,128]{1,0:T(8,128)(2,1)S(1)}, bf16[640,128]{1,0:T(8,128)(2,1)S(1)}, u32[]{:S(2)}, u32[]{:S(2)}) collective-permute-start(bf16[640,128]{1,0:T(8,128)(2,1)S(1)} %get-tuple-element.49), channel_id=1, source_target_pairs={{0,24},{8,16},{16,8},{24,0},{1,25},{9,17},{17,9},{25,1},{2,26},{10... | collective-permute-start | bytes 491528 | tf_op jit(solution)/shard_map/ppermute | solution.py:269
  36.3 10.2 %collective-permute-start.10 = (bf16[128,256]{1,0:T(8,128)(2,1)S(1)}, bf16[128,256]{1,0:T(8,128)(2,1)S(1)}, u32[]{:S(2)}, u32[]{:S(2)}) collective-permute-start(bf16[128,256]{1,0:T(8,128)(2,1)S(1)} %get-tuple-element.42), channel_id=1, source_target_pairs={{6,0},{7,1},{14,8},{15,9},{22,16},{23,17},{30,24},{31,25}} | collective-permute-start | bytes 196616 | tf_op jit(solution)/shard_map/ppermute | solution.py:274
  37.6 10.0 %collective-permute-start.14 = (bf16[128,256]{1,0:T(8,128)(2,1)S(1)}, bf16[128,256]{1,0:T(8,128)(2,1)S(1)}, u32[]{:S(2)}, u32[]{:S(2)}) collective-permute-start(bf16[128,256]{1,0:T(8,128)(2,1)S(1)} %get-tuple-element.52), channel_id=1, source_target_pairs={{4,0},{5,1},{6,2},{7,3},{12,8},{13,9},{14,10},{15,11},{20,16},{21,... | collective-permute-start | bytes 196616 | tf_op jit(solution)/shard_map/ppermute | solution.py:274
  39.0 8.7 %collective-permute-start.16 = (bf16[128,256]{1,0:T(8,128)(2,1)S(1)}, bf16[128,256]{1,0:T(8,128)(2,1)S(1)}, u32[]{:S(2)}, u32[]{:S(2)}) collective-permute-start(bf16[128,256]{1,0:T(8,128)(2,1)S(1)} %get-tuple-element.55), channel_id=1, source_target_pairs={{2,0},{3,1},{4,2},{5,3},{6,4},{7,5},{10,8},{11,9},{12,10},{13,11},... | collective-permute-start | bytes 196616 | tf_op jit(solution)/shard_map/ppermute | solution.py:274

commit v5 on v4

--- a/solution.py
+++ b/solution.py
@@ -14,7 +14,6 @@
 VMEM_LIMIT = 32 * 1024 * 1024
 PACK_LIMIT = 62 * 1024 * 1024
 LOG2E = math.log2(math.e)
-SMEM = pl.BlockSpec(memory_space=pltpu.SMEM)
 VMEM = pl.BlockSpec(memory_space=pltpu.VMEM)
 HBM = pl.BlockSpec(memory_space=pltpu.HBM)
 
@@ -23,17 +22,18 @@
     return -(-rows // 16) * 16
 
 
-def pack_kernel(heads, head, which, cached, after, place_ref, queries, grads, saved, totals, *refs):
+def pack_kernel(heads, head, which, cached, after, queries, grads, saved, totals, *refs):
     cache, refs = refs[:cached], refs[cached + after :]
     outs, refs = refs[: len(which)], refs[len(which) :]
     block, refs = (refs[0], refs[1:]) if cached else (None, refs)
     here, totals_here, ready, sems = refs
     rows = queries.shape[0]
+    here_at = lax.axis_index("section")
     width = heads * head
     groups = queries.shape[1] // width
     ends = []
     for m, k in enumerate(which):
-        columns = pl.ds(pl.multiple_of((place_ref[0] ^ k) * width, 128), width)
+        columns = pl.ds(pl.multiple_of((here_at ^ k) * width, 128), width)
         for i, source in enumerate((grads, saved, queries)):
             ends.append((source.at[:, columns], here.at[m, i]))
     ends.append((totals, totals_here))
@@ -70,7 +70,7 @@
         chosen = totals_here[0:heads, :].astype(jnp.float32)
         for group in range(1, groups):
             part = totals_here[group * heads : (group + 1) * heads, :].astype(jnp.float32)
-            chosen = jnp.where((place_ref[0] ^ k) == group, part, chosen)
+            chosen = jnp.where((here_at ^ k) == group, part, chosen)
         spare = jnp.zeros((message.shape[0] - 2 * heads * rows - EXTRA * heads, 128), jnp.float32)
         extra = jnp.concatenate([chosen, high, middle, low, spare], axis=0)
         message[2 * heads * rows :, :] = extra.astype(jnp.bfloat16)
@@ -79,7 +79,7 @@
         copy.wait()
 
 
-def attend_kernel(layers, heads, head, outer, inv_root, info, *refs):
+def attend_kernel(layers, heads, head, outer, inv_root, *refs):
     messages = refs[:layers]
     own, own_swapped, further, others = refs[layers : layers + 4]
     refs = refs[layers + 4 :]
@@ -88,7 +88,8 @@
     keys, values, query_turned, grad_turned, totals, dots, weights_all, score_all, *refs = refs
     rows = own.shape[0]
     pair = 2 * rows
-    z, x = info[0], info[1]
+    at_seq = lax.axis_index("seq")
+    z, x = at_seq // 2, at_seq % 2
     near = outer // 2
     per_layer = heads * rows
     every = layers * per_layer
@@ -146,13 +147,15 @@
             if turned is not None:
                 turned[columns, here] = jnp.transpose(score_grads)
 
-    def leave(j, key_sum, value_sum):
+    def leave(step, key_sum, value_sum):
         both = [jnp.transpose(total.astype(jnp.bfloat16)) for total in (key_sum, value_sum)]
-        step = z - j
         for half in range(2):
             chosen = jnp.concatenate(
                 [jnp.where(x == half, total[:rows], total[rows:]) for total in both], axis=1
             )
+            if isinstance(step, int):
+                halves[2 * half + (step >= near)][step - near * (step >= near)] = chosen
+                continue
 
             @pl.when(step < near)
             def _():
@@ -170,7 +173,7 @@
             score_all[:, here], keys[pl.ds(at, pair), :], preferred_element_type=jnp.float32
         )
         leave(
-            j,
+            z - j,
             jnp.dot(query_turned[...], score_all[:, here], preferred_element_type=jnp.float32),
             jnp.dot(grad_turned[...], weights_all[:, here], preferred_element_type=jnp.float32),
         )
@@ -199,7 +202,7 @@
         value_sum = jnp.dot(grad_turned[...], weights_all[...], preferred_element_type=jnp.float32)
         for j in range(outer):
             here = slice(j * pair, (j + 1) * pair)
-            leave(j, key_sum[:, here], value_sum[:, here])
+            leave(outer - 1 - j, key_sum[:, here], value_sum[:, here])
         key_turned = jnp.transpose(keys[...])
         for layer in range(layers):
             there = slice(layer * per_layer, (layer + 1) * per_layer)
@@ -233,11 +236,12 @@
         )
 
 
-def place_kernel(heads, head, place_ref, *refs):
+def place_kernel(heads, head, *refs):
     messages, out = refs[:-1], refs[-1]
     rows = out.shape[0]
+    here_at = lax.axis_index("section")
     for k, message in enumerate(messages):
-        start = pl.multiple_of((place_ref[0] ^ k) * heads * head, 128)
+        start = pl.multiple_of((here_at ^ k) * heads * head, 128)
         for h in range(heads):
             at = pl.multiple_of(start + h * head, 128)
             out[:, pl.ds(at, head)] = message[h * rows : (h + 1) * rows, :]
@@ -280,12 +284,10 @@
     sections = lax.axis_size("section")
     seq = lax.axis_size("seq")
     outer = seq // 2
-    section_at = lax.axis_index("section").astype(jnp.int32).reshape(1)
     seq_at = lax.axis_index("seq").astype(jnp.int32)
     rows, head = cache_keys.shape
     heads = log_sums.shape[2] // sections
     inv_root = 1.0 / math.sqrt(head)
-    info = jnp.stack([seq_at // 2, seq_at % 2])
     lines = 2 * heads * rows + up16(EXTRA * heads)
 
     totals = jnp.transpose(log_sums[0])
@@ -294,7 +296,7 @@
     *sent, own = call(
         functools.partial(pack_kernel, heads, head, tuple(range(sections)), 2, 0),
         [(lines, 128)] * sections + [(rows, 2 * head)],
-        [SMEM] + [HBM] * 6,
+        [HBM] * 6,
         [
             pltpu.VMEM((sections, 3, rows, heads * head), jnp.bfloat16),
             pltpu.VMEM(totals.shape, jnp.bfloat16),
@@ -303,7 +305,7 @@
         ],
         limit=PACK_LIMIT,
         out_specs=[HBM] * (sections + 1),
-    )(section_at, queries[0], out_grads[0], saved_out[0], totals, cache_keys, cache_values)
+    )(queries[0], out_grads[0], saved_out[0], totals, cache_keys, cache_values)
     passed = swap(sent[half + 1], "section", 1)
     messages = [sent[0], swap(sent[1], "section", 1), swap(sent[half], "section", half)]
     passed, tied = lax.optimization_barrier((passed, own))
@@ -326,14 +328,14 @@
         functools.partial(attend_kernel, sections, heads, head, outer, inv_root),
         [(outer // 2, rows, 2 * head), (outer - outer // 2, rows, 2 * head)] * 2
         + [(heads * rows, head)] * sections,
-        [SMEM] + [VMEM] * (sections + 4),
+        [VMEM] * (sections + 4),
         [bf16((seq * rows, head))] * 2
         + [bf16((head, every))] * 2
         + [pltpu.VMEM((every, 128), jnp.float32)] * 2
         + [bf16((every, across))] * 2
         + [pltpu.VMEM((every, head), jnp.float32)]
         + ([bf16((across, every))] if outer <= UNROLLED else []),
-    )(info, *messages, *blocks_here)
+    )(*messages, *blocks_here)
 
     def reduced(mine, theirs):
         count = mine.shape[0]
@@ -349,8 +351,8 @@
     (query_grads,) = call(
         functools.partial(place_kernel, heads, head),
         [queries.shape[1:]],
-        [SMEM] + [VMEM] * sections,
-    )(section_at, *back)
+        [VMEM] * sections,
+    )(*back)
     blocks[0], query_grads = lax.optimization_barrier((blocks[0], query_grads))
     key_grads, value_grads = call(total_kernel, [(rows, head)] * 2, [VMEM] * outer)(*blocks)
     return (query_grads[None], key_grads, value_grads)

time: 48.5 us -> 47.4 us (0.977)
  Pallas kernels: 8.36 us -> 7.82 us
  waiting for transfers between devices: 20 us -> 19.5 us
    ppermute x3, waiting for transfers between devices: 6.19 us -> 5.61 us  [move(): lax.ppermute(array, 'seq', [(i, i + step) for i in range(size) if 0 <= i...]
    pallas_call x1, Pallas kernels: 3.71 us -> 3.15 us  [local(): call(functools.partial(attend_kernel, sections, heads, head, outer, inv_r...]
where the time goes in v5:
time: 47.4 us; the launch traced here: 47.2 us
  waiting for transfers between devices  19.5 us (41%)
  starting transfers between devices  19 us (40%)
  Pallas kernels  7.82 us (16%)
  between operations  0.73 us (2%)
    ppermute x14, starting transfers between devices, swap(): return lax.ppermute(array, axis, [(i, i ^ bits) for i in range(size)])  15.2 us
    ppermute x14, waiting for transfers between devices, swap(): return lax.ppermute(array, axis, [(i, i ^ bits) for i in range(size)])  13.9 us
    ppermute x3, waiting for transfers between devices, move(): lax.ppermute(array, 'seq', [(i, i + step) for i in range(size) if 0 <= i...  5.61 us
    ppermute x3, starting transfers between devices, move(): lax.ppermute(array, 'seq', [(i, i + step) for i in range(size) if 0 <= i...  3.88 us
    pallas_call x1, Pallas kernels, local(): call(functools.partial(attend_kernel, sections, heads, head, outer, inv_r...  3.15 us
    pallas_call x1, Pallas kernels, local(): call(functools.partial(pack_kernel, heads, head, tuple(range(sections)),...  2.98 us
    pallas_call x1, Pallas kernels, local(): call(functools.partial(place_kernel, heads, head), [queries.shape[1:]], [...  0.96 us
  transfers between devices with their start and end apart: 17, of which 8 were waited for; matrix products, arithmetic and copies ran while one was open for 0% of the time, Pallas kernels for 2%

profile of v5, /device:TPU:0, one launch (start us, length us, event | category | flops | bytes accessed | tf_op | source)
XLA Modules:
  0.0 47.2 jit_solution(10440353376525935419)
XLA Ops:
  0.6 3.0 %shard_map.85 = (bf16[1312,128]{1,0:T(8,128)(2,1)}, bf16[1312,128]{1,0:T(8,128)(2,1)}, bf16[1312,128]{1,0:T(8,128)(2,1)}, bf16[1312,128]{1,0:T(8,128)(2,1)}, bf16[128,256]{1,0:T(8,128)(2,1)S(1)}) custom-call(bf16[128,2560]{1,0:T(8,128)(2,1)} %bitcast.10, bf16[128,2560]{1,0:T(8,128)(2,1)} %bitcast.11, bf16[128,2560]{1,0:T(8,128)(2,1)} %bitcast.12, ...), custom_call_target="tpu_custom_call" | custom-call | tf_op jit(solution)/shard_map/pallas_call | solution.py:296
  3.6 0.0 copy-start
  3.6 0.5 %collective-permute-start.5 = (bf16[1312,128]{1,0:T(8,128)(2,1)}, bf16[1312,128]{1,0:T(8,128)(2,1)S(1)}, u32[]{:S(2)}, u32[]{:S(2)}) collective-permute-start(bf16[1312,128]{1,0:T(8,128)(2,1)} %get-tuple-element.36), channel_id=1, source_target_pairs={{0,8},{8,0},{16,24},{24,16},{1,9},{9,1},{17,25},{25,17},{2,10},{10... | collective-permute-start | bytes 1007624 | tf_op jit(solution)/shard_map/ppermute | solution.py:273
  4.2 0.1 collective-permute-start.3
  4.2 2.9 %collective-permute-start.4 = (bf16[1312,128]{1,0:T(8,128)(2,1)}, bf16[1312,128]{1,0:T(8,128)(2,1)S(1)}, u32[]{:S(2)}, u32[]{:S(2)}) collective-permute-start(bf16[1312,128]{1,0:T(8,128)(2,1)} %get-tuple-element.35), channel_id=1, source_target_pairs={{0,16},{8,24},{16,0},{24,8},{1,17},{9,25},{17,1},{25,9},{2,18},{10... | collective-permute-start | bytes 1007624 | tf_op jit(solution)/shard_map/ppermute | solution.py:273
  7.2 0.0 collective-permute-done.5
  7.2 9.4 %conditional.1 = (bf16[3,128,256]{2,1,0:T(8,128)(2,1)S(1)}) conditional(s32[]{:T(128)} %convert_element_type.3, () %tuple.18, bf16[128,256]{1,0:T(8,128)(2,1)S(1)} %get-tuple-element.39.refs_4_), branch_computations={%region_0.0_spmd, %region_1.0_spmd} | conditional | flops 196608 | bytes 1179776 | solution.py:321
  7.2 3.6 %collective-permute-start.2 = (bf16[128,256]{1,0:T(8,128)(2,1)S(1)}, bf16[128,256]{1,0:T(8,128)(2,1)S(1)}, u32[]{:S(2)}, u32[]{:S(2)}) collective-permute-start(bf16[128,256]{1,0:T(8,128)(2,1)S(1)} %param.1), channel_id=1, source_target_pairs={{0,6},{1,7},{2,4},{3,5},{4,2},{5,3},{6,0},{7,1},{8,14},{9,15},{10,... | collective-permute-start | bytes 196616 | tf_op jit(solution)/shard_map/cond/branch_1_fun/ppermute | solution.py:273
  10.8 0.0 collective-permute-start.1
  10.8 0.8 %collective-permute-start = (bf16[128,256]{1,0:T(8,128)(2,1)S(1)}, bf16[128,256]{1,0:T(8,128)(2,1)S(1)}, u32[]{:S(2)}, u32[]{:S(2)}) collective-permute-start(bf16[128,256]{1,0:T(8,128)(2,1)S(1)} %param.1), channel_id=1, source_target_pairs={{0,2},{1,3},{2,0},{3,1},{4,6},{5,7},{6,4},{7,5},{8,10},{9,11},{10,... | collective-permute-start | bytes 196616 | tf_op jit(solution)/shard_map/cond/branch_1_fun/ppermute | solution.py:273
  11.6 2.1 %collective-permute-done.2 = bf16[128,256]{1,0:T(8,128)(2,1)S(1)} collective-permute-done((bf16[128,256]{1,0:T(8,128)(2,1)S(1)}, bf16[128,256]{1,0:T(8,128)(2,1)S(1)}, u32[]{:S(2)}, u32[]{:S(2)}) %collective-permute-start.2) | collective-permute-done | bytes 65568 | tf_op jit(solution)/shard_map/cond/branch_1_fun/ppermute | solution.py:273
  13.7 2.8 %collective-permute-done.1 = bf16[128,256]{1,0:T(8,128)(2,1)S(1)} collective-permute-done((bf16[128,256]{1,0:T(8,128)(2,1)S(1)}, bf16[128,256]{1,0:T(8,128)(2,1)S(1)}, u32[]{:S(2)}, u32[]{:S(2)}) %collective-permute-start.1) | collective-permute-done | bytes 65568 | tf_op jit(solution)/shard_map/cond/branch_1_fun/ppermute | solution.py:273
  16.5 0.0 collective-permute-done
  16.5 1.6 %collective-permute-start.6 = (bf16[1312,128]{1,0:T(8,128)(2,1)S(1)}, bf16[1312,128]{1,0:T(8,128)(2,1)S(1)}, u32[]{:S(2)}, u32[]{:S(2)}) collective-permute-start(bf16[1312,128]{1,0:T(8,128)(2,1)S(1)} %collective-permute-done.5), channel_id=1, source_target_pairs={{0,16},{8,24},{16,0},{24,8},{1,17},{9,25},{17,1},{25,9},{2,18},{10... | collective-permute-start | bytes 1007624 | tf_op jit(solution)/shard_map/ppermute | solution.py:273
  18.1 1.5 %collective-permute-start.8 = (bf16[3,128,256]{2,1,0:T(8,128)(2,1)S(1)}, bf16[3,128,256]{2,1,0:T(8,128)(2,1)S(1)}, u32[]{:S(2)}, u32[]{:S(2)}) collective-permute-start(bf16[3,128,256]{2,1,0:T(8,128)(2,1)S(1)} %get-tuple-element.59.refs_6_), channel_id=1, source_target_pairs={{0,1},{1,0},{2,3},{3,2},{4,5},{5,4},{6,7},{7,6},{8,9},{9,8},{10,11... | collective-permute-start | bytes 589832 | tf_op jit(solution)/shard_map/ppermute | solution.py:273
  19.6 0.5 %collective-permute-start.7 = (bf16[128,256]{1,0:T(8,128)(2,1)S(1)}, bf16[128,256]{1,0:T(8,128)(2,1)S(1)}, u32[]{:S(2)}, u32[]{:S(2)}) collective-permute-start(bf16[128,256]{1,0:T(8,128)(2,1)S(1)} %get-tuple-element.39.refs_4_), channel_id=1, source_target_pairs={{0,1},{1,0},{2,3},{3,2},{4,5},{5,4},{6,7},{7,6},{8,9},{9,8},{10,11... | collective-permute-start | bytes 196616 | tf_op jit(solution)/shard_map/ppermute | solution.py:273
  20.1 5.6 %collective-permute-done.7.refs_5_ = bf16[128,256]{1,0:T(8,128)(2,1)S(1)} collective-permute-done((bf16[128,256]{1,0:T(8,128)(2,1)S(1)}, bf16[128,256]{1,0:T(8,128)(2,1)S(1)}, u32[]{:S(2)}, u32[]{:S(2)}) %collective-permute-start.7) | collective-permute-done | bytes 65568 | tf_op jit(solution)/shard_map/ppermute | solution.py:273
  25.7 0.0 collective-permute-done.3.refs_1_
  25.7 0.0 collective-permute-done.4.refs_2_
  25.7 0.0 collective-permute-done.8.refs_7_
  25.7 0.4 collective-permute-done.6.refs_3_
  26.1 0.0 copy-done
  26.1 3.2 %shard_map.86 = (bf16[2,128,256]{2,1,0:T(8,128)(2,1)S(1)}, bf16[2,128,256]{2,1,0:T(8,128)(2,1)S(1)}, bf16[2,128,256]{2,1,0:T(8,128)(2,1)S(1)}, bf16[2,128,256]{2...) custom-call(bf16[1312,128]{1,0:T(8,128)(2,1)S(1)} %copy-done, ...), custom_call_target="tpu_custom_call" | custom-call | tf_op jit(solution)/shard_map/pallas_call | solution.py:327
  29.3 0.1 collective-permute-start.11
  29.3 1.6 %collective-permute-start.9 = (bf16[2,128,256]{2,1,0:T(8,128)(2,1)S(1)}, bf16[2,128,256]{2,1,0:T(8,128)(2,1)S(1)}, u32[]{:S(2)}, u32[]{:S(2)}) collective-permute-start(bf16[2,128,256]{2,1,0:T(8,128)(2,1)S(1)} %get-tuple-element.41), channel_id=1, source_target_pairs={{0,1},{1,0},{2,3},{3,2},{4,5},{5,4},{6,7},{7,6},{8,9},{9,8},{10,11... | collective-permute-start | bytes 393224 | tf_op jit(solution)/shard_map/ppermute | solution.py:273
  30.9 0.5 %collective-permute-start.15 = (bf16[2,128,256]{2,1,0:T(8,128)(2,1)S(1)}, bf16[2,128,256]{2,1,0:T(8,128)(2,1)S(1)}, u32[]{:S(2)}, u32[]{:S(2)}) collective-permute-start(bf16[2,128,256]{2,1,0:T(8,128)(2,1)S(1)} %get-tuple-element.54), channel_id=1, source_target_pairs={{0,1},{1,0},{2,3},{3,2},{4,5},{5,4},{6,7},{7,6},{8,9},{9,8},{10,11... | collective-permute-start | bytes 393224 | tf_op jit(solution)/shard_map/ppermute | solution.py:273
  31.4 0.0 collective-permute-done.11.refs_1_
  31.4 1.5 %collective-permute-start.12 = (bf16[640,128]{1,0:T(8,128)(2,1)S(1)}, bf16[640,128]{1,0:T(8,128)(2,1)S(1)}, u32[]{:S(2)}, u32[]{:S(2)}) collective-permute-start(bf16[640,128]{1,0:T(8,128)(2,1)S(1)} %get-tuple-element.48), channel_id=1, source_target_pairs={{0,16},{8,24},{16,0},{24,8},{1,17},{9,25},{17,1},{25,9},{2,18},{10... | collective-permute-start | bytes 491528 | tf_op jit(solution)/shard_map/ppermute | solution.py:273
  32.9 0.0 collective-permute-start.13
  32.9 2.8 %collective-permute-done.9.theirs = bf16[2,128,256]{2,1,0:T(8,128)(2,1)S(1)} collective-permute-done((bf16[2,128,256]{2,1,0:T(8,128)(2,1)S(1)}, bf16[2,128,256]{2,1,0:T(8,128)(2,1)S(1)}, u32[]{:S(2)}, u32[]{:S(2)}) %collective-permute-start.9) | collective-permute-done | bytes 131104 | tf_op jit(solution)/shard_map/ppermute | solution.py:273
  35.7 1.3 %collective-permute-start.10 = (bf16[128,256]{1,0:T(8,128)(2,1)S(1)}, bf16[128,256]{1,0:T(8,128)(2,1)S(1)}, u32[]{:S(2)}, u32[]{:S(2)}) collective-permute-start(bf16[128,256]{1,0:T(8,128)(2,1)S(1)} %get-tuple-element.42), channel_id=1, source_target_pairs={{6,0},{7,1},{14,8},{15,9},{22,16},{23,17},{30,24},{31,25}} | collective-permute-start | bytes 196616 | tf_op jit(solution)/shard_map/ppermute | solution.py:278
  37.0 1.3 %collective-permute-start.14 = (bf16[128,256]{1,0:T(8,128)(2,1)S(1)}, bf16[128,256]{1,0:T(8,128)(2,1)S(1)}, u32[]{:S(2)}, u32[]{:S(2)}) collective-permute-start(bf16[128,256]{1,0:T(8,128)(2,1)S(1)} %get-tuple-element.52), channel_id=1, source_target_pairs={{4,0},{5,1},{6,2},{7,3},{12,8},{13,9},{14,10},{15,11},{20,16},{21,... | collective-permute-start | bytes 196616 | tf_op jit(solution)/shard_map/ppermute | solution.py:278
  38.3 0.0 collective-permute-done.15.theirs
  38.4 1.3 %collective-permute-start.16 = (bf16[128,256]{1,0:T(8,128)(2,1)S(1)}, bf16[128,256]{1,0:T(8,128)(2,1)S(1)}, u32[]{:S(2)}, u32[]{:S(2)}) collective-permute-start(bf16[128,256]{1,0:T(8,128)(2,1)S(1)} %get-tuple-element.55), channel_id=1, source_target_pairs={{2,0},{3,1},{4,2},{5,3},{6,4},{7,5},{10,8},{11,9},{12,10},{13,11},... | collective-permute-start | bytes 196616 | tf_op jit(solution)/shard_map/ppermute | solution.py:278
  39.7 0.0 collective-permute-done.12.refs_2_
  39.7 0.2 collective-permute-done.13.refs_3_
  39.9 1.0 %shard_map.88 = bf16[128,2560]{1,0:T(8,128)(2,1)} custom-call(bf16[640,128]{1,0:T(8,128)(2,1)S(1)} %get-tuple-element.43.refs_0_, bf16[640,128]{1,0:T(8,128)(2,1)S(1)} %collective-permute-done.11.refs_1_, bf16[640,128]{1,0:T(8,128)(2,1)S(1)} %collective-permute-done.12.refs_2_, bf16[640,128]{1,0:T(8,128)(2,1)S(1)} %collective-permute-done.13.refs_3_), custom_call_target="tpu_custom_call" | custom-call | tf_op jit(solution)/shard_map/pallas_call | solution.py:351
  40.9 4.8 %collective-permute-done.10.refs_0_ = bf16[128,256]{1,0:T(8,128)(2,1)S(1)} collective-permute-done((bf16[128,256]{1,0:T(8,128)(2,1)S(1)}, bf16[128,256]{1,0:T(8,128)(2,1)S(1)}, u32[]{:S(2)}, u32[]{:S(2)}) %collective-permute-start.10) | collective-permute-done | bytes 65568 | tf_op jit(solution)/shard_map/ppermute | solution.py:278
  45.7 0.8 %collective-permute-done.14.refs_1_ = bf16[128,256]{1,0:T(8,128)(2,1)S(1)} collective-permute-done((bf16[128,256]{1,0:T(8,128)(2,1)S(1)}, bf16[128,256]{1,0:T(8,128)(2,1)S(1)}, u32[]{:S(2)}, u32[]{:S(2)}) %collective-permute-start.14) | collective-permute-done | bytes 65568 | tf_op jit(solution)/shard_map/ppermute | solution.py:278
  46.5 0.0 collective-permute-done.16.refs_2_
  46.5 0.7 %shard_map.90 = (bf16[128,128]{1,0:T(8,128)(2,1)}, bf16[128,128]{1,0:T(8,128)(2,1)}) custom-call(bf16[128,256]{1,0:T(8,128)(2,1)S(1)} %collective-permute-done.10.refs_0_, bf16[128,256]{1,0:T(8,128)(2,1)S(1)} %collective-permute-done.14.refs_1_, bf16[128,256]{1,0:T(8,128)(2,1)S(1)} %collective-permute-done.16.refs_2_, ...), custom_call_target="tpu_custom_call" | custom-call | tf_op jit(solution)/shard_map/pallas_call | solution.py:357
  (3 shorter events, 0.1 us)
Async XLA Ops:
  3.6 22.5 %copy-start = (bf16[1312,128]{1,0:T(8,128)(2,1)S(1)}, bf16[1312,128]{1,0:T(8,128)(2,1)}, u32[]{:S(2)}) copy-start(bf16[1312,128]{1,0:T(8,128)(2,1)} %get-tuple-element.33.refs_0_) | copy-start | bytes 1007620
  3.6 3.5 %collective-permute-start.5 = (bf16[1312,128]{1,0:T(8,128)(2,1)}, bf16[1312,128]{1,0:T(8,128)(2,1)S(1)}, u32[]{:S(2)}, u32[]{:S(2)}) collective-permute-start(bf16[1312,128]{1,0:T(8,128)(2,1)} %get-tuple-element.36), channel_id=1, source_target_pairs={{0,8},{8,0},{16,24},{24,16},{1,9},{9,1},{17,25},{25,17},{2,10},{10... | collective-permute-start | bytes 1007624 | tf_op jit(solution)/shard_map/ppermute | solution.py:273
  4.2 21.6 %collective-permute-start.3 = (bf16[1312,128]{1,0:T(8,128)(2,1)}, bf16[1312,128]{1,0:T(8,128)(2,1)S(1)}, u32[]{:S(2)}, u32[]{:S(2)}) collective-permute-start(bf16[1312,128]{1,0:T(8,128)(2,1)} %get-tuple-element.34), channel_id=1, source_target_pairs={{0,8},{8,0},{16,24},{24,16},{1,9},{9,1},{17,25},{25,17},{2,10},{10... | collective-permute-start | bytes 1007624 | tf_op jit(solution)/shard_map/ppermute | solution.py:273
  4.2 21.5 %collective-permute-start.4 = (bf16[1312,128]{1,0:T(8,128)(2,1)}, bf16[1312,128]{1,0:T(8,128)(2,1)S(1)}, u32[]{:S(2)}, u32[]{:S(2)}) collective-permute-start(bf16[1312,128]{1,0:T(8,128)(2,1)} %get-tuple-element.35), channel_id=1, source_target_pairs={{0,16},{8,24},{16,0},{24,8},{1,17},{9,25},{17,1},{25,9},{2,18},{10... | collective-permute-start | bytes 1007624 | tf_op jit(solution)/shard_map/ppermute | solution.py:273
  7.2 6.5 %collective-permute-start.2 = (bf16[128,256]{1,0:T(8,128)(2,1)S(1)}, bf16[128,256]{1,0:T(8,128)(2,1)S(1)}, u32[]{:S(2)}, u32[]{:S(2)}) collective-permute-start(bf16[128,256]{1,0:T(8,128)(2,1)S(1)} %param.1), channel_id=1, source_target_pairs={{0,6},{1,7},{2,4},{3,5},{4,2},{5,3},{6,0},{7,1},{8,14},{9,15},{10,... | collective-permute-start | bytes 196616 | tf_op jit(solution)/shard_map/cond/branch_1_fun/ppermute | solution.py:273
  10.8 5.7 %collective-permute-start.1 = (bf16[128,256]{1,0:T(8,128)(2,1)S(1)}, bf16[128,256]{1,0:T(8,128)(2,1)S(1)}, u32[]{:S(2)}, u32[]{:S(2)}) collective-permute-start(bf16[128,256]{1,0:T(8,128)(2,1)S(1)} %param.1), channel_id=1, source_target_pairs={{0,4},{1,5},{2,6},{3,7},{4,0},{5,1},{6,2},{7,3},{8,12},{9,13},{10,... | collective-permute-start | bytes 196616 | tf_op jit(solution)/shard_map/cond/branch_1_fun/ppermute | solution.py:273
  10.8 5.7 %collective-permute-start = (bf16[128,256]{1,0:T(8,128)(2,1)S(1)}, bf16[128,256]{1,0:T(8,128)(2,1)S(1)}, u32[]{:S(2)}, u32[]{:S(2)}) collective-permute-start(bf16[128,256]{1,0:T(8,128)(2,1)S(1)} %param.1), channel_id=1, source_target_pairs={{0,2},{1,3},{2,0},{3,1},{4,6},{5,7},{6,4},{7,5},{8,10},{9,11},{10,... | collective-permute-start | bytes 196616 | tf_op jit(solution)/shard_map/cond/branch_1_fun/ppermute | solution.py:273
  16.5 9.6 %collective-permute-start.6 = (bf16[1312,128]{1,0:T(8,128)(2,1)S(1)}, bf16[1312,128]{1,0:T(8,128)(2,1)S(1)}, u32[]{:S(2)}, u32[]{:S(2)}) collective-permute-start(bf16[1312,128]{1,0:T(8,128)(2,1)S(1)} %collective-permute-done.5), channel_id=1, source_target_pairs={{0,16},{8,24},{16,0},{24,8},{1,17},{9,25},{17,1},{25,9},{2,18},{10... | collective-permute-start | bytes 1007624 | tf_op jit(solution)/shard_map/ppermute | solution.py:273
  18.1 7.6 %collective-permute-start.8 = (bf16[3,128,256]{2,1,0:T(8,128)(2,1)S(1)}, bf16[3,128,256]{2,1,0:T(8,128)(2,1)S(1)}, u32[]{:S(2)}, u32[]{:S(2)}) collective-permute-start(bf16[3,128,256]{2,1,0:T(8,128)(2,1)S(1)} %get-tuple-element.59.refs_6_), channel_id=1, source_target_pairs={{0,1},{1,0},{2,3},{3,2},{4,5},{5,4},{6,7},{7,6},{8,9},{9,8},{10,11... | collective-permute-start | bytes 589832 | tf_op jit(solution)/shard_map/ppermute | solution.py:273
  19.6 6.1 %collective-permute-start.7 = (bf16[128,256]{1,0:T(8,128)(2,1)S(1)}, bf16[128,256]{1,0:T(8,128)(2,1)S(1)}, u32[]{:S(2)}, u32[]{:S(2)}) collective-permute-start(bf16[128,256]{1,0:T(8,128)(2,1)S(1)} %get-tuple-element.39.refs_4_), channel_id=1, source_target_pairs={{0,1},{1,0},{2,3},{3,2},{4,5},{5,4},{6,7},{7,6},{8,9},{9,8},{10,11... | collective-permute-start | bytes 196616 | tf_op jit(solution)/shard_map/ppermute | solution.py:273
  29.3 2.2 %collective-permute-start.11 = (bf16[640,128]{1,0:T(8,128)(2,1)S(1)}, bf16[640,128]{1,0:T(8,128)(2,1)S(1)}, u32[]{:S(2)}, u32[]{:S(2)}) collective-permute-start(bf16[640,128]{1,0:T(8,128)(2,1)S(1)} %get-tuple-element.44), channel_id=1, source_target_pairs={{0,8},{8,0},{16,24},{24,16},{1,9},{9,1},{17,25},{25,17},{2,10},{10... | collective-permute-start | bytes 491528 | tf_op jit(solution)/shard_map/ppermute | solution.py:273
  29.3 6.4 %collective-permute-start.9 = (bf16[2,128,256]{2,1,0:T(8,128)(2,1)S(1)}, bf16[2,128,256]{2,1,0:T(8,128)(2,1)S(1)}, u32[]{:S(2)}, u32[]{:S(2)}) collective-permute-start(bf16[2,128,256]{2,1,0:T(8,128)(2,1)S(1)} %get-tuple-element.41), channel_id=1, source_target_pairs={{0,1},{1,0},{2,3},{3,2},{4,5},{5,4},{6,7},{7,6},{8,9},{9,8},{10,11... | collective-permute-start | bytes 393224 | tf_op jit(solution)/shard_map/ppermute | solution.py:273
  30.9 7.4 %collective-permute-start.15 = (bf16[2,128,256]{2,1,0:T(8,128)(2,1)S(1)}, bf16[2,128,256]{2,1,0:T(8,128)(2,1)S(1)}, u32[]{:S(2)}, u32[]{:S(2)}) collective-permute-start(bf16[2,128,256]{2,1,0:T(8,128)(2,1)S(1)} %get-tuple-element.54), channel_id=1, source_target_pairs={{0,1},{1,0},{2,3},{3,2},{4,5},{5,4},{6,7},{7,6},{8,9},{9,8},{10,11... | collective-permute-start | bytes 393224 | tf_op jit(solution)/shard_map/ppermute | solution.py:273
  31.4 8.3 %collective-permute-start.12 = (bf16[640,128]{1,0:T(8,128)(2,1)S(1)}, bf16[640,128]{1,0:T(8,128)(2,1)S(1)}, u32[]{:S(2)}, u32[]{:S(2)}) collective-permute-start(bf16[640,128]{1,0:T(8,128)(2,1)S(1)} %get-tuple-element.48), channel_id=1, source_target_pairs={{0,16},{8,24},{16,0},{24,8},{1,17},{9,25},{17,1},{25,9},{2,18},{10... | collective-permute-start | bytes 491528 | tf_op jit(solution)/shard_map/ppermute | solution.py:273
  32.9 7.0 %collective-permute-start.13 = (bf16[640,128]{1,0:T(8,128)(2,1)S(1)}, bf16[640,128]{1,0:T(8,128)(2,1)S(1)}, u32[]{:S(2)}, u32[]{:S(2)}) collective-permute-start(bf16[640,128]{1,0:T(8,128)(2,1)S(1)} %get-tuple-element.49), channel_id=1, source_target_pairs={{0,24},{8,16},{16,8},{24,0},{1,25},{9,17},{17,9},{25,1},{2,26},{10... | collective-permute-start | bytes 491528 | tf_op jit(solution)/shard_map/ppermute | solution.py:273
  35.7 9.9 %collective-permute-start.10 = (bf16[128,256]{1,0:T(8,128)(2,1)S(1)}, bf16[128,256]{1,0:T(8,128)(2,1)S(1)}, u32[]{:S(2)}, u32[]{:S(2)}) collective-permute-start(bf16[128,256]{1,0:T(8,128)(2,1)S(1)} %get-tuple-element.42), channel_id=1, source_target_pairs={{6,0},{7,1},{14,8},{15,9},{22,16},{23,17},{30,24},{31,25}} | collective-permute-start | bytes 196616 | tf_op jit(solution)/shard_map/ppermute | solution.py:278
  37.0 9.5 %collective-permute-start.14 = (bf16[128,256]{1,0:T(8,128)(2,1)S(1)}, bf16[128,256]{1,0:T(8,128)(2,1)S(1)}, u32[]{:S(2)}, u32[]{:S(2)}) collective-permute-start(bf16[128,256]{1,0:T(8,128)(2,1)S(1)} %get-tuple-element.52), channel_id=1, source_target_pairs={{4,0},{5,1},{6,2},{7,3},{12,8},{13,9},{14,10},{15,11},{20,16},{21,... | collective-permute-start | bytes 196616 | tf_op jit(solution)/shard_map/ppermute | solution.py:278
  38.4 8.1 %collective-permute-start.16 = (bf16[128,256]{1,0:T(8,128)(2,1)S(1)}, bf16[128,256]{1,0:T(8,128)(2,1)S(1)}, u32[]{:S(2)}, u32[]{:S(2)}) collective-permute-start(bf16[128,256]{1,0:T(8,128)(2,1)S(1)} %get-tuple-element.55), channel_id=1, source_target_pairs={{2,0},{3,1},{4,2},{5,3},{6,4},{7,5},{10,8},{11,9},{12,10},{13,11},... | collective-permute-start | bytes 196616 | tf_op jit(solution)/shard_map/ppermute | solution.py:278

commit v6 on v5

--- a/solution.py
+++ b/solution.py
@@ -26,7 +26,7 @@
     cache, refs = refs[:cached], refs[cached + after :]
     outs, refs = refs[: len(which)], refs[len(which) :]
     block, refs = (refs[0], refs[1:]) if cached else (None, refs)
-    here, totals_here, ready, sems = refs
+    here, ready, sems = refs
     rows = queries.shape[0]
     here_at = lax.axis_index("section")
     width = heads * head
@@ -36,7 +36,6 @@
         columns = pl.ds(pl.multiple_of((here_at ^ k) * width, 128), width)
         for i, source in enumerate((grads, saved, queries)):
             ends.append((source.at[:, columns], here.at[m, i]))
-    ends.append((totals, totals_here))
     for i, source in enumerate(cache):
         ends.append((source, block.at[:, pl.ds(i * head, head)]))
     loads = [pltpu.make_async_copy(*pair, sems.at[i]) for i, pair in enumerate(ends)]
@@ -65,17 +64,16 @@
         rest = dots - high
         middle = rest.astype(jnp.bfloat16).astype(jnp.float32)
         low = rest - middle
-        if m == 0:
-            loads[3 * len(which)].wait()
-        chosen = totals_here[0:heads, :].astype(jnp.float32)
+        every_total = totals[...].astype(jnp.float32)
+        chosen = every_total[0:heads]
         for group in range(1, groups):
-            part = totals_here[group * heads : (group + 1) * heads, :].astype(jnp.float32)
+            part = every_total[group * heads : (group + 1) * heads]
             chosen = jnp.where((here_at ^ k) == group, part, chosen)
         spare = jnp.zeros((message.shape[0] - 2 * heads * rows - EXTRA * heads, 128), jnp.float32)
         extra = jnp.concatenate([chosen, high, middle, low, spare], axis=0)
         message[2 * heads * rows :, :] = extra.astype(jnp.bfloat16)
         stores[m].start()
-    for copy in loads[3 * len(which) + 1 :] + stores:
+    for copy in loads[3 * len(which) :] + stores:
         copy.wait()
 
 
@@ -296,12 +294,11 @@
     *sent, own = call(
         functools.partial(pack_kernel, heads, head, tuple(range(sections)), 2, 0),
         [(lines, 128)] * sections + [(rows, 2 * head)],
-        [HBM] * 6,
+        [HBM] * 3 + [VMEM] + [HBM] * 2,
         [
             pltpu.VMEM((sections, 3, rows, heads * head), jnp.bfloat16),
-            pltpu.VMEM(totals.shape, jnp.bfloat16),
             pltpu.VMEM((sections, lines, 128), jnp.bfloat16),
-            pltpu.SemaphoreType.DMA((4 * sections + 3,)),
+            pltpu.SemaphoreType.DMA((4 * sections + 2,)),
         ],
         limit=PACK_LIMIT,
         out_specs=[HBM] * (sections + 1),

time: 47.4 us -> 48 us (1.013)
  Pallas kernels: 7.82 us -> 8.36 us
    pallas_call x1, Pallas kernels: 2.98 us -> 3.52 us  [local(): call(functools.partial(pack_kernel, heads, head, tuple(range(sections)),...]
where the time goes in v6:
time: 48 us; the launch traced here: 47.7 us
  waiting for transfers between devices  19.5 us (41%)
  starting transfers between devices  19 us (40%)
  Pallas kernels  8.36 us (17%)
  between operations  0.73 us (2%)
    ppermute x14, starting transfers between devices, swap(): return lax.ppermute(array, axis, [(i, i ^ bits) for i in range(size)])  15.2 us
    ppermute x14, waiting for transfers between devices, swap(): return lax.ppermute(array, axis, [(i, i ^ bits) for i in range(size)])  13.9 us
    ppermute x3, waiting for transfers between devices, move(): lax.ppermute(array, 'seq', [(i, i + step) for i in range(size) if 0 <= i...  5.61 us
    ppermute x3, starting transfers between devices, move(): lax.ppermute(array, 'seq', [(i, i + step) for i in range(size) if 0 <= i...  3.88 us
    pallas_call x1, Pallas kernels, local(): call(functools.partial(pack_kernel, heads, head, tuple(range(sections)),...  3.52 us
    pallas_call x1, Pallas kernels, local(): call(functools.partial(attend_kernel, sections, heads, head, outer, inv_r...  3.15 us
    pallas_call x1, Pallas kernels, local(): call(functools.partial(place_kernel, heads, head), [queries.shape[1:]], [...  0.96 us
  transfers between devices with their start and end apart: 17, of which 8 were waited for; matrix products, arithmetic and copies ran while one was open for 0% of the time, Pallas kernels for 2%

profile of v6, /device:TPU:0, one launch (start us, length us, event | category | flops | bytes accessed | tf_op | source)
XLA Modules:
  0.0 47.7 jit_solution(8517518901806303036)
XLA Ops:
  0.6 3.5 %shard_map.85 = (bf16[1312,128]{1,0:T(8,128)(2,1)}, bf16[1312,128]{1,0:T(8,128)(2,1)}, bf16[1312,128]{1,0:T(8,128)(2,1)}, bf16[1312,128]{1,0:T(8,128)(2,1)}, bf16[128,256]{1,0:T(8,128)(2,1)S(1)}) custom-call(bf16[128,2560]{1,0:T(8,128)(2,1)} %bitcast.10, bf16[128,2560]{1,0:T(8,128)(2,1)} %bitcast.11, bf16[128,2560]{1,0:T(8,128)(2,1)} %bitcast.12, ...), custom_call_target="tpu_custom_call" | custom-call | tf_op jit(solution)/shard_map/pallas_call | solution.py:294
  4.2 0.0 copy-start
  4.2 0.5 %collective-permute-start.5 = (bf16[1312,128]{1,0:T(8,128)(2,1)}, bf16[1312,128]{1,0:T(8,128)(2,1)S(1)}, u32[]{:S(2)}, u32[]{:S(2)}) collective-permute-start(bf16[1312,128]{1,0:T(8,128)(2,1)} %get-tuple-element.36), channel_id=1, source_target_pairs={{0,8},{8,0},{16,24},{24,16},{1,9},{9,1},{17,25},{25,17},{2,10},{10... | collective-permute-start | bytes 1007624 | tf_op jit(solution)/shard_map/ppermute | solution.py:271
  4.7 0.1 collective-permute-start.3
  4.8 2.9 %collective-permute-start.4 = (bf16[1312,128]{1,0:T(8,128)(2,1)}, bf16[1312,128]{1,0:T(8,128)(2,1)S(1)}, u32[]{:S(2)}, u32[]{:S(2)}) collective-permute-start(bf16[1312,128]{1,0:T(8,128)(2,1)} %get-tuple-element.35), channel_id=1, source_target_pairs={{0,16},{8,24},{16,0},{24,8},{1,17},{9,25},{17,1},{25,9},{2,18},{10... | collective-permute-start | bytes 1007624 | tf_op jit(solution)/shard_map/ppermute | solution.py:271
  7.7 0.0 collective-permute-done.5
  7.7 9.4 %conditional.1 = (bf16[3,128,256]{2,1,0:T(8,128)(2,1)S(1)}) conditional(s32[]{:T(128)} %convert_element_type.3, () %tuple.18, bf16[128,256]{1,0:T(8,128)(2,1)S(1)} %get-tuple-element.39.refs_4_), branch_computations={%region_0.0_spmd, %region_1.0_spmd} | conditional | flops 196608 | bytes 1179776 | solution.py:318
  7.7 3.6 %collective-permute-start.2 = (bf16[128,256]{1,0:T(8,128)(2,1)S(1)}, bf16[128,256]{1,0:T(8,128)(2,1)S(1)}, u32[]{:S(2)}, u32[]{:S(2)}) collective-permute-start(bf16[128,256]{1,0:T(8,128)(2,1)S(1)} %param.1), channel_id=1, source_target_pairs={{0,6},{1,7},{2,4},{3,5},{4,2},{5,3},{6,0},{7,1},{8,14},{9,15},{10,... | collective-permute-start | bytes 196616 | tf_op jit(solution)/shard_map/cond/branch_1_fun/ppermute | solution.py:271
  11.3 0.0 collective-permute-start.1
  11.3 0.8 %collective-permute-start = (bf16[128,256]{1,0:T(8,128)(2,1)S(1)}, bf16[128,256]{1,0:T(8,128)(2,1)S(1)}, u32[]{:S(2)}, u32[]{:S(2)}) collective-permute-start(bf16[128,256]{1,0:T(8,128)(2,1)S(1)} %param.1), channel_id=1, source_target_pairs={{0,2},{1,3},{2,0},{3,1},{4,6},{5,7},{6,4},{7,5},{8,10},{9,11},{10,... | collective-permute-start | bytes 196616 | tf_op jit(solution)/shard_map/cond/branch_1_fun/ppermute | solution.py:271
  12.1 2.1 %collective-permute-done.2 = bf16[128,256]{1,0:T(8,128)(2,1)S(1)} collective-permute-done((bf16[128,256]{1,0:T(8,128)(2,1)S(1)}, bf16[128,256]{1,0:T(8,128)(2,1)S(1)}, u32[]{:S(2)}, u32[]{:S(2)}) %collective-permute-start.2) | collective-permute-done | bytes 65568 | tf_op jit(solution)/shard_map/cond/branch_1_fun/ppermute | solution.py:271
  14.2 2.8 %collective-permute-done.1 = bf16[128,256]{1,0:T(8,128)(2,1)S(1)} collective-permute-done((bf16[128,256]{1,0:T(8,128)(2,1)S(1)}, bf16[128,256]{1,0:T(8,128)(2,1)S(1)}, u32[]{:S(2)}, u32[]{:S(2)}) %collective-permute-start.1) | collective-permute-done | bytes 65568 | tf_op jit(solution)/shard_map/cond/branch_1_fun/ppermute | solution.py:271
  17.0 0.0 collective-permute-done
  17.1 1.6 %collective-permute-start.6 = (bf16[1312,128]{1,0:T(8,128)(2,1)S(1)}, bf16[1312,128]{1,0:T(8,128)(2,1)S(1)}, u32[]{:S(2)}, u32[]{:S(2)}) collective-permute-start(bf16[1312,128]{1,0:T(8,128)(2,1)S(1)} %collective-permute-done.5), channel_id=1, source_target_pairs={{0,16},{8,24},{16,0},{24,8},{1,17},{9,25},{17,1},{25,9},{2,18},{10... | collective-permute-start | bytes 1007624 | tf_op jit(solution)/shard_map/ppermute | solution.py:271
  18.6 1.5 %collective-permute-start.8 = (bf16[3,128,256]{2,1,0:T(8,128)(2,1)S(1)}, bf16[3,128,256]{2,1,0:T(8,128)(2,1)S(1)}, u32[]{:S(2)}, u32[]{:S(2)}) collective-permute-start(bf16[3,128,256]{2,1,0:T(8,128)(2,1)S(1)} %get-tuple-element.59.refs_6_), channel_id=1, source_target_pairs={{0,1},{1,0},{2,3},{3,2},{4,5},{5,4},{6,7},{7,6},{8,9},{9,8},{10,11... | collective-permute-start | bytes 589832 | tf_op jit(solution)/shard_map/ppermute | solution.py:271
  20.1 0.5 %collective-permute-start.7 = (bf16[128,256]{1,0:T(8,128)(2,1)S(1)}, bf16[128,256]{1,0:T(8,128)(2,1)S(1)}, u32[]{:S(2)}, u32[]{:S(2)}) collective-permute-start(bf16[128,256]{1,0:T(8,128)(2,1)S(1)} %get-tuple-element.39.refs_4_), channel_id=1, source_target_pairs={{0,1},{1,0},{2,3},{3,2},{4,5},{5,4},{6,7},{7,6},{8,9},{9,8},{10,11... | collective-permute-start | bytes 196616 | tf_op jit(solution)/shard_map/ppermute | solution.py:271
  20.7 5.6 %collective-permute-done.7.refs_5_ = bf16[128,256]{1,0:T(8,128)(2,1)S(1)} collective-permute-done((bf16[128,256]{1,0:T(8,128)(2,1)S(1)}, bf16[128,256]{1,0:T(8,128)(2,1)S(1)}, u32[]{:S(2)}, u32[]{:S(2)}) %collective-permute-start.7) | collective-permute-done | bytes 65568 | tf_op jit(solution)/shard_map/ppermute | solution.py:271
  26.3 0.0 collective-permute-done.3.refs_1_
  26.3 0.0 collective-permute-done.4.refs_2_
  26.3 0.0 collective-permute-done.8.refs_7_
  26.3 0.4 collective-permute-done.6.refs_3_
  26.6 0.0 copy-done
  26.6 3.2 %shard_map.86 = (bf16[2,128,256]{2,1,0:T(8,128)(2,1)S(1)}, bf16[2,128,256]{2,1,0:T(8,128)(2,1)S(1)}, bf16[2,128,256]{2,1,0:T(8,128)(2,1)S(1)}, bf16[2,128,256]{2...) custom-call(bf16[1312,128]{1,0:T(8,128)(2,1)S(1)} %copy-done, ...), custom_call_target="tpu_custom_call" | custom-call | tf_op jit(solution)/shard_map/pallas_call | solution.py:324
  29.8 0.1 collective-permute-start.11
  29.9 1.6 %collective-permute-start.9 = (bf16[2,128,256]{2,1,0:T(8,128)(2,1)S(1)}, bf16[2,128,256]{2,1,0:T(8,128)(2,1)S(1)}, u32[]{:S(2)}, u32[]{:S(2)}) collective-permute-start(bf16[2,128,256]{2,1,0:T(8,128)(2,1)S(1)} %get-tuple-element.41), channel_id=1, source_target_pairs={{0,1},{1,0},{2,3},{3,2},{4,5},{5,4},{6,7},{7,6},{8,9},{9,8},{10,11... | collective-permute-start | bytes 393224 | tf_op jit(solution)/shard_map/ppermute | solution.py:271
  31.4 0.5 %collective-permute-start.15 = (bf16[2,128,256]{2,1,0:T(8,128)(2,1)S(1)}, bf16[2,128,256]{2,1,0:T(8,128)(2,1)S(1)}, u32[]{:S(2)}, u32[]{:S(2)}) collective-permute-start(bf16[2,128,256]{2,1,0:T(8,128)(2,1)S(1)} %get-tuple-element.54), channel_id=1, source_target_pairs={{0,1},{1,0},{2,3},{3,2},{4,5},{5,4},{6,7},{7,6},{8,9},{9,8},{10,11... | collective-permute-start | bytes 393224 | tf_op jit(solution)/shard_map/ppermute | solution.py:271
  32.0 0.0 collective-permute-done.11.refs_1_
  32.0 1.5 %collective-permute-start.12 = (bf16[640,128]{1,0:T(8,128)(2,1)S(1)}, bf16[640,128]{1,0:T(8,128)(2,1)S(1)}, u32[]{:S(2)}, u32[]{:S(2)}) collective-permute-start(bf16[640,128]{1,0:T(8,128)(2,1)S(1)} %get-tuple-element.48), channel_id=1, source_target_pairs={{0,16},{8,24},{16,0},{24,8},{1,17},{9,25},{17,1},{25,9},{2,18},{10... | collective-permute-start | bytes 491528 | tf_op jit(solution)/shard_map/ppermute | solution.py:271
  33.5 0.0 collective-permute-start.13
  33.5 2.8 %collective-permute-done.9.theirs = bf16[2,128,256]{2,1,0:T(8,128)(2,1)S(1)} collective-permute-done((bf16[2,128,256]{2,1,0:T(8,128)(2,1)S(1)}, bf16[2,128,256]{2,1,0:T(8,128)(2,1)S(1)}, u32[]{:S(2)}, u32[]{:S(2)}) %collective-permute-start.9) | collective-permute-done | bytes 131104 | tf_op jit(solution)/shard_map/ppermute | solution.py:271
  36.3 1.3 %collective-permute-start.10 = (bf16[128,256]{1,0:T(8,128)(2,1)S(1)}, bf16[128,256]{1,0:T(8,128)(2,1)S(1)}, u32[]{:S(2)}, u32[]{:S(2)}) collective-permute-start(bf16[128,256]{1,0:T(8,128)(2,1)S(1)} %get-tuple-element.42), channel_id=1, source_target_pairs={{6,0},{7,1},{14,8},{15,9},{22,16},{23,17},{30,24},{31,25}} | collective-permute-start | bytes 196616 | tf_op jit(solution)/shard_map/ppermute | solution.py:276
  37.6 1.3 %collective-permute-start.14 = (bf16[128,256]{1,0:T(8,128)(2,1)S(1)}, bf16[128,256]{1,0:T(8,128)(2,1)S(1)}, u32[]{:S(2)}, u32[]{:S(2)}) collective-permute-start(bf16[128,256]{1,0:T(8,128)(2,1)S(1)} %get-tuple-element.52), channel_id=1, source_target_pairs={{4,0},{5,1},{6,2},{7,3},{12,8},{13,9},{14,10},{15,11},{20,16},{21,... | collective-permute-start | bytes 196616 | tf_op jit(solution)/shard_map/ppermute | solution.py:276
  38.9 0.0 collective-permute-done.15.theirs
  38.9 1.3 %collective-permute-start.16 = (bf16[128,256]{1,0:T(8,128)(2,1)S(1)}, bf16[128,256]{1,0:T(8,128)(2,1)S(1)}, u32[]{:S(2)}, u32[]{:S(2)}) collective-permute-start(bf16[128,256]{1,0:T(8,128)(2,1)S(1)} %get-tuple-element.55), channel_id=1, source_target_pairs={{2,0},{3,1},{4,2},{5,3},{6,4},{7,5},{10,8},{11,9},{12,10},{13,11},... | collective-permute-start | bytes 196616 | tf_op jit(solution)/shard_map/ppermute | solution.py:276
  40.2 0.0 collective-permute-done.12.refs_2_
  40.3 0.2 collective-permute-done.13.refs_3_
  40.5 1.0 %shard_map.88 = bf16[128,2560]{1,0:T(8,128)(2,1)} custom-call(bf16[640,128]{1,0:T(8,128)(2,1)S(1)} %get-tuple-element.43.refs_0_, bf16[640,128]{1,0:T(8,128)(2,1)S(1)} %collective-permute-done.11.refs_1_, bf16[640,128]{1,0:T(8,128)(2,1)S(1)} %collective-permute-done.12.refs_2_, bf16[640,128]{1,0:T(8,128)(2,1)S(1)} %collective-permute-done.13.refs_3_), custom_call_target="tpu_custom_call" | custom-call | tf_op jit(solution)/shard_map/pallas_call | solution.py:348
  41.4 4.8 %collective-permute-done.10.refs_0_ = bf16[128,256]{1,0:T(8,128)(2,1)S(1)} collective-permute-done((bf16[128,256]{1,0:T(8,128)(2,1)S(1)}, bf16[128,256]{1,0:T(8,128)(2,1)S(1)}, u32[]{:S(2)}, u32[]{:S(2)}) %collective-permute-start.10) | collective-permute-done | bytes 65568 | tf_op jit(solution)/shard_map/ppermute | solution.py:276
  46.2 0.8 %collective-permute-done.14.refs_1_ = bf16[128,256]{1,0:T(8,128)(2,1)S(1)} collective-permute-done((bf16[128,256]{1,0:T(8,128)(2,1)S(1)}, bf16[128,256]{1,0:T(8,128)(2,1)S(1)}, u32[]{:S(2)}, u32[]{:S(2)}) %collective-permute-start.14) | collective-permute-done | bytes 65568 | tf_op jit(solution)/shard_map/ppermute | solution.py:276
  47.0 0.0 collective-permute-done.16.refs_2_
  47.0 0.7 %shard_map.90 = (bf16[128,128]{1,0:T(8,128)(2,1)}, bf16[128,128]{1,0:T(8,128)(2,1)}) custom-call(bf16[128,256]{1,0:T(8,128)(2,1)S(1)} %collective-permute-done.10.refs_0_, bf16[128,256]{1,0:T(8,128)(2,1)S(1)} %collective-permute-done.14.refs_1_, bf16[128,256]{1,0:T(8,128)(2,1)S(1)} %collective-permute-done.16.refs_2_, ...), custom_call_target="tpu_custom_call" | custom-call | tf_op jit(solution)/shard_map/pallas_call | solution.py:354
  (3 shorter events, 0.1 us)
Async XLA Ops:
  4.2 22.5 %copy-start = (bf16[1312,128]{1,0:T(8,128)(2,1)S(1)}, bf16[1312,128]{1,0:T(8,128)(2,1)}, u32[]{:S(2)}) copy-start(bf16[1312,128]{1,0:T(8,128)(2,1)} %get-tuple-element.33.refs_0_) | copy-start | bytes 1007620
  4.2 3.5 %collective-permute-start.5 = (bf16[1312,128]{1,0:T(8,128)(2,1)}, bf16[1312,128]{1,0:T(8,128)(2,1)S(1)}, u32[]{:S(2)}, u32[]{:S(2)}) collective-permute-start(bf16[1312,128]{1,0:T(8,128)(2,1)} %get-tuple-element.36), channel_id=1, source_target_pairs={{0,8},{8,0},{16,24},{24,16},{1,9},{9,1},{17,25},{25,17},{2,10},{10... | collective-permute-start | bytes 1007624 | tf_op jit(solution)/shard_map/ppermute | solution.py:271
  4.7 21.6 %collective-permute-start.3 = (bf16[1312,128]{1,0:T(8,128)(2,1)}, bf16[1312,128]{1,0:T(8,128)(2,1)S(1)}, u32[]{:S(2)}, u32[]{:S(2)}) collective-permute-start(bf16[1312,128]{1,0:T(8,128)(2,1)} %get-tuple-element.34), channel_id=1, source_target_pairs={{0,8},{8,0},{16,24},{24,16},{1,9},{9,1},{17,25},{25,17},{2,10},{10... | collective-permute-start | bytes 1007624 | tf_op jit(solution)/shard_map/ppermute | solution.py:271
  4.8 21.5 %collective-permute-start.4 = (bf16[1312,128]{1,0:T(8,128)(2,1)}, bf16[1312,128]{1,0:T(8,128)(2,1)S(1)}, u32[]{:S(2)}, u32[]{:S(2)}) collective-permute-start(bf16[1312,128]{1,0:T(8,128)(2,1)} %get-tuple-element.35), channel_id=1, source_target_pairs={{0,16},{8,24},{16,0},{24,8},{1,17},{9,25},{17,1},{25,9},{2,18},{10... | collective-permute-start | bytes 1007624 | tf_op jit(solution)/shard_map/ppermute | solution.py:271
  7.7 6.5 %collective-permute-start.2 = (bf16[128,256]{1,0:T(8,128)(2,1)S(1)}, bf16[128,256]{1,0:T(8,128)(2,1)S(1)}, u32[]{:S(2)}, u32[]{:S(2)}) collective-permute-start(bf16[128,256]{1,0:T(8,128)(2,1)S(1)} %param.1), channel_id=1, source_target_pairs={{0,6},{1,7},{2,4},{3,5},{4,2},{5,3},{6,0},{7,1},{8,14},{9,15},{10,... | collective-permute-start | bytes 196616 | tf_op jit(solution)/shard_map/cond/branch_1_fun/ppermute | solution.py:271
  11.3 5.7 %collective-permute-start.1 = (bf16[128,256]{1,0:T(8,128)(2,1)S(1)}, bf16[128,256]{1,0:T(8,128)(2,1)S(1)}, u32[]{:S(2)}, u32[]{:S(2)}) collective-permute-start(bf16[128,256]{1,0:T(8,128)(2,1)S(1)} %param.1), channel_id=1, source_target_pairs={{0,4},{1,5},{2,6},{3,7},{4,0},{5,1},{6,2},{7,3},{8,12},{9,13},{10,... | collective-permute-start | bytes 196616 | tf_op jit(solution)/shard_map/cond/branch_1_fun/ppermute | solution.py:271
  11.3 5.7 %collective-permute-start = (bf16[128,256]{1,0:T(8,128)(2,1)S(1)}, bf16[128,256]{1,0:T(8,128)(2,1)S(1)}, u32[]{:S(2)}, u32[]{:S(2)}) collective-permute-start(bf16[128,256]{1,0:T(8,128)(2,1)S(1)} %param.1), channel_id=1, source_target_pairs={{0,2},{1,3},{2,0},{3,1},{4,6},{5,7},{6,4},{7,5},{8,10},{9,11},{10,... | collective-permute-start | bytes 196616 | tf_op jit(solution)/shard_map/cond/branch_1_fun/ppermute | solution.py:271
  17.1 9.6 %collective-permute-start.6 = (bf16[1312,128]{1,0:T(8,128)(2,1)S(1)}, bf16[1312,128]{1,0:T(8,128)(2,1)S(1)}, u32[]{:S(2)}, u32[]{:S(2)}) collective-permute-start(bf16[1312,128]{1,0:T(8,128)(2,1)S(1)} %collective-permute-done.5), channel_id=1, source_target_pairs={{0,16},{8,24},{16,0},{24,8},{1,17},{9,25},{17,1},{25,9},{2,18},{10... | collective-permute-start | bytes 1007624 | tf_op jit(solution)/shard_map/ppermute | solution.py:271
  18.6 7.6 %collective-permute-start.8 = (bf16[3,128,256]{2,1,0:T(8,128)(2,1)S(1)}, bf16[3,128,256]{2,1,0:T(8,128)(2,1)S(1)}, u32[]{:S(2)}, u32[]{:S(2)}) collective-permute-start(bf16[3,128,256]{2,1,0:T(8,128)(2,1)S(1)} %get-tuple-element.59.refs_6_), channel_id=1, source_target_pairs={{0,1},{1,0},{2,3},{3,2},{4,5},{5,4},{6,7},{7,6},{8,9},{9,8},{10,11... | collective-permute-start | bytes 589832 | tf_op jit(solution)/shard_map/ppermute | solution.py:271
  20.1 6.1 %collective-permute-start.7 = (bf16[128,256]{1,0:T(8,128)(2,1)S(1)}, bf16[128,256]{1,0:T(8,128)(2,1)S(1)}, u32[]{:S(2)}, u32[]{:S(2)}) collective-permute-start(bf16[128,256]{1,0:T(8,128)(2,1)S(1)} %get-tuple-element.39.refs_4_), channel_id=1, source_target_pairs={{0,1},{1,0},{2,3},{3,2},{4,5},{5,4},{6,7},{7,6},{8,9},{9,8},{10,11... | collective-permute-start | bytes 196616 | tf_op jit(solution)/shard_map/ppermute | solution.py:271
  29.8 2.2 %collective-permute-start.11 = (bf16[640,128]{1,0:T(8,128)(2,1)S(1)}, bf16[640,128]{1,0:T(8,128)(2,1)S(1)}, u32[]{:S(2)}, u32[]{:S(2)}) collective-permute-start(bf16[640,128]{1,0:T(8,128)(2,1)S(1)} %get-tuple-element.44), channel_id=1, source_target_pairs={{0,8},{8,0},{16,24},{24,16},{1,9},{9,1},{17,25},{25,17},{2,10},{10... | collective-permute-start | bytes 491528 | tf_op jit(solution)/shard_map/ppermute | solution.py:271
  29.9 6.4 %collective-permute-start.9 = (bf16[2,128,256]{2,1,0:T(8,128)(2,1)S(1)}, bf16[2,128,256]{2,1,0:T(8,128)(2,1)S(1)}, u32[]{:S(2)}, u32[]{:S(2)}) collective-permute-start(bf16[2,128,256]{2,1,0:T(8,128)(2,1)S(1)} %get-tuple-element.41), channel_id=1, source_target_pairs={{0,1},{1,0},{2,3},{3,2},{4,5},{5,4},{6,7},{7,6},{8,9},{9,8},{10,11... | collective-permute-start | bytes 393224 | tf_op jit(solution)/shard_map/ppermute | solution.py:271
  31.4 7.4 %collective-permute-start.15 = (bf16[2,128,256]{2,1,0:T(8,128)(2,1)S(1)}, bf16[2,128,256]{2,1,0:T(8,128)(2,1)S(1)}, u32[]{:S(2)}, u32[]{:S(2)}) collective-permute-start(bf16[2,128,256]{2,1,0:T(8,128)(2,1)S(1)} %get-tuple-element.54), channel_id=1, source_target_pairs={{0,1},{1,0},{2,3},{3,2},{4,5},{5,4},{6,7},{7,6},{8,9},{9,8},{10,11... | collective-permute-start | bytes 393224 | tf_op jit(solution)/shard_map/ppermute | solution.py:271
  32.0 8.3 %collective-permute-start.12 = (bf16[640,128]{1,0:T(8,128)(2,1)S(1)}, bf16[640,128]{1,0:T(8,128)(2,1)S(1)}, u32[]{:S(2)}, u32[]{:S(2)}) collective-permute-start(bf16[640,128]{1,0:T(8,128)(2,1)S(1)} %get-tuple-element.48), channel_id=1, source_target_pairs={{0,16},{8,24},{16,0},{24,8},{1,17},{9,25},{17,1},{25,9},{2,18},{10... | collective-permute-start | bytes 491528 | tf_op jit(solution)/shard_map/ppermute | solution.py:271
  33.5 7.0 %collective-permute-start.13 = (bf16[640,128]{1,0:T(8,128)(2,1)S(1)}, bf16[640,128]{1,0:T(8,128)(2,1)S(1)}, u32[]{:S(2)}, u32[]{:S(2)}) collective-permute-start(bf16[640,128]{1,0:T(8,128)(2,1)S(1)} %get-tuple-element.49), channel_id=1, source_target_pairs={{0,24},{8,16},{16,8},{24,0},{1,25},{9,17},{17,9},{25,1},{2,26},{10... | collective-permute-start | bytes 491528 | tf_op jit(solution)/shard_map/ppermute | solution.py:271
  36.3 9.9 %collective-permute-start.10 = (bf16[128,256]{1,0:T(8,128)(2,1)S(1)}, bf16[128,256]{1,0:T(8,128)(2,1)S(1)}, u32[]{:S(2)}, u32[]{:S(2)}) collective-permute-start(bf16[128,256]{1,0:T(8,128)(2,1)S(1)} %get-tuple-element.42), channel_id=1, source_target_pairs={{6,0},{7,1},{14,8},{15,9},{22,16},{23,17},{30,24},{31,25}} | collective-permute-start | bytes 196616 | tf_op jit(solution)/shard_map/ppermute | solution.py:276
  37.6 9.5 %collective-permute-start.14 = (bf16[128,256]{1,0:T(8,128)(2,1)S(1)}, bf16[128,256]{1,0:T(8,128)(2,1)S(1)}, u32[]{:S(2)}, u32[]{:S(2)}) collective-permute-start(bf16[128,256]{1,0:T(8,128)(2,1)S(1)} %get-tuple-element.52), channel_id=1, source_target_pairs={{4,0},{5,1},{6,2},{7,3},{12,8},{13,9},{14,10},{15,11},{20,16},{21,... | collective-permute-start | bytes 196616 | tf_op jit(solution)/shard_map/ppermute | solution.py:276
  38.9 8.1 %collective-permute-start.16 = (bf16[128,256]{1,0:T(8,128)(2,1)S(1)}, bf16[128,256]{1,0:T(8,128)(2,1)S(1)}, u32[]{:S(2)}, u32[]{:S(2)}) collective-permute-start(bf16[128,256]{1,0:T(8,128)(2,1)S(1)} %get-tuple-element.55), channel_id=1, source_target_pairs={{2,0},{3,1},{4,2},{5,3},{6,4},{7,5},{10,8},{11,9},{12,10},{13,11},... | collective-permute-start | bytes 196616 | tf_op jit(solution)/shard_map/ppermute | solution.py:276
